TPU v7x, 256 devices: a whole 4x4x8 slice. The times are simulated.
256 devices in a mesh: dp: 16 (over z_hi, y, core), seq: 16 (over x, z_lo).
Axes of the slice: x: 4, y: 4, z: 8 (z_hi: 2, z_lo: 4; z = z_hi * 4 + z_lo), core: 2. Of those that a mesh axis runs over, the one named last changes fastest.
Arguments:
- hidden: bfloat16 [16, 2048, 7168], P('dp', 'seq'), may hold values from -6 to 6
- queries: bfloat16 [16, 2048, 2, 4096], P('dp', 'seq'), may hold values from -7 to 7
- keys: bfloat16 [16, 2048, 1024], P('dp', 'seq'), may hold values from -7 to 7
- cotangent: bfloat16 [16, 2048, 2, 4096], P('dp', 'seq'), may hold values from -6 to 6
- segments: int32 [16, 2048], P('dp'), may hold values from 0 to 7, never falling along the last dimension, each value on 1 to 512 neighbouring positions
- weight: bfloat16 [1024, 7168], P(None, 'seq'), may hold values from -6 to 6
- master: float32 [1024, 7168], P('dp', 'seq'), may hold values from -6 to 6
- first_moment: float32 [1024, 7168], P('dp', 'seq'), may hold values from -6 to 6
- second_moment: float32 [1024, 7168], P('dp', 'seq'), may hold values from 0.5 to 4
Outputs:
- attention: bfloat16 [16, 2, 2048, 4096], P('dp', None, None, 'seq')
- new_master: float32 [1024, 7168], P('dp', 'seq')
- new_first: float32 [1024, 7168], P('dp', 'seq')
- new_second: float32 [1024, 7168], P('dp', 'seq')
- new_weight: bfloat16 [1024, 7168], P(None, 'seq')
All inputs are finite; a program needn't handle non-finite values.
Results may differ from a plain program's by a relative error of at most 0.024.
Values may be sent and summed in bfloat16 or wider, within the bound.
No kernel may reach another device: no remote copies, remote signals or barrier semaphores. Data moves between devices by JAX's collectives and lax.ppermute only.
A program may use at most 128 MiB of HBM per device.

v0:
```python
import jax
import jax.numpy as jnp
from jax import lax
from jax.sharding import PartitionSpec as P

D = 7168
KVH = 8
HD = 128


beta_one = 0.9
beta_two = 0.95
rate = 0.05
stability_offset = 1e-08
first_fix = 1.0 - 0.9**20
second_fix = 1.0 - 0.95**20


def adam_update(gradient, master, first_moment, second_moment):
    new_first = beta_one * first_moment + (1.0 - beta_one) * gradient
    new_second = beta_two * second_moment + (1.0 - beta_two) * gradient * gradient
    step_size = new_first / first_fix / (jnp.sqrt(new_second / second_fix) + stability_offset)
    new_master = master - rate * step_size
    return (new_master, new_first, new_second)


def attend_blocks(heads, gradient_list, key_head, value_tensors, seg):
    length = heads.shape[1]
    block_rows = min(512, length)
    positions = jnp.arange(length)
    outputs = []
    value_grad = jnp.zeros((value_tensors.shape[0], length), jnp.float32)
    for start_row_index in range(0, length, block_rows):
        final_row_index = start_row_index + block_rows
        scores = jnp.einsum(
            "hyc,sc->hys",
            heads[:, start_row_index:final_row_index],
            key_head[:final_row_index],
            preferred_element_type=jnp.float32,
        ) * HD ** (-0.5)
        allowed = (seg[start_row_index:final_row_index, None] == seg[None, :final_row_index]) & (
            positions[start_row_index:final_row_index, None] >= positions[None, :final_row_index]
        )
        row_max = jnp.max(jnp.where(allowed, scores, -jnp.inf), axis=-1, keepdims=True)
        exp_scores = jnp.where(allowed, jnp.exp(scores - row_max), 0.0)
        probabilities = (exp_scores / jnp.sum(exp_scores, axis=-1, keepdims=True)).astype(
            jnp.bfloat16
        )
        outputs.append(
            jnp.einsum(
                "inp,jp->inj",
                probabilities,
                value_tensors[:, :final_row_index],
                preferred_element_type=jnp.float32,
            ).astype(jnp.bfloat16)
        )
        contrib = jnp.einsum(
            "nmp,nmh->hp",
            probabilities,
            gradient_list[:, start_row_index:final_row_index],
            preferred_element_type=jnp.float32,
        )
        value_grad = value_grad + jnp.pad(contrib, ((0, 0), (0, length - final_row_index)))
    return (jnp.concatenate(outputs, axis=1), value_grad)


def per_device(
    hidden, queries, keys, cotangent, segments, weight, master, first_moment, second_moment
):
    groups = lax.axis_size("seq")
    repeat = groups // KVH
    tok_rows = hidden.shape[1]
    scale = D ** (-0.5)
    key_copies = jnp.broadcast_to(
        keys[0].reshape(tok_rows, KVH, 1, HD), (tok_rows, KVH, repeat, HD)
    ).reshape(tok_rows, 1, KVH * repeat * HD)
    query_ex, grad_ex, key_ex, feature_ex = (
        lax.all_to_all(queries[0], "seq", split_axis=2, concat_axis=0, tiled=True),
        lax.all_to_all(cotangent[0], "seq", split_axis=2, concat_axis=0, tiled=True),
        lax.all_to_all(key_copies, "seq", split_axis=2, concat_axis=0, tiled=True),
        lax.all_to_all(
            hidden[0].reshape(tok_rows, 1, D), "seq", split_axis=2, concat_axis=0, tiled=True
        ),
    )
    length = query_ex.shape[0]
    local_heads = query_ex.shape[2] // HD
    key_head = key_ex[:, 0, :]
    feature_rows = feature_ex[:, 0, :]
    value_width = weight.shape[0]
    weight_copies = jnp.broadcast_to(
        weight.reshape(KVH, 1, HD, weight.shape[1]), (KVH, repeat, HD, weight.shape[1])
    ).reshape(KVH * repeat * HD, weight.shape[1])
    value_tensors = lax.psum_scatter(
        (
            lax.dot_general(
                weight_copies,
                feature_rows,
                (((1,), (1,)), ((), ())),
                preferred_element_type=jnp.float32,
            )
            * scale
        ).astype(jnp.bfloat16),
        "seq",
        scatter_dimension=0,
        tiled=True,
    )
    heads = query_ex.reshape(length, 2 * local_heads, HD).transpose(1, 0, 2)
    gradient_list = grad_ex.reshape(length, 2 * local_heads, HD).transpose(1, 0, 2)
    attended, value_grad = attend_blocks(heads, gradient_list, key_head, value_tensors, segments[0])
    grad_part = value_grad.astype(jnp.bfloat16)
    every_part = lax.all_gather(grad_part, "seq", axis=0, tiled=True)
    summed = (
        jnp.sum(every_part.reshape(KVH, repeat, HD, length).astype(jnp.float32), axis=1)
        .astype(jnp.bfloat16)
        .reshape(value_width, length)
    )
    gradient = jnp.dot(summed, feature_rows, preferred_element_type=jnp.float32) * scale
    gradient_slice = lax.psum_scatter(
        gradient.astype(jnp.bfloat16), "dp", scatter_dimension=0, tiled=True
    ).astype(jnp.float32)
    new_master, new_first, new_second = adam_update(
        gradient_slice, master, first_moment, second_moment
    )
    fresh = lax.all_gather(new_master.astype(jnp.bfloat16), "dp", axis=0, tiled=True)
    attention = (
        attended.reshape(2, local_heads, length, HD)
        .transpose(0, 2, 1, 3)
        .reshape(1, 2, length, local_heads * HD)
    )
    return (attention, new_master, new_first, new_second, fresh)


def solution(mesh):
    in_specs = (
        P("dp", "seq", None),
        P("dp", "seq", None, None),
        P("dp", "seq", None),
        P("dp", "seq", None, None),
        P("dp", None),
        P(None, "seq"),
        P("dp", "seq"),
        P("dp", "seq"),
        P("dp", "seq"),
    )
    out_specs = (
        P("dp", None, None, "seq"),
        P("dp", "seq"),
        P("dp", "seq"),
        P("dp", "seq"),
        P(None, "seq"),
    )
    return jax.shard_map(
        per_device, mesh=mesh, in_specs=in_specs, out_specs=out_specs, check_vma=False
    )
```

profile of v0, /device:TPU:33, one launch (start us, length us, event | category | flops | bytes accessed | tf_op | source)
XLA Modules:
  0.0 800.5 jit_solution(13620617866045864057)
XLA Ops:
  7.2 1.1 copy.105
  8.4 8.1 %copy.132 = bf16[128,1,2048]{0,1,2:T(2,128)(2,1)S(1)} copy(bf16[128,1,2048]{0,2,1:T(8,128)(2,1)S(1)} %bitcast.150) | data formatting | bytes 1048576 | tf_op jit(solution)/shard_map/reshape | solution.py:76
  17.1 11.5 %reduce.3 = bf16[2048,128]{1,0:T(8,128)(2,1)S(1)} reduce(bf16[2048,1,128]{2,1,0:T(2,128)(2,1)S(1)} %bitcast.149, bf16[]{:T(256)} %broadcast.44), dimensions={1}, to_apply=%bitcast.126.reduce_sub_computation | reduce | bytes 1048578
  29.5 7.9 all-to-all-start.1
  37.4 8.0 %copy.80 = bf16[1,128,2,4096]{1,2,3,0:T(2,128)(2,1)} copy(bf16[1,128,2,4096]{3,2,1,0:T(2,128)(2,1)} %param.10) | data formatting | bytes 4194304 | tf_op args[1]
  45.4 4.5 all-to-all-done.1
  49.9 6.8 all-to-all-start
  56.8 8.0 %copy.94 = bf16[1,128,2,4096]{1,2,3,0:T(2,128)(2,1)} copy(bf16[1,128,2,4096]{3,2,1,0:T(2,128)(2,1)} %param.12) | data formatting | bytes 4194304 | tf_op args[3]
  64.8 38.5 %all-to-all-done = bf16[128,2,4096]{0,1,2:T(2,128)(2,1)S(1)} async-done(((bf16[128,2,4096]{0,1,2:T(2,128)(2,1)}), bf16[128,2,4096]{0,1,2:T(2,128)(2,1)S(1)}, u32[]{:S(2)}, u32[]{:S(2)}) %all-to-all-start) | async-done | bytes 2097184 | tf_op jit(solution)/shard_map/all_to_all | solution.py:78
  103.3 7.6 all-to-all-start.3
  111.3 1.0 compare_and_fusion.2
  112.3 1.3 compare_and_fusion.1
  113.6 2.2 fusion.28
  115.8 1.6 compare_and_fusion
  117.4 1.8 reshape.98
  119.1 1.3 copy.107
  120.5 1.0 copy.92
  122.7 2.7 copy.131
  125.4 2.8 reshape.76
  128.2 2.5 copy.82
  130.7 26.8 %all-to-all-done.3 = bf16[128,2,4096]{0,1,2:T(2,128)(2,1)} async-done(((bf16[128,2,4096]{0,1,2:T(2,128)(2,1)}), bf16[128,2,4096]{0,1,2:T(2,128)(2,1)}, u32[]{:S(2)}, u32[]{:S(2)}) %all-to-all-start.3) | async-done | bytes 2097184 | tf_op jit(solution)/shard_map/all_to_all | solution.py:79
  157.5 2.9 copy.130
  160.5 2.3 reshape.81
  162.8 4.1 copy.96
  166.8 3.9 fusion.105
  170.7 2.8 divide_convert_fusion.3
  173.6 2.5 convolution_bitcast_fusion.3
  176.0 8.2 %fusion.100 = (f32[4,512]{1,0:T(4,128)S(1)}, f32[4,512,1024]{2,1,0:T(8,128)}) fusion(pred[512,1024]{1,0:T(8,128)(4,1)S(1)} %copy-done.7, bf16[1024,128,1]{1,0,2:T(8,128)(2,1)S(1)} %bitcast.162, bf16[4,2048,128]{2,1,0:T(8,128)(2,1)} %bitcast.142), kind=kOutput, calls=%fused_computation.109 | convolution fusion | flops 1086325760 | bytes 11018240 | tf_op jit(solution)/shard_map/sub | solution.py:45
  184.2 4.4 divide_convert_fusion.2
  188.6 2.0 copy-done.3
  190.6 3.3 convolution_bitcast_fusion.2
  193.9 6.3 fusion.56
  200.2 16.4 %fusion.99 = (f32[4,512]{1,0:T(4,128)S(1)}, f32[4,512,1536]{2,1,0:T(8,128)}) fusion(f32[4,512,1536]{2,1,0:T(8,128)} %fusion.56, pred[512,1536]{1,0:T(8,128)(4,1)S(1)} %copy-done.6), kind=kOutput, calls=%fused_computation.108 | output fusion | flops 18875904 | bytes 25960448 | tf_op jit(solution)/shard_map/sub | solution.py:45
  216.6 8.8 %divide_convert_fusion.1 = bf16[4,512,1536]{2,1,0:T(8,128)(2,1)} fusion(f32[4,512,1536]{2,1,0:T(8,128)} %get-tuple-element.41, f32[4,512]{1,0:T(4,128)S(1)} %get-tuple-element.40), kind=kLoop, calls=%fused_computation.10 | loop fusion | flops 6291456 | bytes 18882560 | tf_op jit(solution)/shard_map/convert_element_type | solution.py:46
  225.4 5.7 convolution_bitcast_fusion.1
  231.1 13.4 %fusion.94 = (f32[4,512]{1,0:T(4,128)S(1)}, f32[4,512,2048]{2,1,0:T(8,128)}) fusion(pred[512,2048]{1,0:T(8,128)(4,1)S(1)} %copy-done.5, bf16[2048,128,1]{1,0,2:T(8,128)(2,1)} %bitcast.161, bf16[4,2048,128]{2,1,0:T(8,128)(2,1)} %bitcast.143), kind=kOutput, calls=%fused_computation.107 | convolution fusion | flops 2172651520 | bytes 20979712 | tf_op jit(solution)/shard_map/sub | solution.py:45
  244.4 7.3 divide_convert_fusion
  251.7 3.2 copy-done
  254.9 4.4 fusion.34
  259.3 8.6 %copy.87 = bf16[128,1,7168]{0,1,2:T(2,128)(2,1)} copy(bf16[128,1,7168]{2,0,1:T(8,128)(2,1)} %bitcast.158) | data formatting | bytes 3670016 | tf_op jit(solution)/shard_map/reshape;squeeze | solution.py:82
  267.9 41.2 %reduce.4 = bf16[7168,128]{1,0:T(8,128)(2,1)} reduce(bf16[7168,1,128]{2,1,0:T(2,128)(2,1)} %bitcast.127, bf16[]{:T(256)} %broadcast.44), dimensions={1}, to_apply=%bitcast.105.reduce_sub_computation | reduce | bytes 3670018
  309.1 4.8 reshape.99
  313.9 7.7 all-to-all-start.2
  321.6 1.5 copy.106
  323.1 79.8 %all-to-all-done.2 = bf16[16,2,28672]{2,1,0:T(2,128)(2,1)} async-done(((bf16[16,2,28672]{2,1,0:T(2,128)(2,1)}), bf16[16,2,28672]{2,1,0:T(2,128)(2,1)}, u32[]{:S(2)}, u32[]{:S(2)}) %all-to-all-start.2) | async-done | bytes 1835040 | tf_op jit(solution)/shard_map/all_to_all | solution.py:81
  402.9 10.2 %reshape.100 = bf16[7168,1,128]{2,1,0:T(2,128)(2,1)} reshape(bf16[16,2,28672]{2,1,0:T(2,128)(2,1)} %all-to-all-done.2) | data formatting | bytes 3670016
  413.1 2.3 copy.108
  415.4 1.2 copy.88
  416.8 1.0 copy-done.4
  417.8 7.1 multiply_convert_fusion
  425.0 58.9 %all-gather.2.cloned.1.call-done = bf16[2048,2048]{0,1:T(8,128)(2,1)} async-done(((bf16[128,2048]{0,1:T(8,128)(2,1)}), bf16[2048,2048]{0,1:T(8,128)(2,1)}) %all-gather.2.cloned.1.call-update) | async-done | bytes 8388624 | tf_op jit(solution)/shard_map/all_gather | solution.py:111
  483.9 14.5 %reshape.82 = bf16[8,2,128,2048]{2,1,0,3:T(2,128)(2,1)} reshape(bf16[2048,2048]{0,1:T(8,128)(2,1)} %all-gather.2.cloned.1.call-done) | data formatting | bytes 16777216 | tf_op jit(solution)/shard_map/reshape | solution.py:113
  498.4 23.7 %reduce_sum.52 = bf16[8,128,2048]{1,0,2:T(8,128)(2,1)} reduce(bf16[8,2,128,2048]{2,1,0,3:T(2,128)(2,1)} %reshape.82, bf16[]{:T(256)} %constant.5.clone.1), dimensions={1}, to_apply=%region_9.10 | reduce | flops 2097152 | bytes 12582914 | tf_op jit(solution)/shard_map/reduce_sum | solution.py:113
  522.1 6.2 multiply_convert_fusion.1
  528.4 143.5 %reduce-scatter.3.cloned.1.call-done = bf16[128,2048]{1,0:T(8,128)(2,1)} async-done(((bf16[2048,2048]{1,0:T(8,128)(2,1)}), bf16[128,2048]{1,0:T(8,128)(2,1)}) %reduce-scatter.3.cloned.1.call-update) | async-done | bytes 524304 | tf_op jit(solution)/shard_map/reduce_scatter | solution.py:93
  671.9 3.6 convolution_convert_fusion.1
  676.3 4.9 convolution_convert_fusion
  681.3 2.4 convolution_convert_fusion.2
  683.9 20.0 %copy.93 = bf16[2,2048,2,128]{3,2,1,0:T(2,128)(2,1)S(1)} copy(bf16[2,2048,2,128]{3,1,2,0:T(8,128)(2,1)S(1)} %bitcast.134) | data formatting | bytes 4194304 | tf_op jit(solution)/shard_map/transpose | solution.py:127
  703.9 2.6 reshape.80
  706.5 52.3 %reduce-scatter.5.cloned.1.call-done = bf16[64,448]{1,0:T(8,128)(2,1)} async-done(((bf16[1024,448]{1,0:T(8,128)(2,1)}), bf16[64,448]{1,0:T(8,128)(2,1)}) %reduce-scatter.5.cloned.1.call-update) | async-done | bytes 57360 | tf_op jit(solution)/shard_map/reduce_scatter | solution.py:118
  758.8 1.6 fusion.90
  760.5 31.8 %all_gather.7 = bf16[1024,448]{1,0:T(8,128)(2,1)S(1)} all-gather(bf16[64,448]{1,0:T(8,128)(2,1)S(1)} %get-tuple-element.30), channel_id=1, replica_groups=mesh['dp'=16,'seq'=16] {'dp'}, dimensions={0}, use_global_device_ids=true | all-gather | bytes 974848 | tf_op jit(solution)/shard_map/all_gather | solution.py:124
  792.2 1.3 copy.100
  (66 shorter events, 4.4 us)
Async XLA Ops:
  29.5 20.4 %all-to-all-start.1 = ((bf16[16,2,8192]{2,1,0:T(2,128)(2,1)}), bf16[16,2,8192]{2,1,0:T(2,128)(2,1)S(1)}, u32[]{:S(2)}, u32[]{:S(2)}) async-start(bf16[16,2,8192]{2,1,0:T(2,128)(2,1)} %reshape.97), calls=%async_computation.1 | async-start | bytes 1048576 | tf_op jit(solution)/shard_map/all_to_all | solution.py:80
  49.9 53.4 %all-to-all-start = ((bf16[128,2,4096]{0,1,2:T(2,128)(2,1)}), bf16[128,2,4096]{0,1,2:T(2,128)(2,1)S(1)}, u32[]{:S(2)}, u32[]{:S(2)}) async-start(bf16[128,2,4096]{0,1,2:T(2,128)(2,1)} %bitcast.133), calls=%async_computation | async-start | bytes 4194304 | tf_op jit(solution)/shard_map/all_to_all | solution.py:78
  56.7 54.5 %copy-start.13 = (s32[1,2048]{1,0:T(1,128)S(1)}, s32[1,2048]{1,0:T(1,128)}, u32[]{:S(2)}) copy-start(s32[1,2048]{1,0:T(1,128)} %param.13) | copy-start | bytes 24580
  56.8 55.6 %slice-start.2 = ((s32[1,2048]{1,0:T(1,128)}), s32[1,1024]{1,0:T(1,128)S(1)}, s32[]{:S(2)}) async-start(s32[1,2048]{1,0:T(1,128)} %param.13), calls=%async_computation.11 | async-start | bytes 8192 | tf_op jit(solution)/shard_map/slice | solution.py:41
  103.3 54.2 %all-to-all-start.3 = ((bf16[128,2,4096]{0,1,2:T(2,128)(2,1)}), bf16[128,2,4096]{0,1,2:T(2,128)(2,1)}, u32[]{:S(2)}, u32[]{:S(2)}) async-start(bf16[128,2,4096]{0,1,2:T(2,128)(2,1)} %bitcast.132), calls=%async_computation.4 | async-start | bytes 4194304 | tf_op jit(solution)/shard_map/all_to_all | solution.py:79
  110.9 372.9 %all-gather.2.cloned.1.call-start = ((), (), s32[]{:S(2)}) async-start(), calls=%async_computation.7 | async-start | bytes 8912896 | tf_op jit(solution)/shard_map/all_gather | solution.py:111
  160.4 6.4 copy-start.8
  160.5 6.4 copy-start.12
  162.8 4.1 copy-start.1
  170.7 5.3 copy-start.7
  188.6 2.0 copy-start.3
  190.6 3.3 copy-start.2
  193.9 6.3 copy-start.6
  225.4 5.7 copy-start.5
  244.4 10.5 %copy-start.15 = (f32[128,512]{0,1:T(8,128)S(1)}, f32[128,512]{0,1:T(8,128)}, u32[]{:S(2)}) copy-start(f32[128,512]{0,1:T(8,128)} %convolution_bitcast_fusion.3) | copy-start | bytes 786436
  244.4 10.5 %copy-start.16 = (f32[128,1024]{0,1:T(8,128)S(1)}, f32[128,1024]{0,1:T(8,128)}, u32[]{:S(2)}) copy-start(f32[128,1024]{0,1:T(8,128)} %convolution_bitcast_fusion.2) | copy-start | bytes 1572868
  244.4 10.5 %copy-start.17 = (f32[128,1536]{0,1:T(8,128)S(1)}, f32[128,1536]{0,1:T(8,128)}, u32[]{:S(2)}) copy-start(f32[128,1536]{0,1:T(8,128)} %convolution_bitcast_fusion.1) | copy-start | bytes 2359300
  251.7 3.2 copy-start
  313.9 89.0 %all-to-all-start.2 = ((bf16[16,2,28672]{2,1,0:T(2,128)(2,1)}), bf16[16,2,28672]{2,1,0:T(2,128)(2,1)}, u32[]{:S(2)}, u32[]{:S(2)}) async-start(bf16[16,2,28672]{2,1,0:T(2,128)(2,1)} %reshape.99), calls=%async_computation.2 | async-start | bytes 3670016 | tf_op jit(solution)/shard_map/all_to_all | solution.py:81
  321.5 350.4 %reduce-scatter.3.cloned.1.call-start = ((), (), s32[]{:S(2)}) async-start(), calls=%async_computation.6 | async-start | bytes 8912896 | tf_op jit(solution)/shard_map/reduce_scatter | solution.py:93
  416.6 1.2 copy-start.4
  424.9 333.9 %reduce-scatter.5.cloned.1.call-start = ((), (), s32[]{:S(2)}) async-start(), calls=%async_computation.8 | async-start | bytes 1114112 | tf_op jit(solution)/shard_map/reduce_scatter | solution.py:118
  671.9 3.6 copy-start.14
  671.9 9.3 %slice-start = ((s8[8388608]{0:T(1024)(128)(4,1)}), s8[4194304]{0:T(1024)(128)(4,1)S(1)}, s32[]{:S(2)}) async-start(s8[8388608]{0:T(1024)(128)(4,1)} %bitcast.129), calls=%async_computation.9 | async-start | bytes 8388608
  675.6 5.7 slice-start.1
  683.8 75.0 %copy-start.9 = (f32[64,448]{1,0:T(8,128)S(1)}, f32[64,448]{1,0:T(8,128)}, u32[]{:S(2)}) copy-start(f32[64,448]{1,0:T(8,128)} %param.15) | copy-start | bytes 344068
  683.8 75.0 %copy-start.10 = (f32[64,448]{1,0:T(8,128)S(1)}, f32[64,448]{1,0:T(8,128)}, u32[]{:S(2)}) copy-start(f32[64,448]{1,0:T(8,128)} %param.16) | copy-start | bytes 344068
  683.9 75.0 %copy-start.11 = (f32[64,448]{1,0:T(8,128)S(1)}, f32[64,448]{1,0:T(8,128)}, u32[]{:S(2)}) copy-start(f32[64,448]{1,0:T(8,128)} %param.17) | copy-start | bytes 344068
Sparse Core Ops, SparseCore 0:
  259.4 224.3 all-gather.1
  486.4 185.4 reduce-scatter.2
  676.0 82.7 reduce-scatter.4
where the time goes:
time: 813 us; the launch traced here: 800 us
  waiting for transfers between devices  405 us (50%)
  other arithmetic  124 us (15%)
  local copies, waits for them, and re-layouts  123 us (15%)
  matrix products  72.5 us (9%)
  blocking collectives  31.8 us (4%)
  starting transfers between devices  30.4 us (4%)
  between operations  14.6 us (2%)
    reduce_scatter x1, waiting for transfers between devices, per_device(): lax.psum_scatter((lax.dot_general(weight_copies, feature_rows, (((1,), (1...  144 us
    all_to_all x1, waiting for transfers between devices, per_device(): lax.all_to_all(hidden[0].reshape(tok_rows, 1, D), 'seq', split_axis=2, co...  79.8 us
    all_gather x1, waiting for transfers between devices, per_device(): every_part = lax.all_gather(grad_part, 'seq', axis=0, tiled=True)  58.9 us
    unnamed x3, other arithmetic  52.7 us
    reduce_scatter x1, waiting for transfers between devices, per_device(): lax.psum_scatter(gradient.astype(jnp.bfloat16), 'dp', scatter_dimension=0...  52.3 us
    unnamed x50, local copies, waits for them, and re-layouts  45.3 us
    all_to_all x1, waiting for transfers between devices, per_device(): lax.all_to_all(queries[0], 'seq', split_axis=2, concat_axis=0, tiled=True)  38.5 us
    all_gather x1, blocking collectives, per_device(): lax.all_gather(new_master.astype(jnp.bfloat16), 'dp', axis=0, tiled=True)  31.8 us
  transfers between devices with their start and end apart: 7, of which 7 were waited for; matrix products, arithmetic and copies ran while one was open for 24% of the time, Pallas kernels for 0%

commit v1 on v0

v1 whole, which is shorter than its diff:
```python
import jax
import jax.numpy as jnp
from jax import lax
from jax.experimental import pallas as pl
from jax.experimental.pallas import tpu as pltpu
from jax.sharding import Mesh, PartitionSpec as P

D = 7168
KVH = 8
HD = 128
BLOCK = 128
BACK = 5
FEATS = D // 4
LOG2E = 1.4426950408889634
MASKED = -1e30
VMEM_LIMIT = 48 * 1024 * 1024

beta_one = 0.9
beta_two = 0.95
rate = 0.05
stability_offset = 1e-08
first_fix = 1.0 - 0.9**20
second_fix = 1.0 - 0.95**20

bf16 = jnp.bfloat16
f32 = jnp.float32
DP = ("zh", "y", "core")
SEQ = ("x", "z")


def adam_update(gradient, master, first_moment, second_moment):
    new_first = beta_one * first_moment + (1.0 - beta_one) * gradient
    new_second = beta_two * second_moment + (1.0 - beta_two) * gradient * gradient
    step_size = new_first / first_fix / (jnp.sqrt(new_second / second_fix) + stability_offset)
    new_master = master - rate * step_size
    return (new_master, new_first, new_second)


def params(**more):
    return pltpu.CompilerParams(vmem_limit_bytes=VMEM_LIMIT, **more)


def cost(flops, nbytes, exps=0):
    return pl.CostEstimate(flops=flops, bytes_accessed=nbytes, transcendentals=exps)


def pack_columns(rows):
    tokens, width = rows.shape
    part = width // 4

    def body(in_ref, out_ref):
        out_ref[0] = in_ref[...]

    return pl.pallas_call(
        body,
        grid=(4,),
        in_specs=[pl.BlockSpec((tokens, part), lambda i: (0, i))],
        out_specs=pl.BlockSpec((1, tokens, part), lambda i: (i, 0, 0)),
        out_shape=jax.ShapeDtypeStruct((4, tokens, part), rows.dtype),
        compiler_params=params(),
        cost_estimate=cost(0, 4 * tokens * width),
        name="pack_columns",
    )(rows)


def pack_layers(rows):
    tokens, layers, width = rows.shape
    part = width // 4

    def body(in_ref, out_ref):
        out_ref[0] = jnp.swapaxes(in_ref[...], 0, 1)

    return pl.pallas_call(
        body,
        grid=(4,),
        in_specs=[pl.BlockSpec((tokens, layers, part), lambda i: (0, 0, i))],
        out_specs=pl.BlockSpec((1, layers, tokens, part), lambda i: (i, 0, 0, 0)),
        out_shape=jax.ShapeDtypeStruct((4, layers, tokens, part), rows.dtype),
        compiler_params=params(),
        cost_estimate=cost(0, 4 * tokens * layers * width),
        name="pack_layers",
    )(rows)


def key_places(i, z):
    places = []
    for back in range(BACK):
        if back == 0:
            at = i
        elif back == 4:
            at = i - 1
        else:
            at = jnp.where(z < back, i - 1, i)
        places.append((back % 4, jnp.maximum(at, 0)))
    return places


def mask_bias(i, z, start_row):
    block = 4 * i + z
    inside = lax.broadcasted_iota(jnp.int32, (BLOCK, BLOCK), 0)
    query_at = block * BLOCK + lax.broadcasted_iota(jnp.int32, (BLOCK, BLOCK), 1)
    start = jnp.broadcast_to(start_row, (BLOCK, BLOCK))
    pieces = []
    for back in range(BACK):
        key_at = (block - back) * BLOCK + inside
        allowed = key_at >= start
        if back == 0:
            allowed = allowed & (key_at <= query_at)
        pieces.append(jnp.where(allowed, 0.0, MASKED).astype(f32))
    return jnp.concatenate(pieces, axis=0)


def head_rows(ref, kv):
    return jnp.concatenate(
        [
            ref[0, layer, :, pl.ds((4 * kv + head) * HD, HD)]
            for layer in range(2)
            for head in range(4)
        ],
        axis=0,
    )


def exp_scores(key_refs, places, queries, bias, kv):
    keys = jnp.concatenate(
        [key_refs[shift][at, :, pl.ds(kv * HD, HD)] for shift, at in places], axis=0
    )
    scores = lax.dot_general(keys, queries, (((1,), (1,)), ((), ())), preferred_element_type=f32)
    scores = scores * (HD**-0.5 * LOG2E) + jnp.concatenate([bias] * 8, axis=1)
    exps = jnp.exp2(scores - jnp.max(scores, axis=0, keepdims=True))
    return exps, 1.0 / jnp.sum(exps, axis=0, keepdims=True)


def value_grad_kernel(z_ref, start_ref, q_ref, g_ref, k0, k1, k2, k3, o0, o1, o2, o3, acc):
    i = pl.program_id(0)
    z = z_ref[0]

    @pl.when(i == 0)
    def _():
        acc[...] = jnp.zeros_like(acc)

    places = key_places(i, z)
    bias = mask_bias(i, z, start_ref[0])
    for kv in range(2):
        exps, inverse = exp_scores((k0, k1, k2, k3), places, head_rows(q_ref, kv), bias, kv)
        probabilities = (exps * inverse).astype(bf16)
        contrib = jnp.dot(probabilities, head_rows(g_ref, kv), preferred_element_type=f32)
        for back, (shift, at) in enumerate(places):
            acc[shift, at, :, pl.ds(kv * HD, HD)] += contrib[back * BLOCK : (back + 1) * BLOCK]

    @pl.when(i == 3)
    def _():
        for shift, out in enumerate((o0, o1, o2, o3)):
            out[...] = acc[shift].astype(bf16)


def attention_kernel(z_ref, start_ref, q_ref, k0, k1, k2, k3, v0, v1, v2, v3, out_ref):
    i = pl.program_id(0)
    z = z_ref[0]
    places = key_places(i, z)
    bias = mask_bias(i, z, start_ref[0])
    for kv in range(2):
        exps, inverse = exp_scores((k0, k1, k2, k3), places, head_rows(q_ref, kv), bias, kv)
        values = jnp.concatenate(
            [
                ref[at, :, pl.ds(kv * HD, HD)]
                for (shift, at) in places
                for ref in ((v0, v1, v2, v3)[shift],)
            ],
            axis=0,
        )
        mixed = lax.dot_general(
            values, exps.astype(bf16), (((0,), (0,)), ((), ())), preferred_element_type=f32
        )
        mixed = mixed * inverse
        for layer in range(2):
            for head in range(4):
                at = (4 * layer + head) * BLOCK
                out_ref[2 * kv + head // 2, layer, 0, :, pl.ds((head % 2) * HD, HD)] = (
                    mixed[:, at : at + BLOCK].T.astype(bf16)
                )


def attention_specs():
    whole = pl.BlockSpec((4, BLOCK, 2 * HD), lambda i, z: (0, 0, 0))
    start = pl.BlockSpec((1, 1, BLOCK), lambda i, z: (4 * i + z[0], 0, 0))
    heads = pl.BlockSpec((1, 2, BLOCK, 8 * HD), lambda i, z: (i, 0, 0, 0))
    return whole, start, heads


SCORES = 8 * BACK * BLOCK * 8 * BLOCK


def value_grad_parts(z, start, queries, cotangent, keys):
    whole, start_spec, heads = attention_specs()
    part = jax.ShapeDtypeStruct((4, BLOCK, 2 * HD), bf16)
    return pl.pallas_call(
        value_grad_kernel,
        grid_spec=pltpu.PrefetchScalarGridSpec(
            num_scalar_prefetch=1,
            grid=(4,),
            in_specs=[start_spec, heads, heads] + [whole] * 4,
            out_specs=[whole] * 4,
            scratch_shapes=[pltpu.VMEM((4, 4, BLOCK, 2 * HD), f32)],
        ),
        out_shape=[part] * 4,
        compiler_params=params(),
        cost_estimate=cost(4 * HD * SCORES, 6 << 20, SCORES),
        name="value_grad_parts",
    )(z, start, queries, cotangent, *keys)


def attend(z, start, queries, keys, values):
    whole, start_spec, heads = attention_specs()
    return pl.pallas_call(
        attention_kernel,
        grid_spec=pltpu.PrefetchScalarGridSpec(
            num_scalar_prefetch=1,
            grid=(4,),
            in_specs=[start_spec, heads] + [whole] * 8,
            out_specs=pl.BlockSpec((4, 2, 1, BLOCK, 2 * HD), lambda i, z: (0, 0, i, 0, 0)),
        ),
        out_shape=jax.ShapeDtypeStruct((4, 2, 4, BLOCK, 2 * HD), bf16),
        compiler_params=params(),
        cost_estimate=cost(4 * HD * SCORES, 6 << 20, SCORES),
        name="attend",
    )(z, start, queries, *keys, *values)


def value_parts_kernel(at_ref, h_ref, w_ref, a1, a2, a3, b1, b2, b3, out_ref, w_all):
    z = at_ref[0]
    core = at_ref[1]
    half = w_ref.shape[0] // 2
    w_all[pl.ds(pl.multiple_of(z * 2 * half, 16), 2 * half), :] = w_ref[...]
    for shift, (mine, other) in enumerate(((a1, b1), (a2, b2), (a3, b3)), 1):
        base = lax.rem(z + 4 - shift, 4) * 2 * half
        w_all[pl.ds(pl.multiple_of(base + core * half, 16), half), :] = mine[...]
        w_all[pl.ds(pl.multiple_of(base + (1 - core) * half, 16), half), :] = other[...]
    part = jnp.dot(h_ref[...], w_all[...], preferred_element_type=f32)
    out_ref[0] = (part * D**-0.5).astype(bf16)


def value_parts(place, features, weight_rows, mine, other):
    tokens = features.shape[0]
    rows, channels = weight_rows.shape
    piece = pl.BlockSpec((rows // 2, 256), lambda n, at: (0, n))
    return pl.pallas_call(
        value_parts_kernel,
        grid_spec=pltpu.PrefetchScalarGridSpec(
            num_scalar_prefetch=1,
            grid=(channels // 256,),
            in_specs=[
                pl.BlockSpec((tokens, FEATS), lambda n, at: (0, 0)),
                pl.BlockSpec((rows, 256), lambda n, at: (0, n)),
            ]
            + [piece] * 6,
            out_specs=pl.BlockSpec((1, tokens, 256), lambda n, at: (n, 0, 0)),
            scratch_shapes=[pltpu.VMEM((FEATS, 256), bf16)],
        ),
        out_shape=jax.ShapeDtypeStruct((channels // 256, tokens, 256), bf16),
        compiler_params=params(),
        cost_estimate=cost(2 * tokens * FEATS * channels, 7 << 20),
        name="value_parts",
    )(place, features, weight_rows, *mine, *other)


def sum_transposed(pieces):
    def body(p0, p1, p2, p3, out_ref):
        for block in range(4):
            total = (p0[block].astype(f32) + p1[block].astype(f32)) + (
                p2[block].astype(f32) + p3[block].astype(f32)
            )
            out_ref[:, pl.ds(block * BLOCK, BLOCK)] = total.T.astype(bf16)

    return pl.pallas_call(
        body,
        out_shape=jax.ShapeDtypeStruct((2 * HD, 4 * BLOCK), bf16),
        compiler_params=params(),
        cost_estimate=cost(1 << 19, 5 << 18),
        name="sum_transposed",
    )(*pieces)


def gradient_kernel(at_ref, g0, g1, g2, g3, h_ref, keep_ref, send_ref):
    x = at_ref[2]
    low = at_ref[1] == 0
    features = h_ref[...]
    for shift, piece in enumerate((g0, g1, g2, g3)):
        owner = lax.rem(x + 4 - shift, 4)
        part = jnp.dot(piece[...], features, preferred_element_type=f32) * D**-0.5
        for pair in range(2):
            first = part[pair * 128 : pair * 128 + 64].astype(bf16)
            second = part[pair * 128 + 64 : pair * 128 + 128].astype(bf16)
            y = 2 * lax.rem(owner, 2) + pair
            keep_ref[y, owner // 2] = jnp.where(low, first, second)
            send_ref[y, owner // 2] = jnp.where(low, second, first)


def gradient_parts(place, pieces, features):
    tokens = features.shape[0]
    piece = pl.BlockSpec((2 * HD, tokens), lambda n, at: (0, 0))
    out = pl.BlockSpec((4, 2, 64, 256), lambda n, at: (0, 0, 0, n))
    shape = jax.ShapeDtypeStruct((4, 2, 64, FEATS), bf16)
    return pl.pallas_call(
        gradient_kernel,
        grid_spec=pltpu.PrefetchScalarGridSpec(
            num_scalar_prefetch=1,
            grid=(FEATS // 256,),
            in_specs=[piece] * 4 + [pl.BlockSpec((tokens, 256), lambda n, at: (0, n))],
            out_specs=[out, out],
        ),
        out_shape=[shape, shape],
        compiler_params=params(),
        cost_estimate=cost(2 * tokens * FEATS * 1024, 7 << 20),
        name="gradient_parts",
    )(place, *pieces, features)


def sum_and_split(parts):
    width = FEATS // 4

    def body(in_ref, out_ref):
        for zh in range(2):
            total = (in_ref[0, zh].astype(f32) + in_ref[1, zh].astype(f32)) + (
                in_ref[2, zh].astype(f32) + in_ref[3, zh].astype(f32)
            )
            for z in range(4):
                out_ref[4 * zh + z] = total[:, z * width : (z + 1) * width].astype(bf16)

    return pl.pallas_call(
        body,
        out_shape=jax.ShapeDtypeStruct((8, 64, width), bf16),
        compiler_params=params(),
        cost_estimate=cost(1 << 20, 5 << 19),
        name="sum_and_split",
    )(parts)


def join_cores(place, mine, other):
    count, rows, width = mine.shape

    def body(at_ref, mine_ref, other_ref, out_ref):
        low = at_ref[1] == 0
        for at in range(count):
            a = mine_ref[at].astype(f32)
            b = other_ref[at].astype(f32)
            both = jnp.concatenate([jnp.where(low, a, b), jnp.where(low, b, a)], axis=0)
            out_ref[:, pl.ds(at * 2 * rows, 2 * rows)] = both.T.astype(bf16)

    whole = pl.BlockSpec(mine.shape, lambda at: (0, 0, 0))
    return pl.pallas_call(
        body,
        grid_spec=pltpu.PrefetchScalarGridSpec(
            num_scalar_prefetch=1,
            grid=(),
            in_specs=[whole, whole],
            out_specs=pl.BlockSpec((width, 2 * count * rows), lambda at: (0, 0)),
        ),
        out_shape=jax.ShapeDtypeStruct((width, 2 * count * rows), bf16),
        compiler_params=params(),
        cost_estimate=cost(0, 2 << 20),
        name="join_cores",
    )(place, mine, other)


def exchange(parts, axes):
    return lax.all_to_all(parts, axes, split_axis=0, concat_axis=0, tiled=True)


def from_lower(array, axis, shift):
    return lax.ppermute(array, axis, [(i, (i + shift) % 4) for i in range(4)])


def swap_cores(array):
    return lax.ppermute(array, "core", [(0, 1), (1, 0)])


def per_device(
    hidden, queries, keys, cotangent, segments, weight, master, first_moment, second_moment
):
    x, z, core = lax.axis_index("x"), lax.axis_index("z"), lax.axis_index("core")
    place = jnp.stack([z, core, x]).astype(jnp.int32)

    own_keys = exchange(pack_columns(keys[0]), "x")
    own_queries = exchange(pack_layers(queries[0]), "x")
    own_cotangent = exchange(pack_layers(cotangent[0]), "x")
    own_features = exchange(pack_columns(hidden[0]), "x").reshape(4 * BLOCK, FEATS)
    all_keys = [own_keys] + [from_lower(own_keys, "z", shift) for shift in (1, 2, 3)]

    weight_rows = weight.T
    half = weight_rows.shape[0] // 2
    own_half = lax.dynamic_slice_in_dim(weight_rows, core * half, half, 0)
    mine = [from_lower(own_half, "z", shift) for shift in (1, 2, 3)]
    other = [swap_cores(piece) for piece in mine]

    documents = jnp.arange(8, dtype=jnp.int32)
    first_of = jnp.sum((segments[0][None, :] < documents[:, None]).astype(jnp.int32), axis=1)
    start = jnp.sum(
        jnp.where(segments[0][None, :] == documents[:, None], first_of[:, None], 0), axis=0
    ).reshape(16, 1, BLOCK)

    grad_parts = value_grad_parts(place, start, own_queries, own_cotangent, all_keys)
    grad_rows = sum_transposed(
        [grad_parts[0]] + [from_lower(grad_parts[shift], "z", -shift) for shift in (1, 2, 3)]
    )
    pieces = [grad_rows] + [from_lower(grad_rows, "x", shift) for shift in (1, 2, 3)]
    keep, send = gradient_parts(place, pieces, own_features)
    both = (keep.astype(f32) + swap_cores(send).astype(f32)).astype(bf16)
    by_feature = exchange(sum_and_split(exchange(both, "y")), ("zh", "z"))
    gradient = jnp.sum(by_feature.astype(f32), axis=0)
    new_master, new_first, new_second = adam_update(gradient, master, first_moment, second_moment)
    shard = new_master.astype(bf16)
    shards = exchange(jnp.broadcast_to(shard[None], (8,) + shard.shape), ("zh", "y"))
    fresh = join_cores(place, shards, swap_cores(shards)).T

    parts = exchange(value_parts(place, own_features, weight_rows, mine, other), "x")
    own_values = jnp.sum(parts.astype(f32), axis=0).astype(bf16).reshape(4, BLOCK, 2 * HD)
    all_values = [own_values] + [from_lower(own_values, "z", shift) for shift in (1, 2, 3)]
    mixed = exchange(attend(place, start, own_queries, all_keys, all_values), "z")
    attention = mixed.transpose(1, 2, 0, 3, 4).reshape(1, 2, 16 * BLOCK, 2 * HD)
    return (attention, new_master, new_first, new_second, fresh)


def solution(mesh):
    fine = Mesh(mesh.devices.reshape(2, 4, 2, 4, 4), DP + SEQ)
    in_specs = (
        P(DP, SEQ, None),
        P(DP, SEQ, None, None),
        P(DP, SEQ, None),
        P(DP, SEQ, None, None),
        P(DP, None),
        P(None, SEQ),
        P(DP, SEQ),
        P(DP, SEQ),
        P(DP, SEQ),
    )
    out_specs = (
        P(DP, None, None, SEQ),
        P(DP, SEQ),
        P(DP, SEQ),
        P(DP, SEQ),
        P(None, SEQ),
    )
    return jax.shard_map(
        per_device, mesh=fine, in_specs=in_specs, out_specs=out_specs, check_vma=False
    )
```

time: 813 us -> 361 us (0.44); the launches traced: 800 us -> 358 us
  waiting for transfers between devices: 405 us -> 224 us
  other arithmetic: 124 us -> 3.11 us
  local copies, waits for them, and re-layouts: 123 us -> 7.34 us
  matrix products: 72.5 us -> 0 us
  Pallas kernels: 0 us -> 47.1 us
  starting transfers between devices: 30.4 us -> 75.2 us
  blocking collectives: 31.8 us -> 0 us
  between operations: 14.6 us -> 0.85 us
    reduce_scatter x2 -> x0, waiting for transfers between devices: 196 us -> none  [the longest x1 144 us: per_device(): lax.psum_scatter((lax.dot_general(weight_copies, feature_rows, (((1,), (1...]
    ppermute x0 -> x20, waiting for transfers between devices: none -> 104 us  [the longest x15 99.1 us: from_lower(): return lax.ppermute(array, axis, [(i, (i + shift) % 4) for i in range(4)])]
    all_gather x1 -> x0, waiting for transfers between devices: 58.9 us -> none  [per_device(): every_part = lax.all_gather(grad_part, 'seq', axis=0, tiled=True)]
    unnamed x3 -> x0, other arithmetic: 52.7 us -> none
    pallas_call x0 -> x11, Pallas kernels: none -> 47.1 us  [the longest x1 12.3 us: value_grad_parts(): pl.pallas_call(value_grad_kernel, grid_spec=pltpu.PrefetchScalarGridSpec(...]
    dot_general x11 -> x0, matrix products: 47.1 us -> none  [the longest x4 15.8 us: attend_blocks(): jnp.einsum('nmp,nmh->hp', probabilities, gradient_list[:, start_row_index...]
    unnamed x50 -> x28, local copies, waits for them, and re-layouts: 45.3 us -> 2.58 us
    reshape x7 -> x0, local copies, waits for them, and re-layouts: 37 us -> none  [the longest x1 14.5 us: per_device(): every_part.reshape(KVH, repeat, HD, length).astype(jnp.float32)]
  transfers between devices with their start and end apart: 7 -> 29, of which waited for: 7 -> 20; matrix products, arithmetic and copies ran while one was open for 24% -> 1% of each run, Pallas kernels for 0% -> 10%
where the time goes in v1:
time: 361 us; the launch traced here: 358 us
  waiting for transfers between devices  224 us (62%)
  starting transfers between devices  75.2 us (21%)
  Pallas kernels  47.1 us (13%)
  local copies, waits for them, and re-layouts  7.34 us (2%)
    all_to_all x9, waiting for transfers between devices, exchange(): return lax.all_to_all(parts, axes, split_axis=0, concat_axis=0, tiled=True)  120 us
    ppermute x15, waiting for transfers between devices, from_lower(): return lax.ppermute(array, axis, [(i, (i + shift) % 4) for i in range(4)])  99.1 us
    all_to_all x9, starting transfers between devices, exchange(): return lax.all_to_all(parts, axes, split_axis=0, concat_axis=0, tiled=True)  48.5 us
    ppermute x15, starting transfers between devices, from_lower(): return lax.ppermute(array, axis, [(i, (i + shift) % 4) for i in range(4)])  17.6 us
    pallas_call x1, Pallas kernels, value_grad_parts(): pl.pallas_call(value_grad_kernel, grid_spec=pltpu.PrefetchScalarGridSpec(...  12.3 us
    pallas_call x1, Pallas kernels, attend(): pl.pallas_call(attention_kernel, grid_spec=pltpu.PrefetchScalarGridSpec(n...  11.2 us
    ppermute x5, starting transfers between devices, swap_cores(): return lax.ppermute(array, 'core', [(0, 1), (1, 0)])  9.15 us
  transfers between devices with their start and end apart: 29, of which 20 were waited for; matrix products, arithmetic and copies ran while one was open for 1% of the time, Pallas kernels for 10%

profile of v1, /device:TPU:33, one launch (start us, length us, event | category | flops | bytes accessed | tf_op | source)
XLA Modules:
  0.0 357.9 jit_solution(17177092299258019137)
XLA Ops:
  0.6 0.9 copy-done.3
  1.6 1.3 pack_columns.2
  2.9 4.0 %all-to-all-start.1 = ((bf16[4,128,256]{2,1,0:T(8,128)(2,1)}), bf16[4,128,256]{2,1,0:T(8,128)(2,1)S(1)}, u32[]{:S(2)}, u32[]{:S(2)}) async-start(bf16[4,128,256]{2,1,0:T(8,128)(2,1)} %pack_columns.2), calls=%async_computation.1 | async-start | bytes 524288 | tf_op jit(solution)/shard_map/all_to_all | solution.py:367
  6.9 1.6 copy-done
  8.5 2.2 pack_layers.2
  10.7 1.8 all-to-all-done.1.k0
  12.5 4.4 %all-to-all-start = ((bf16[4,2,128,1024]{3,2,1,0:T(8,128)(2,1)}), bf16[4,2,128,1024]{3,2,1,0:T(8,128)(2,1)}, u32[]{:S(2)}, u32[]{:S(2)}) async-start(bf16[4,2,128,1024]{3,2,1,0:T(8,128)(2,1)} %pack_layers.2), calls=%async_computation | async-start | bytes 4194304 | tf_op jit(solution)/shard_map/all_to_all | solution.py:367
  16.9 2.2 pack_layers.3
  19.2 22.1 %all-to-all-done.q_ref = bf16[4,2,128,1024]{3,2,1,0:T(8,128)(2,1)} async-done(((bf16[4,2,128,1024]{3,2,1,0:T(8,128)(2,1)}), bf16[4,2,128,1024]{3,2,1,0:T(8,128)(2,1)}, u32[]{:S(2)}, u32[]{:S(2)}) %all-to-all-start) | async-done | bytes 2097184 | tf_op jit(solution)/shard_map/all_to_all | solution.py:367
  41.3 4.5 %all-to-all-start.5 = ((bf16[4,2,128,1024]{3,2,1,0:T(8,128)(2,1)}), bf16[4,2,128,1024]{3,2,1,0:T(8,128)(2,1)}, u32[]{:S(2)}, u32[]{:S(2)}) async-start(bf16[4,2,128,1024]{3,2,1,0:T(8,128)(2,1)} %pack_layers.3), calls=%async_computation.5 | async-start | bytes 4194304 | tf_op jit(solution)/shard_map/all_to_all | solution.py:367
  45.7 1.9 pack_columns.3
  47.6 21.5 %all-to-all-done.5.g_ref = bf16[4,2,128,1024]{3,2,1,0:T(8,128)(2,1)} async-done(((bf16[4,2,128,1024]{3,2,1,0:T(8,128)(2,1)}), bf16[4,2,128,1024]{3,2,1,0:T(8,128)(2,1)}, u32[]{:S(2)}, u32[]{:S(2)}) %all-to-all-start.5) | async-done | bytes 2097184 | tf_op jit(solution)/shard_map/all_to_all | solution.py:367
  69.2 3.6 %all-to-all-start.2 = ((bf16[4,128,1792]{2,1,0:T(8,128)(2,1)}), bf16[4,128,1792]{2,1,0:T(8,128)(2,1)S(1)}, u32[]{:S(2)}, u32[]{:S(2)}) async-start(bf16[4,128,1792]{2,1,0:T(8,128)(2,1)} %pack_columns.3), calls=%async_computation.2 | async-start | bytes 3670016 | tf_op jit(solution)/shard_map/all_to_all | solution.py:367
  72.8 1.7 collective-permute-start
  74.5 1.5 collective-permute-start.1
  75.9 1.4 collective-permute-start.2
  77.6 0.5 collective-permute-done.k1
  78.1 16.5 %collective-permute-done.1.k2 = bf16[4,128,256]{2,1,0:T(8,128)(2,1)S(1)} collective-permute-done((bf16[4,128,256]{2,1,0:T(8,128)(2,1)S(1)}, bf16[4,128,256]{2,1,0:T(8,128)(2,1)S(1)}, u32[]{:S(2)}, u32[]{:S(2)}) %collective-permute-start.1) | collective-permute-done | bytes 262176 | tf_op jit(solution)/shard_map/ppermute | solution.py:371
  94.6 4.9 %collective-permute-done.2.k3 = bf16[4,128,256]{2,1,0:T(8,128)(2,1)S(1)} collective-permute-done((bf16[4,128,256]{2,1,0:T(8,128)(2,1)S(1)}, bf16[4,128,256]{2,1,0:T(8,128)(2,1)S(1)}, u32[]{:S(2)}, u32[]{:S(2)}) %collective-permute-start.2) | collective-permute-done | bytes 262176 | tf_op jit(solution)/shard_map/ppermute | solution.py:371
  99.5 12.3 %value_grad_parts.1 = (bf16[4,128,256]{2,1,0:T(8,128)(2,1)S(1)}, bf16[4,128,256]{2,1,0:T(8,128)(2,1)S(1)}, bf16[4,128,256]{2,1,0:T(8,128)(2,1)S(1)}, bf16[4,128,256]{2,1,0:T(8,128)(2,1)S(1)}) custom-call(s32[3]{0:T(128)S(1)} %pad_add_fusion.at_ref.z_ref, s32[16,1,128]{2,1,0:T(1,128)S(1)} %bitcast.26, bf16[4,2,128,1024]{3,2,1,0:T(8,128)(2,1)} %all-to-all-done.q_ref, ...), custom_call_target="tpu_custom_call" | custom-call | flops 2684354560 | bytes 6291456 | tf_op jit(solution)/shard_map/value_grad_parts/pallas_call | solution.py:197
  111.9 0.4 collective-permute-start.13
  112.4 1.0 collective-permute-start.14
  113.4 7.1 %collective-permute-done.12.p1 = bf16[4,128,256]{2,1,0:T(8,128)(2,1)S(1)} collective-permute-done((bf16[4,128,256]{2,1,0:T(8,128)(2,1)S(1)}, bf16[4,128,256]{2,1,0:T(8,128)(2,1)S(1)}, u32[]{:S(2)}, u32[]{:S(2)}) %collective-permute-start.12) | collective-permute-done | bytes 262176 | tf_op jit(solution)/shard_map/ppermute | solution.py:371
  120.5 7.8 %collective-permute-done.13.p2 = bf16[4,128,256]{2,1,0:T(8,128)(2,1)S(1)} collective-permute-done((bf16[4,128,256]{2,1,0:T(8,128)(2,1)S(1)}, bf16[4,128,256]{2,1,0:T(8,128)(2,1)S(1)}, u32[]{:S(2)}, u32[]{:S(2)}) %collective-permute-start.13) | collective-permute-done | bytes 262176 | tf_op jit(solution)/shard_map/ppermute | solution.py:371
  128.3 5.6 %collective-permute-done.14.p3 = bf16[4,128,256]{2,1,0:T(8,128)(2,1)S(1)} collective-permute-done((bf16[4,128,256]{2,1,0:T(8,128)(2,1)S(1)}, bf16[4,128,256]{2,1,0:T(8,128)(2,1)S(1)}, u32[]{:S(2)}, u32[]{:S(2)}) %collective-permute-start.14) | collective-permute-done | bytes 262176 | tf_op jit(solution)/shard_map/ppermute | solution.py:371
  134.1 1.4 collective-permute-start.15
  135.6 2.4 collective-permute-start.16
  138.0 0.5 collective-permute-start.17
  138.5 4.3 %collective-permute-done.15.g1 = bf16[256,512]{1,0:T(8,128)(2,1)S(1)} collective-permute-done((bf16[256,512]{1,0:T(8,128)(2,1)S(1)}, bf16[256,512]{1,0:T(8,128)(2,1)S(1)}, u32[]{:S(2)}, u32[]{:S(2)}) %collective-permute-start.15) | collective-permute-done | bytes 262176 | tf_op jit(solution)/shard_map/ppermute | solution.py:371
  142.8 6.7 %collective-permute-done.16.g2 = bf16[256,512]{1,0:T(8,128)(2,1)S(1)} collective-permute-done((bf16[256,512]{1,0:T(8,128)(2,1)S(1)}, bf16[256,512]{1,0:T(8,128)(2,1)S(1)}, u32[]{:S(2)}, u32[]{:S(2)}) %collective-permute-start.16) | collective-permute-done | bytes 262176 | tf_op jit(solution)/shard_map/ppermute | solution.py:371
  149.5 6.4 %gradient_parts.1 = (bf16[4,2,64,1792]{3,2,1,0:T(8,128)(2,1)S(1)}, bf16[4,2,64,1792]{3,2,1,0:T(8,128)(2,1)S(1)}) custom-call(s32[3]{0:T(128)S(1)} %pad_add_fusion.at_ref.z_ref, bf16[256,512]{1,0:T(8,128)(2,1)S(1)} %sum_transposed.1.g0, bf16[256,512]{1,0:T(8,128)(2,1)S(1)} %collective-permute-done.15.g1, bf16[256,512]{1,0:T(8,128)(2,1)S(1)} %collective-permute-done.16.g2, ...), custom_call_target="tpu_custom_call" | custom-call | flops 1879048192 | bytes 7340032 | tf_op jit(solution)/shard_map/gradient_parts/pallas_call | solution.py:304
  155.9 1.4 collective-permute-start.18
  157.3 3.4 collective-permute-done.18
  160.7 1.7 add_convert_fusion
  162.4 4.3 %all-to-all-start.6 = ((bf16[4,2,64,1792]{3,2,1,0:T(8,128)(2,1)}), bf16[4,2,64,1792]{3,2,1,0:T(8,128)(2,1)S(1)}, u32[]{:S(2)}, u32[]{:S(2)}) async-start(bf16[4,2,64,1792]{3,2,1,0:T(8,128)(2,1)} %add_convert_fusion), calls=%async_computation.6 | async-start | bytes 3670016 | tf_op jit(solution)/shard_map/all_to_all | solution.py:367
  166.7 0.8 dynamic-slice_bitcast_fusion
  167.5 2.2 collective-permute-start.3
  169.7 3.3 collective-permute-start.4
  173.0 16.7 %all-to-all-done.6.in_ref = bf16[4,2,64,1792]{3,2,1,0:T(8,128)(2,1)S(1)} async-done(((bf16[4,2,64,1792]{3,2,1,0:T(8,128)(2,1)}), bf16[4,2,64,1792]{3,2,1,0:T(8,128)(2,1)S(1)}, u32[]{:S(2)}, u32[]{:S(2)}) %all-to-all-start.6) | async-done | bytes 1835040 | tf_op jit(solution)/shard_map/all_to_all | solution.py:367
  189.7 1.1 sum_and_split.1
  190.7 10.0 %all-to-all-start.7 = ((bf16[8,64,448]{2,1,0:T(8,128)(2,1)}), bf16[8,64,448]{2,1,0:T(8,128)(2,1)S(1)}, u32[]{:S(2)}, u32[]{:S(2)}) async-start(bf16[8,64,448]{2,1,0:T(8,128)(2,1)} %sum_and_split.1), calls=%async_computation.7 | async-start | bytes 1048576 | tf_op jit(solution)/shard_map/all_to_all | solution.py:367
  200.8 2.1 collective-permute-start.6
  202.8 11.6 %collective-permute-done.4.a2 = bf16[224,1024]{1,0:T(8,128)(2,1)} collective-permute-done((bf16[224,1024]{1,0:T(8,128)(2,1)}, bf16[224,1024]{1,0:T(8,128)(2,1)}, u32[]{:S(2)}, u32[]{:S(2)}) %collective-permute-start.4) | collective-permute-done | bytes 458784 | tf_op jit(solution)/shard_map/ppermute | solution.py:371
  214.5 2.6 collective-permute-start.7
  217.1 1.9 collective-permute-done.5.a3
  219.0 2.4 collective-permute-start.8
  221.5 1.6 collective-permute-done.8.b3
  223.1 6.4 %value_parts.1 = bf16[4,512,256]{2,1,0:T(8,128)(2,1)} custom-call(s32[3]{0:T(128)S(1)} %pad_add_fusion.at_ref.z_ref, bf16[512,1792]{1,0:T(8,128)(2,1)} %bitcast.30, bf16[448,1024]{1,0:T(8,128)(2,1)S(1)} %bitcast.25, bf16[224,1024]{1,0:T(8,128)(2,1)} %collective-permute-done.3.a1, bf16[224,1024]{1,0:T(8,128)(2,1)} %collective-permute-done.4.a2, ...), custom_call_target="tpu_custom_call" | custom-call | flops 1879048192 | bytes 7340032 | tf_op jit(solution)/shard_map/value_parts/pallas_call | solution.py:247
  229.6 3.8 %all-to-all-start.3 = ((bf16[4,512,256]{2,1,0:T(8,128)(2,1)}), bf16[4,512,256]{2,1,0:T(8,128)(2,1)S(1)}, u32[]{:S(2)}, u32[]{:S(2)}) async-start(bf16[4,512,256]{2,1,0:T(8,128)(2,1)} %value_parts.1), calls=%async_computation.3 | async-start | bytes 2097152 | tf_op jit(solution)/shard_map/all_to_all | solution.py:367
  233.5 0.8 fusion.1
  234.3 13.6 %all-to-all-done.3 = bf16[4,512,256]{2,1,0:T(8,128)(2,1)S(1)} async-done(((bf16[4,512,256]{2,1,0:T(8,128)(2,1)}), bf16[4,512,256]{2,1,0:T(8,128)(2,1)S(1)}, u32[]{:S(2)}, u32[]{:S(2)}) %all-to-all-start.3) | async-done | bytes 1048608 | tf_op jit(solution)/shard_map/all_to_all | solution.py:367
  247.9 0.8 broadcast_in_dim.23
  248.8 9.4 %all-to-all-start.8 = ((bf16[8,64,448]{2,1,0:T(8,128)(2,1)}), bf16[8,64,448]{2,1,0:T(8,128)(2,1)S(1)}, u32[]{:S(2)}, u32[]{:S(2)}) async-start(bf16[8,64,448]{2,1,0:T(8,128)(2,1)} %broadcast_in_dim.23), calls=%async_computation.8 | async-start | bytes 1048576 | tf_op jit(solution)/shard_map/all_to_all | solution.py:367
  258.2 0.3 reduce_sum.41
  258.5 0.4 collective-permute-start.11
  258.9 1.1 collective-permute-start.9
  260.1 21.2 %collective-permute-done.10.v2 = bf16[4,128,256]{2,1,0:T(8,128)(2,1)S(1)} collective-permute-done((bf16[4,128,256]{2,1,0:T(8,128)(2,1)S(1)}, bf16[4,128,256]{2,1,0:T(8,128)(2,1)S(1)}, u32[]{:S(2)}, u32[]{:S(2)}) %collective-permute-start.10) | collective-permute-done | bytes 262176 | tf_op jit(solution)/shard_map/ppermute | solution.py:371
  281.2 10.9 %collective-permute-done.11.v3 = bf16[4,128,256]{2,1,0:T(8,128)(2,1)S(1)} collective-permute-done((bf16[4,128,256]{2,1,0:T(8,128)(2,1)S(1)}, bf16[4,128,256]{2,1,0:T(8,128)(2,1)S(1)}, u32[]{:S(2)}, u32[]{:S(2)}) %collective-permute-start.11) | collective-permute-done | bytes 262176 | tf_op jit(solution)/shard_map/ppermute | solution.py:371
  292.2 11.2 %attend.1 = bf16[4,2,4,128,256]{4,3,2,1,0:T(8,128)(2,1)} custom-call(s32[3]{0:T(128)S(1)} %pad_add_fusion.at_ref.z_ref, s32[16,1,128]{2,1,0:T(1,128)S(1)} %bitcast.27, bf16[4,2,128,1024]{3,2,1,0:T(8,128)(2,1)} %all-to-all-done.q_ref, bf16[4,128,256]{2,1,0:T(8,128)(2,1)S(1)} %all-to-all-done.1.k0, bf16[4,128,256]{2,1,0:T(8,128)(2,1)S(1)} %collective-permute-done.k1, ...), custom_call_target="tpu_custom_call" | custom-call | flops 2684354560 | bytes 6291456 | tf_op jit(solution)/shard_map/attend/pallas_call | solution.py:215
  303.3 4.5 %all-to-all-start.4 = ((bf16[4,2,4,128,256]{4,3,2,1,0:T(8,128)(2,1)}), bf16[4,2,4,128,256]{4,3,2,1,0:T(8,128)(2,1)}, u32[]{:S(2)}, u32[]{:S(2)}) async-start(bf16[4,2,4,128,256]{4,3,2,1,0:T(8,128)(2,1)} %attend.1), calls=%async_computation.4 | async-start | bytes 4194304 | tf_op jit(solution)/shard_map/all_to_all | solution.py:367
  307.8 0.6 collective-permute-start.19
  308.4 44.5 %all-to-all-done.4 = bf16[4,2,4,128,256]{4,3,2,1,0:T(8,128)(2,1)} async-done(((bf16[4,2,4,128,256]{4,3,2,1,0:T(8,128)(2,1)}), bf16[4,2,4,128,256]{4,3,2,1,0:T(8,128)(2,1)}, u32[]{:S(2)}, u32[]{:S(2)}) %all-to-all-start.4) | async-done | bytes 2097184 | tf_op jit(solution)/shard_map/all_to_all | solution.py:367
  352.9 3.1 copy.15
  356.0 1.9 join_cores.1
  (43 shorter events, 0.8 us)
Async XLA Ops:
  0.6 1.0 copy-start.3
  2.9 9.6 %all-to-all-start.1 = ((bf16[4,128,256]{2,1,0:T(8,128)(2,1)}), bf16[4,128,256]{2,1,0:T(8,128)(2,1)S(1)}, u32[]{:S(2)}, u32[]{:S(2)}) async-start(bf16[4,128,256]{2,1,0:T(8,128)(2,1)} %pack_columns.2), calls=%async_computation.1 | async-start | bytes 524288 | tf_op jit(solution)/shard_map/all_to_all | solution.py:367
  6.9 1.6 copy-start
  10.7 6.2 %copy-start.1 = (bf16[1,128,2,4096]{3,2,1,0:T(2,128)(2,1)S(1)}, bf16[1,128,2,4096]{3,2,1,0:T(2,128)(2,1)}, u32[]{:S(2)}) copy-start(bf16[1,128,2,4096]{3,2,1,0:T(2,128)(2,1)} %param.12) | copy-start | bytes 6291460
  12.5 28.8 %all-to-all-start = ((bf16[4,2,128,1024]{3,2,1,0:T(8,128)(2,1)}), bf16[4,2,128,1024]{3,2,1,0:T(8,128)(2,1)}, u32[]{:S(2)}, u32[]{:S(2)}) async-start(bf16[4,2,128,1024]{3,2,1,0:T(8,128)(2,1)} %pack_layers.2), calls=%async_computation | async-start | bytes 4194304 | tf_op jit(solution)/shard_map/all_to_all | solution.py:367
  19.2 26.6 %copy-start.2 = (bf16[1,128,7168]{2,1,0:T(8,128)(2,1)S(1)}, bf16[1,128,7168]{2,1,0:T(8,128)(2,1)}, u32[]{:S(2)}) copy-start(bf16[1,128,7168]{2,1,0:T(8,128)(2,1)} %param.9) | copy-start | bytes 5505028
  41.3 27.9 %all-to-all-start.5 = ((bf16[4,2,128,1024]{3,2,1,0:T(8,128)(2,1)}), bf16[4,2,128,1024]{3,2,1,0:T(8,128)(2,1)}, u32[]{:S(2)}, u32[]{:S(2)}) async-start(bf16[4,2,128,1024]{3,2,1,0:T(8,128)(2,1)} %pack_layers.3), calls=%async_computation.5 | async-start | bytes 4194304 | tf_op jit(solution)/shard_map/all_to_all | solution.py:367
  47.6 29.8 %copy-start.13 = (s32[1,2048]{1,0:T(1,128)S(1)}, s32[1,2048]{1,0:T(1,128)}, u32[]{:S(2)}) copy-start(s32[1,2048]{1,0:T(1,128)} %param.13) | copy-start | bytes 24580
  69.2 69.3 %all-to-all-start.2 = ((bf16[4,128,1792]{2,1,0:T(8,128)(2,1)}), bf16[4,128,1792]{2,1,0:T(8,128)(2,1)S(1)}, u32[]{:S(2)}, u32[]{:S(2)}) async-start(bf16[4,128,1792]{2,1,0:T(8,128)(2,1)} %pack_columns.3), calls=%async_computation.2 | async-start | bytes 3670016 | tf_op jit(solution)/shard_map/all_to_all | solution.py:367
  72.8 5.3 %collective-permute-start = (bf16[4,128,256]{2,1,0:T(8,128)(2,1)S(1)}, bf16[4,128,256]{2,1,0:T(8,128)(2,1)S(1)}, u32[]{:S(2)}, u32[]{:S(2)}) collective-permute-start(bf16[4,128,256]{2,1,0:T(8,128)(2,1)S(1)} %all-to-all-done.1.k0), channel_id=1, source_target_pairs={{0,1},{1,2},{2,3},{3,0},{4,5},{5,6},{6,7},{7,4},{8,9},{9,10},{10,1... | collective-permute-start | bytes 786440 | tf_op jit(solution)/shard_map/ppermute | solution.py:371
  74.5 20.1 %collective-permute-start.1 = (bf16[4,128,256]{2,1,0:T(8,128)(2,1)S(1)}, bf16[4,128,256]{2,1,0:T(8,128)(2,1)S(1)}, u32[]{:S(2)}, u32[]{:S(2)}) collective-permute-start(bf16[4,128,256]{2,1,0:T(8,128)(2,1)S(1)} %all-to-all-done.1.k0), channel_id=1, source_target_pairs={{0,2},{1,3},{2,0},{3,1},{4,6},{5,7},{6,4},{7,5},{8,10},{9,11},{10,... | collective-permute-start | bytes 786440 | tf_op jit(solution)/shard_map/ppermute | solution.py:371
  75.9 23.6 %collective-permute-start.2 = (bf16[4,128,256]{2,1,0:T(8,128)(2,1)S(1)}, bf16[4,128,256]{2,1,0:T(8,128)(2,1)S(1)}, u32[]{:S(2)}, u32[]{:S(2)}) collective-permute-start(bf16[4,128,256]{2,1,0:T(8,128)(2,1)S(1)} %all-to-all-done.1.k0), channel_id=1, source_target_pairs={{0,3},{1,0},{2,1},{3,2},{4,7},{5,4},{6,5},{7,6},{8,11},{9,8},{10,9... | collective-permute-start | bytes 786440 | tf_op jit(solution)/shard_map/ppermute | solution.py:371
  94.6 17.2 %copy-start.5 = (bf16[4,128,256]{2,1,0:T(8,128)(2,1)}, bf16[4,128,256]{2,1,0:T(8,128)(2,1)S(1)}, u32[]{:S(2)}) copy-start(bf16[4,128,256]{2,1,0:T(8,128)(2,1)S(1)} %collective-permute-done.1.k2) | copy-start | bytes 786436
  99.5 12.4 %copy-start.7 = (bf16[4,128,256]{2,1,0:T(8,128)(2,1)}, bf16[4,128,256]{2,1,0:T(8,128)(2,1)S(1)}, u32[]{:S(2)}) copy-start(bf16[4,128,256]{2,1,0:T(8,128)(2,1)S(1)} %collective-permute-done.2.k3) | copy-start | bytes 786436
  111.9 8.7 %collective-permute-start.12 = (bf16[4,128,256]{2,1,0:T(8,128)(2,1)S(1)}, bf16[4,128,256]{2,1,0:T(8,128)(2,1)S(1)}, u32[]{:S(2)}, u32[]{:S(2)}) collective-permute-start(bf16[4,128,256]{2,1,0:T(8,128)(2,1)S(1)} %get-tuple-element.12), channel_id=1, source_target_pairs={{0,3},{1,0},{2,1},{3,2},{4,7},{5,4},{6,5},{7,6},{8,11},{9,8},{10,9... | collective-permute-start | bytes 786440 | tf_op jit(solution)/shard_map/ppermute | solution.py:371
  111.9 16.4 %collective-permute-start.13 = (bf16[4,128,256]{2,1,0:T(8,128)(2,1)S(1)}, bf16[4,128,256]{2,1,0:T(8,128)(2,1)S(1)}, u32[]{:S(2)}, u32[]{:S(2)}) collective-permute-start(bf16[4,128,256]{2,1,0:T(8,128)(2,1)S(1)} %get-tuple-element.13), channel_id=1, source_target_pairs={{0,2},{1,3},{2,0},{3,1},{4,6},{5,7},{6,4},{7,5},{8,10},{9,11},{10,... | collective-permute-start | bytes 786440 | tf_op jit(solution)/shard_map/ppermute | solution.py:371
  112.4 21.5 %collective-permute-start.14 = (bf16[4,128,256]{2,1,0:T(8,128)(2,1)S(1)}, bf16[4,128,256]{2,1,0:T(8,128)(2,1)S(1)}, u32[]{:S(2)}, u32[]{:S(2)}) collective-permute-start(bf16[4,128,256]{2,1,0:T(8,128)(2,1)S(1)} %get-tuple-element.14), channel_id=1, source_target_pairs={{0,1},{1,2},{2,3},{3,0},{4,5},{5,6},{6,7},{7,4},{8,9},{9,10},{10,1... | collective-permute-start | bytes 786440 | tf_op jit(solution)/shard_map/ppermute | solution.py:371
  134.1 8.7 %collective-permute-start.15 = (bf16[256,512]{1,0:T(8,128)(2,1)S(1)}, bf16[256,512]{1,0:T(8,128)(2,1)S(1)}, u32[]{:S(2)}, u32[]{:S(2)}) collective-permute-start(bf16[256,512]{1,0:T(8,128)(2,1)S(1)} %sum_transposed.1.g0), channel_id=1, source_target_pairs={{0,4},{4,8},{8,12},{12,0},{1,5},{5,9},{9,13},{13,1},{2,6},{6,10},{... | collective-permute-start | bytes 786440 | tf_op jit(solution)/shard_map/ppermute | solution.py:371
  135.6 13.9 %collective-permute-start.16 = (bf16[256,512]{1,0:T(8,128)(2,1)S(1)}, bf16[256,512]{1,0:T(8,128)(2,1)S(1)}, u32[]{:S(2)}, u32[]{:S(2)}) collective-permute-start(bf16[256,512]{1,0:T(8,128)(2,1)S(1)} %sum_transposed.1.g0), channel_id=1, source_target_pairs={{0,8},{4,12},{8,0},{12,4},{1,9},{5,13},{9,1},{13,5},{2,10},{6,14},... | collective-permute-start | bytes 786440 | tf_op jit(solution)/shard_map/ppermute | solution.py:371
  138.0 11.5 %collective-permute-start.17 = (bf16[256,512]{1,0:T(8,128)(2,1)S(1)}, bf16[256,512]{1,0:T(8,128)(2,1)S(1)}, u32[]{:S(2)}, u32[]{:S(2)}) collective-permute-start(bf16[256,512]{1,0:T(8,128)(2,1)S(1)} %sum_transposed.1.g0), channel_id=1, source_target_pairs={{0,12},{4,0},{8,4},{12,8},{1,13},{5,1},{9,5},{13,9},{2,14},{6,2},{... | collective-permute-start | bytes 786440 | tf_op jit(solution)/shard_map/ppermute | solution.py:371
  138.5 11.0 %copy-start.9 = (bf16[4,128,1792]{2,1,0:T(8,128)(2,1)}, bf16[4,128,1792]{2,1,0:T(8,128)(2,1)S(1)}, u32[]{:S(2)}) copy-start(bf16[4,128,1792]{2,1,0:T(8,128)(2,1)S(1)} %all-to-all-done.2) | copy-start | bytes 5505028
  155.9 4.8 %collective-permute-start.18 = (bf16[4,2,64,1792]{3,2,1,0:T(8,128)(2,1)S(1)}, bf16[4,2,64,1792]{3,2,1,0:T(8,128)(2,1)S(1)}, u32[]{:S(2)}, u32[]{:S(2)}) collective-permute-start(bf16[4,2,64,1792]{3,2,1,0:T(8,128)(2,1)S(1)} %get-tuple-element.16), channel_id=1, source_target_pairs={{0,16},{16,0},{1,17},{17,1},{2,18},{18,2},{3,19},{19,3},{4,20},{20... | collective-permute-start | bytes 5505032 | tf_op jit(solution)/shard_map/ppermute | solution.py:375
  162.4 4.3 %copy-start.4 = (bf16[1024,448]{0,1:T(8,128)(2,1)S(1)}, bf16[1024,448]{0,1:T(8,128)(2,1)}, u32[]{:S(2)}) copy-start(bf16[1024,448]{0,1:T(8,128)(2,1)} %param.14) | copy-start | bytes 2752516
  162.4 27.3 %all-to-all-start.6 = ((bf16[4,2,64,1792]{3,2,1,0:T(8,128)(2,1)}), bf16[4,2,64,1792]{3,2,1,0:T(8,128)(2,1)S(1)}, u32[]{:S(2)}, u32[]{:S(2)}) async-start(bf16[4,2,64,1792]{3,2,1,0:T(8,128)(2,1)} %add_convert_fusion), calls=%async_computation.6 | async-start | bytes 3670016 | tf_op jit(solution)/shard_map/all_to_all | solution.py:367
  167.5 33.3 %collective-permute-start.3 = (bf16[224,1024]{1,0:T(8,128)(2,1)}, bf16[224,1024]{1,0:T(8,128)(2,1)}, u32[]{:S(2)}, u32[]{:S(2)}) collective-permute-start(bf16[224,1024]{1,0:T(8,128)(2,1)} %dynamic-slice_bitcast_fusion), channel_id=1, source_target_pairs={{0,1},{1,2},{2,3},{3,0},{4,5},{5,6},{6,7},{7,4},{8,9},{9,10},{10,1... | collective-permute-start | bytes 1376264 | tf_op jit(solution)/shard_map/ppermute | solution.py:371
  169.7 44.8 %collective-permute-start.4 = (bf16[224,1024]{1,0:T(8,128)(2,1)}, bf16[224,1024]{1,0:T(8,128)(2,1)}, u32[]{:S(2)}, u32[]{:S(2)}) collective-permute-start(bf16[224,1024]{1,0:T(8,128)(2,1)} %dynamic-slice_bitcast_fusion), channel_id=1, source_target_pairs={{0,2},{1,3},{2,0},{3,1},{4,6},{5,7},{6,4},{7,5},{8,10},{9,11},{10,... | collective-permute-start | bytes 1376264 | tf_op jit(solution)/shard_map/ppermute | solution.py:371
  173.0 46.0 %collective-permute-start.5 = (bf16[224,1024]{1,0:T(8,128)(2,1)}, bf16[224,1024]{1,0:T(8,128)(2,1)}, u32[]{:S(2)}, u32[]{:S(2)}) collective-permute-start(bf16[224,1024]{1,0:T(8,128)(2,1)} %dynamic-slice_bitcast_fusion), channel_id=1, source_target_pairs={{0,3},{1,0},{2,1},{3,2},{4,7},{5,4},{6,5},{7,6},{8,11},{9,8},{10,9... | collective-permute-start | bytes 1376264 | tf_op jit(solution)/shard_map/ppermute | solution.py:371
  190.7 38.8 %all-to-all-start.7 = ((bf16[8,64,448]{2,1,0:T(8,128)(2,1)}), bf16[8,64,448]{2,1,0:T(8,128)(2,1)S(1)}, u32[]{:S(2)}, u32[]{:S(2)}) async-start(bf16[8,64,448]{2,1,0:T(8,128)(2,1)} %sum_and_split.1), calls=%async_computation.7 | async-start | bytes 1048576 | tf_op jit(solution)/shard_map/all_to_all | solution.py:367
  200.8 20.7 %collective-permute-start.6 = (bf16[224,1024]{1,0:T(8,128)(2,1)}, bf16[224,1024]{1,0:T(8,128)(2,1)S(1)}, u32[]{:S(2)}, u32[]{:S(2)}) collective-permute-start(bf16[224,1024]{1,0:T(8,128)(2,1)} %collective-permute-done.3.a1), channel_id=1, source_target_pairs={{0,16},{16,0},{1,17},{17,1},{2,18},{18,2},{3,19},{19,3},{4,20},{20... | collective-permute-start | bytes 1376264 | tf_op jit(solution)/shard_map/ppermute | solution.py:375
  214.5 7.0 %collective-permute-start.7 = (bf16[224,1024]{1,0:T(8,128)(2,1)}, bf16[224,1024]{1,0:T(8,128)(2,1)S(1)}, u32[]{:S(2)}, u32[]{:S(2)}) collective-permute-start(bf16[224,1024]{1,0:T(8,128)(2,1)} %collective-permute-done.4.a2), channel_id=1, source_target_pairs={{0,16},{16,0},{1,17},{17,1},{2,18},{18,2},{3,19},{19,3},{4,20},{20... | collective-permute-start | bytes 1376264 | tf_op jit(solution)/shard_map/ppermute | solution.py:375
  219.0 4.1 %collective-permute-start.8 = (bf16[224,1024]{1,0:T(8,128)(2,1)}, bf16[224,1024]{1,0:T(8,128)(2,1)S(1)}, u32[]{:S(2)}, u32[]{:S(2)}) collective-permute-start(bf16[224,1024]{1,0:T(8,128)(2,1)} %collective-permute-done.5.a3), channel_id=1, source_target_pairs={{0,16},{16,0},{1,17},{17,1},{2,18},{18,2},{3,19},{19,3},{4,20},{20... | collective-permute-start | bytes 1376264 | tf_op jit(solution)/shard_map/ppermute | solution.py:375
  229.5 3.9 %copy-start.10 = (f32[64,448]{1,0:T(8,128)S(1)}, f32[64,448]{1,0:T(8,128)}, u32[]{:S(2)}) copy-start(f32[64,448]{1,0:T(8,128)} %param.15) | copy-start | bytes 344068
  229.6 3.9 %copy-start.11 = (f32[64,448]{1,0:T(8,128)S(1)}, f32[64,448]{1,0:T(8,128)}, u32[]{:S(2)}) copy-start(f32[64,448]{1,0:T(8,128)} %param.16) | copy-start | bytes 344068
  229.6 3.9 %copy-start.12 = (f32[64,448]{1,0:T(8,128)S(1)}, f32[64,448]{1,0:T(8,128)}, u32[]{:S(2)}) copy-start(f32[64,448]{1,0:T(8,128)} %param.17) | copy-start | bytes 344068
  229.6 18.3 %all-to-all-start.3 = ((bf16[4,512,256]{2,1,0:T(8,128)(2,1)}), bf16[4,512,256]{2,1,0:T(8,128)(2,1)S(1)}, u32[]{:S(2)}, u32[]{:S(2)}) async-start(bf16[4,512,256]{2,1,0:T(8,128)(2,1)} %value_parts.1), calls=%async_computation.3 | async-start | bytes 2097152 | tf_op jit(solution)/shard_map/all_to_all | solution.py:367
  233.5 58.7 %copy-start.6 = (bf16[4,128,256]{2,1,0:T(8,128)(2,1)S(1)}, bf16[4,128,256]{2,1,0:T(8,128)(2,1)}, u32[]{:S(2)}) copy-start(bf16[4,128,256]{2,1,0:T(8,128)(2,1)} %copy-done.5) | copy-start | bytes 786436
  233.5 58.7 %copy-start.8 = (bf16[4,128,256]{2,1,0:T(8,128)(2,1)S(1)}, bf16[4,128,256]{2,1,0:T(8,128)(2,1)}, u32[]{:S(2)}) copy-start(bf16[4,128,256]{2,1,0:T(8,128)(2,1)} %copy-done.7) | copy-start | bytes 786436
  248.8 54.6 %all-to-all-start.8 = ((bf16[8,64,448]{2,1,0:T(8,128)(2,1)}), bf16[8,64,448]{2,1,0:T(8,128)(2,1)S(1)}, u32[]{:S(2)}, u32[]{:S(2)}) async-start(bf16[8,64,448]{2,1,0:T(8,128)(2,1)} %broadcast_in_dim.23), calls=%async_computation.8 | async-start | bytes 1048576 | tf_op jit(solution)/shard_map/all_to_all | solution.py:367
  258.4 22.8 %collective-permute-start.10 = (bf16[4,128,256]{2,1,0:T(8,128)(2,1)S(1)}, bf16[4,128,256]{2,1,0:T(8,128)(2,1)S(1)}, u32[]{:S(2)}, u32[]{:S(2)}) collective-permute-start(bf16[4,128,256]{2,1,0:T(8,128)(2,1)S(1)} %bitcast.20), channel_id=1, source_target_pairs={{0,2},{1,3},{2,0},{3,1},{4,6},{5,7},{6,4},{7,5},{8,10},{9,11},{10,... | collective-permute-start | bytes 786440 | tf_op jit(solution)/shard_map/ppermute | solution.py:371
  258.5 33.6 %collective-permute-start.11 = (bf16[4,128,256]{2,1,0:T(8,128)(2,1)S(1)}, bf16[4,128,256]{2,1,0:T(8,128)(2,1)S(1)}, u32[]{:S(2)}, u32[]{:S(2)}) collective-permute-start(bf16[4,128,256]{2,1,0:T(8,128)(2,1)S(1)} %bitcast.21), channel_id=1, source_target_pairs={{0,3},{1,0},{2,1},{3,2},{4,7},{5,4},{6,5},{7,6},{8,11},{9,8},{10,9... | collective-permute-start | bytes 786440 | tf_op jit(solution)/shard_map/ppermute | solution.py:371
  258.9 33.2 %collective-permute-start.9 = (bf16[4,128,256]{2,1,0:T(8,128)(2,1)S(1)}, bf16[4,128,256]{2,1,0:T(8,128)(2,1)S(1)}, u32[]{:S(2)}, u32[]{:S(2)}) collective-permute-start(bf16[4,128,256]{2,1,0:T(8,128)(2,1)S(1)} %bitcast.22), channel_id=1, source_target_pairs={{0,1},{1,2},{2,3},{3,0},{4,5},{5,6},{6,7},{7,4},{8,9},{9,10},{10,1... | collective-permute-start | bytes 786440 | tf_op jit(solution)/shard_map/ppermute | solution.py:371
  303.3 49.6 %all-to-all-start.4 = ((bf16[4,2,4,128,256]{4,3,2,1,0:T(8,128)(2,1)}), bf16[4,2,4,128,256]{4,3,2,1,0:T(8,128)(2,1)}, u32[]{:S(2)}, u32[]{:S(2)}) async-start(bf16[4,2,4,128,256]{4,3,2,1,0:T(8,128)(2,1)} %attend.1), calls=%async_computation.4 | async-start | bytes 4194304 | tf_op jit(solution)/shard_map/all_to_all | solution.py:367
  307.8 48.2 %collective-permute-start.19 = (bf16[8,64,448]{2,1,0:T(8,128)(2,1)S(1)}, bf16[8,64,448]{2,1,0:T(8,128)(2,1)S(1)}, u32[]{:S(2)}, u32[]{:S(2)}) collective-permute-start(bf16[8,64,448]{2,1,0:T(8,128)(2,1)S(1)} %all-to-all-done.8.mine_ref), channel_id=1, source_target_pairs={{0,16},{16,0},{1,17},{17,1},{2,18},{18,2},{3,19},{19,3},{4,20},{20... | collective-permute-start | bytes 1376264 | tf_op jit(solution)/shard_map/ppermute | solution.py:375

commit v2 on v1

v2 whole, which is shorter than its diff:
```python
import jax
import jax.numpy as jnp
from jax import lax
from jax.experimental import pallas as pl
from jax.experimental.pallas import tpu as pltpu
from jax.sharding import Mesh, PartitionSpec as P

D = 7168
KVH = 8
HD = 128
BLOCK = 128
BACK = 5
FEATS = D // 4
LOG2E = 1.4426950408889634
MASKED = -1e30
VMEM_LIMIT = 32 * 1024 * 1024

beta_one = 0.9
beta_two = 0.95
rate = 0.05
stability_offset = 1e-08
first_fix = 1.0 - 0.9**20
second_fix = 1.0 - 0.95**20

bf16 = jnp.bfloat16
f32 = jnp.float32
DP = ("zh", "y", "core")
SEQ = ("x", "z")


def adam_update(gradient, master, first_moment, second_moment):
    new_first = beta_one * first_moment + (1.0 - beta_one) * gradient
    new_second = beta_two * second_moment + (1.0 - beta_two) * gradient * gradient
    step_size = new_first / first_fix / (jnp.sqrt(new_second / second_fix) + stability_offset)
    new_master = master - rate * step_size
    return (new_master, new_first, new_second)


def params(**more):
    return pltpu.CompilerParams(vmem_limit_bytes=VMEM_LIMIT, **more)


def cost(flops, nbytes, exps=0):
    return pl.CostEstimate(flops=flops, bytes_accessed=nbytes, transcendentals=exps)


def corner(array):
    shape = (1,) * (array.ndim - 2) + (16, 128)
    return pl.BlockSpec(shape, lambda *at: (0,) * array.ndim)


def call(
    body, place, arrays, in_specs, out_specs, out_shape, grid, estimate, name, scratch=(), after=()
):
    count = len(arrays)

    def kernel(at_ref, *refs):
        body(at_ref, *refs[:count], *refs[count + len(after) :])

    return pl.pallas_call(
        kernel,
        grid_spec=pltpu.PrefetchScalarGridSpec(
            num_scalar_prefetch=1,
            grid=grid,
            in_specs=list(in_specs) + [corner(array) for array in after],
            out_specs=out_specs,
            scratch_shapes=list(scratch),
        ),
        out_shape=out_shape,
        compiler_params=params(),
        cost_estimate=estimate,
        name=name,
    )(place, *arrays, *after)


def pack_columns(place, rows, after=()):
    tokens, width = rows.shape
    part = width // 4

    def body(at_ref, in_ref, out_ref):
        out_ref[0] = in_ref[...]

    return call(
        body,
        place,
        [rows],
        [pl.BlockSpec((tokens, part), lambda i, at: (0, i))],
        pl.BlockSpec((1, tokens, part), lambda i, at: (i, 0, 0)),
        jax.ShapeDtypeStruct((4, tokens, part), rows.dtype),
        (4,),
        cost(0, 4 * tokens * width),
        "pack_columns",
        after=after,
    )


def pack_layers(first, second):
    tokens, layers, width = first.shape
    part = width // 4

    def body(first_ref, second_ref, out_ref):
        out_ref[0, 0] = jnp.swapaxes(first_ref[...], 0, 1)
        out_ref[0, 1] = jnp.swapaxes(second_ref[...], 0, 1)

    piece = pl.BlockSpec((tokens, layers, part), lambda i: (0, 0, i))
    return pl.pallas_call(
        body,
        grid=(4,),
        in_specs=[piece, piece],
        out_specs=pl.BlockSpec((1, 2, layers, tokens, part), lambda i: (i, 0, 0, 0, 0)),
        out_shape=jax.ShapeDtypeStruct((4, 2, layers, tokens, part), first.dtype),
        compiler_params=pltpu.CompilerParams(vmem_limit_bytes=60 * 1024 * 1024),
        cost_estimate=cost(0, 8 * tokens * layers * width),
        name="pack_layers",
    )(first, second)


def own_quarter(place, rows, after=()):
    count, width = rows.shape

    def body(at_ref, in_ref, out_ref):
        out_ref[...] = in_ref[...]

    return call(
        body,
        place,
        [rows],
        [pl.BlockSpec((count // 4, width), lambda i, at: (2 * at[1] + at[3], 0))],
        pl.BlockSpec((count // 4, width), lambda i, at: (0, 0)),
        jax.ShapeDtypeStruct((count // 4, width), rows.dtype),
        (1,),
        cost(0, count * width),
        "own_quarter",
        after=after,
    )


def stack(place, arrays, after=()):
    shape = arrays[0].shape
    zeros = (0,) * len(shape)

    def body(at_ref, *refs):
        *in_refs, out_ref = refs
        for i, ref in enumerate(in_refs):
            out_ref[i] = ref[...]

    return call(
        body,
        place,
        arrays,
        [pl.BlockSpec(shape, lambda i, at: zeros)] * len(arrays),
        pl.BlockSpec((len(arrays),) + shape, lambda i, at: (0,) + zeros),
        jax.ShapeDtypeStruct((len(arrays),) + shape, arrays[0].dtype),
        (1,),
        cost(0, 4 * len(arrays) * arrays[0].size),
        "stack",
        after=after,
    )


def key_places(i, z, shift):
    own = lax.rem(z + 4 - shift, 4)
    places = []
    for back in range(BACK):
        if back == 0:
            at = i
        elif back == 4:
            at = i - 1
        else:
            at = jnp.where(own < back, i - 1, i)
        places.append(((shift + back) % 4, jnp.maximum(at, 0)))
    return own, places


def mask_bias(i, z, start_row):
    block = 4 * i + z
    inside = lax.broadcasted_iota(jnp.int32, (BLOCK, BLOCK), 0)
    query_at = block * BLOCK + lax.broadcasted_iota(jnp.int32, (BLOCK, BLOCK), 1)
    start = jnp.broadcast_to(start_row, (BLOCK, BLOCK))
    pieces = []
    for back in range(BACK):
        key_at = (block - back) * BLOCK + inside
        allowed = key_at >= start
        if back == 0:
            allowed = allowed & (key_at <= query_at)
        pieces.append(jnp.where(allowed, 0.0, MASKED).astype(f32))
    return jnp.concatenate(pieces, axis=0)


def head_rows(ref, kv):
    return jnp.concatenate(
        [
            ref[0, 0, layer, :, pl.ds((4 * kv + head) * HD, HD)]
            for layer in range(2)
            for head in range(4)
        ],
        axis=0,
    )


def exp_scores(keys, queries, bias):
    scores = lax.dot_general(keys, queries, (((1,), (1,)), ((), ())), preferred_element_type=f32)
    copies = queries.shape[0] // BLOCK
    scores = scores * (HD**-0.5 * LOG2E) + jnp.concatenate([bias] * copies, axis=1)
    exps = jnp.exp2(scores - jnp.max(scores, axis=0, keepdims=True))
    return exps, 1.0 / jnp.sum(exps, axis=0, keepdims=True)


def value_grad_kernel(
    at_ref, start_ref, q_ref, g_ref, key_ref, out_ref, head_ref, acc
):
    i = pl.program_id(0)
    z = at_ref[0]

    @pl.when(i == 0)
    def _():
        acc[...] = jnp.zeros_like(acc)

    own, places = key_places(i, z, 0)
    bias = mask_bias(i, own, start_ref[4 * i + own])
    for kv in range(2):
        keys = jnp.concatenate(
            [key_ref[held, at, :, pl.ds(kv * HD, HD)] for held, at in places], axis=0
        )
        exps, inverse = exp_scores(keys, head_rows(q_ref, kv), bias)
        probabilities = (exps * inverse).astype(bf16)
        contrib = jnp.dot(probabilities, head_rows(g_ref, kv), preferred_element_type=f32)
        for back, (held, at) in enumerate(places):
            acc[held, at, :, pl.ds(kv * HD, HD)] += contrib[back * BLOCK : (back + 1) * BLOCK]

    @pl.when(i == 3)
    def _():
        for held in range(4):
            out_ref[lax.rem(z + 4 - held, 4)] = acc[held].astype(bf16)
        head_ref[...] = key_ref[:, :, :, pl.ds(pl.multiple_of((z // 2) * HD, HD), HD)]


def attention_kernel(
    at_ref, start_ref, q0, q1, q2, q3, key_ref, v0, v1, v2, v3, out_ref
):
    i = pl.program_id(0)
    z = at_ref[0]
    for shift, q_ref in enumerate((q0, q1, q2, q3)):
        own, places = key_places(i, z, shift)
        bias = mask_bias(i, own, start_ref[4 * i + own])
        keys = jnp.concatenate([key_ref[held, at] for held, at in places], axis=0)
        values = jnp.concatenate([(v0, v1, v2, v3)[held][at] for held, at in places], axis=0)
        queries = jnp.concatenate(
            [
                (q_ref[0, 0] if shift == 0 else q_ref[0])[layer, :, head * HD : (head + 1) * HD]
                for layer in range(2)
                for head in range(2)
            ],
            axis=0,
        )
        exps, inverse = exp_scores(keys, queries, bias)
        mixed = lax.dot_general(
            values, exps.astype(bf16), (((0,), (0,)), ((), ())), preferred_element_type=f32
        )
        mixed = mixed * inverse
        for layer in range(2):
            for head in range(2):
                at = (2 * layer + head) * BLOCK
                out_ref[layer, 0, own, :, pl.ds(head * HD, HD)] = (
                    mixed[:, at : at + BLOCK].T.astype(bf16)
                )


SCORES = 8 * BACK * BLOCK * 8 * BLOCK
STARTS = pl.BlockSpec((16, 1, BLOCK), lambda i, at: (0, 0, 0))


def value_grad_parts(place, start, heads_and_grads, keys):
    whole = pl.BlockSpec((4, 4, BLOCK, 2 * HD), lambda i, at: (0, 0, 0, 0))
    heads = [
        pl.BlockSpec((1, 1, 2, BLOCK, 8 * HD), lambda i, at, which=which: (i, which, 0, 0, 0))
        for which in range(2)
    ]
    return call(
        value_grad_kernel,
        place,
        [start, heads_and_grads, heads_and_grads, keys],
        [STARTS] + heads + [whole],
        [whole, pl.BlockSpec((4, 4, BLOCK, HD), lambda i, at: (0, 0, 0, 0))],
        [
            jax.ShapeDtypeStruct((4, 4, BLOCK, 2 * HD), bf16),
            jax.ShapeDtypeStruct((4, 4, BLOCK, HD), bf16),
        ],
        (4,),
        cost(4 * HD * SCORES, 6 << 20, SCORES),
        "value_grad_parts",
        scratch=[pltpu.VMEM((4, 4, BLOCK, 2 * HD), f32)],
    )


def split_queries(place, heads_and_grads, hidden, after=()):
    def body(at_ref, in_ref, hidden_ref, *out_refs):
        *head_refs, features_ref = out_refs
        for shift, out in enumerate(head_refs, 1):
            pair = lax.rem(at_ref[0] + shift, 4)
            out[0] = in_ref[0, 0, :, :, pl.ds(pl.multiple_of(pair * 2 * HD, 2 * HD), 2 * HD)]
        features_ref[0] = hidden_ref[...]

    piece = pl.BlockSpec((1, 2, BLOCK, 2 * HD), lambda i, at: (i, 0, 0, 0))
    return call(
        body,
        place,
        [heads_and_grads, hidden],
        [
            pl.BlockSpec((1, 1, 2, BLOCK, 8 * HD), lambda i, at: (i, 0, 0, 0, 0)),
            pl.BlockSpec((BLOCK, FEATS), lambda i, at: (0, i)),
        ],
        [piece] * 3 + [pl.BlockSpec((1, BLOCK, FEATS), lambda i, at: (i, 0, 0))],
        [jax.ShapeDtypeStruct((4, 2, BLOCK, 2 * HD), bf16)] * 3
        + [jax.ShapeDtypeStruct((4, BLOCK, FEATS), bf16)],
        (4,),
        cost(0, 8 << 20),
        "split_queries",
        after=after,
    )


def attend(place, start, queries, keys, values):
    block = pl.BlockSpec((1, 2, BLOCK, 2 * HD), lambda i, at: (i, 0, 0, 0))
    return pl.pallas_call(
        attention_kernel,
        grid_spec=pltpu.PrefetchScalarGridSpec(
            num_scalar_prefetch=1,
            grid=(4,),
            in_specs=[
                STARTS,
                pl.BlockSpec((1, 1, 2, BLOCK, 2 * HD), lambda i, at: (i, 0, 0, 0, at[0])),
            ]
            + [block] * 3
            + [pl.BlockSpec((4, 4, BLOCK, HD), lambda i, at: (0, 0, 0, 0))]
            + [pl.BlockSpec((4, BLOCK, HD), lambda i, at: (0, 0, 0))] * 4,
            out_specs=pl.BlockSpec((2, 1, 4, BLOCK, 2 * HD), lambda i, at: (0, i, 0, 0, 0)),
        ),
        out_shape=jax.ShapeDtypeStruct((2, 4, 4, BLOCK, 2 * HD), bf16),
        compiler_params=params(),
        cost_estimate=cost(4 * HD * SCORES, 6 << 20, SCORES),
        name="attend",
    )(place, start, *queries, keys, *values).reshape(1, 2, 16 * BLOCK, 2 * HD)


def value_parts_kernel(at_ref, h_ref, w_ref, mine_ref, near_ref, far_ref, *refs):
    *out_refs, w_all = refs
    z = at_ref[0]
    core = at_ref[1]
    odd = at_ref[3]
    rows = w_ref.shape[0]
    quarter = rows // 4
    w_all[pl.ds(pl.multiple_of(z * rows, 16), rows), :] = w_ref[...]
    for shift in (1, 2, 3):
        base = lax.rem(z + 4 - shift, 4) * rows
        for piece, whose in (
            (mine_ref[shift - 1], 2 * core + odd),
            (near_ref[shift - 1], 2 * core + 1 - odd),
            (far_ref[0, shift - 1], 2 * (1 - core) + odd),
            (far_ref[1, shift - 1], 2 * (1 - core) + 1 - odd),
        ):
            at = pl.multiple_of(base + whose * quarter, 16)
            w_all[pl.ds(at, quarter), :] = piece
    part = jnp.dot(h_ref[...], w_all[...], preferred_element_type=f32)
    part = (part * D**-0.5).astype(bf16)
    for shift, out in enumerate(out_refs):

        @pl.when(pl.program_id(0) == shift)
        def _():
            out[...] = part


def value_parts(place, features, weight_rows, mine, near, far, after=()):
    tokens = features.shape[0]
    rows, channels = weight_rows.shape
    piece = pl.BlockSpec((3, rows // 4, 256), lambda n, at: (0, 0, lax.rem(at[2] + n, 4)))
    return call(
        value_parts_kernel,
        place,
        [features, weight_rows, mine, near, far],
        [
            pl.BlockSpec((tokens, FEATS), lambda n, at: (0, 0)),
            pl.BlockSpec((rows, 256), lambda n, at: (0, lax.rem(at[2] + n, 4))),
            piece,
            piece,
            pl.BlockSpec((2, 3, rows // 4, 256), lambda n, at: (0, 0, 0, lax.rem(at[2] + n, 4))),
        ],
        [pl.BlockSpec((tokens, 256), lambda n, at: (0, 0))] * 4,
        [jax.ShapeDtypeStruct((tokens, 256), bf16)] * 4,
        (channels // 256,),
        cost(2 * tokens * FEATS * channels, 7 << 20),
        "value_parts",
        scratch=[pltpu.VMEM((FEATS, 256), bf16)],
        after=after,
    )


def sum_values(place, parts):
    tokens = parts[0].shape[0]

    def body(at_ref, p0, p1, p2, p3, *out_refs):
        total = (p0[...].astype(f32) + p1[...].astype(f32)) + (
            p2[...].astype(f32) + p3[...].astype(f32)
        )
        total = total.astype(bf16).reshape(4, BLOCK, 2 * HD)
        for shift, out in enumerate(out_refs):
            low = lax.rem(at_ref[0] + shift, 4) < 2
            out[...] = jnp.where(low, total[:, :, :HD], total[:, :, HD:])

    piece = pl.BlockSpec((4, BLOCK, HD), lambda i, at: (0, 0, 0))
    return pl.pallas_call(
        body,
        grid_spec=pltpu.PrefetchScalarGridSpec(
            num_scalar_prefetch=1,
            grid=(1,),
            in_specs=[pl.BlockSpec((tokens, 2 * HD), lambda i, at: (0, 0))] * 4,
            out_specs=[piece] * 4,
        ),
        out_shape=[jax.ShapeDtypeStruct((4, BLOCK, HD), bf16)] * 4,
        compiler_params=params(),
        cost_estimate=cost(1 << 19, 3 << 19),
        name="sum_values",
    )(place, *parts)


def sum_transposed(place, parts, after=()):
    def body(at_ref, in_ref, out_ref):
        for block in range(4):
            total = (in_ref[0, block].astype(f32) + in_ref[1, block].astype(f32)) + (
                in_ref[2, block].astype(f32) + in_ref[3, block].astype(f32)
            )
            out_ref[:, block * BLOCK : (block + 1) * BLOCK] = total.T.astype(bf16)

    return call(
        body,
        place,
        [parts],
        [pl.BlockSpec((4, 4, BLOCK, 2 * HD), lambda i, at: (0, 0, 0, 0))],
        pl.BlockSpec((2 * HD, 4 * BLOCK), lambda i, at: (0, 0)),
        jax.ShapeDtypeStruct((2 * HD, 4 * BLOCK), bf16),
        (1,),
        cost(1 << 19, 5 << 18),
        "sum_transposed",
        after=after,
    )


def gradient_kernel(at_ref, g0, g1, g2, g3, h_ref, keep_ref, send_ref):
    x = at_ref[2]
    low = at_ref[1] == 0
    features = h_ref[...]
    for shift, piece in enumerate((g0, g1, g2, g3)):
        owner = lax.rem(x + 4 - shift, 4)
        part = jnp.dot(piece[...], features, preferred_element_type=f32) * D**-0.5
        for pair in range(2):
            first = part[pair * 128 : pair * 128 + 64].astype(bf16)
            second = part[pair * 128 + 64 : pair * 128 + 128].astype(bf16)
            y = 2 * lax.rem(owner, 2) + pair
            keep_ref[y, owner // 2] = jnp.where(low, first, second)
            send_ref[y, owner // 2] = jnp.where(low, second, first)


def gradient_parts(place, pieces, features, after=()):
    tokens = features.shape[0]
    out = pl.BlockSpec((4, 2, 64, 256), lambda n, at: (0, 0, 0, n))
    return call(
        gradient_kernel,
        place,
        [*pieces, features],
        [pl.BlockSpec((2 * HD, tokens), lambda n, at: (0, 0))] * 4
        + [pl.BlockSpec((tokens, 256), lambda n, at: (0, n))],
        [out, out],
        [jax.ShapeDtypeStruct((4, 2, 64, FEATS), bf16)] * 2,
        (FEATS // 256,),
        cost(2 * tokens * FEATS * 1024, 7 << 20),
        "gradient_parts",
        after=after,
    )


def add(place, first, second, after=()):
    shape = first.shape
    block = pl.BlockSpec((1,) + shape[1:], lambda i, at: (i,) + (0,) * (len(shape) - 1))

    def body(at_ref, first_ref, second_ref, out_ref):
        total = first_ref[...].astype(f32) + second_ref[...].astype(f32)
        out_ref[...] = total.astype(bf16)

    return call(
        body,
        place,
        [first, second],
        [block, block],
        block,
        jax.ShapeDtypeStruct(shape, bf16),
        (shape[0],),
        cost(first.size, 6 * first.size),
        "add",
        after=after,
    )


def sum_and_split(place, parts, after=()):
    width = FEATS // 4

    def body(at_ref, in_ref, out_ref):
        total = (in_ref[0, 0].astype(f32) + in_ref[1, 0].astype(f32)) + (
            in_ref[2, 0].astype(f32) + in_ref[3, 0].astype(f32)
        )
        for z in range(4):
            out_ref[z] = total[:, z * width : (z + 1) * width].astype(bf16)

    return call(
        body,
        place,
        [parts],
        [pl.BlockSpec((4, 1, 64, FEATS), lambda i, at: (0, i, 0, 0))],
        pl.BlockSpec((4, 64, width), lambda i, at: (i, 0, 0)),
        jax.ShapeDtypeStruct((8, 64, width), bf16),
        (2,),
        cost(1 << 20, 5 << 19),
        "sum_and_split",
        after=after,
    )


def update(place, parts, master, first_moment, second_moment, after=()):
    rows, width = master.shape

    def body(at_ref, parts_ref, master_ref, first_ref, second_ref, m_out, a_out, b_out, w_out):
        gradient = parts_ref[0].astype(f32)
        for i in range(1, 8):
            gradient = gradient + parts_ref[i].astype(f32)
        new_master, new_first, new_second = adam_update(
            gradient, master_ref[...], first_ref[...], second_ref[...]
        )
        m_out[...] = new_master
        a_out[...] = new_first
        b_out[...] = new_second
        for i in range(8):
            w_out[i] = new_master.astype(bf16)

    state = pl.BlockSpec((rows, width), lambda i, at: (0, 0))
    eight = pl.BlockSpec((8, rows, width), lambda i, at: (0, 0, 0))
    return call(
        body,
        place,
        [parts, master, first_moment, second_moment],
        [eight, state, state, state],
        [state, state, state, eight],
        [jax.ShapeDtypeStruct((rows, width), f32)] * 3
        + [jax.ShapeDtypeStruct((8, rows, width), bf16)],
        (1,),
        cost(1 << 20, 2 << 20),
        "update",
        after=after,
    )


def join_cores(place, mine, other):
    count, rows, width = mine.shape

    def body(at_ref, mine_ref, other_ref, out_ref):
        low = at_ref[1] == 0
        for at in range(count):
            a = mine_ref[at].astype(f32)
            b = other_ref[at].astype(f32)
            both = jnp.concatenate([jnp.where(low, a, b), jnp.where(low, b, a)], axis=0)
            out_ref[:, pl.ds(at * 2 * rows, 2 * rows)] = both.T.astype(bf16)

    whole = pl.BlockSpec(mine.shape, lambda at: (0, 0, 0))
    return pl.pallas_call(
        body,
        grid_spec=pltpu.PrefetchScalarGridSpec(
            num_scalar_prefetch=1,
            grid=(),
            in_specs=[whole, whole],
            out_specs=pl.BlockSpec((width, 2 * count * rows), lambda at: (0, 0)),
        ),
        out_shape=jax.ShapeDtypeStruct((width, 2 * count * rows), bf16),
        compiler_params=params(),
        cost_estimate=cost(0, 2 << 20),
        name="join_cores",
    )(place, mine, other)


def exchange(parts, axes):
    return lax.all_to_all(parts, axes, split_axis=0, concat_axis=0, tiled=True)


def from_lower(array, axis, shift):
    return lax.ppermute(array, axis, [(i, (i + shift) % 4) for i in range(4)])


def swap_cores(array):
    return lax.ppermute(array, "core", [(0, 1), (1, 0)])


def per_device(
    hidden, queries, keys, cotangent, segments, weight, master, first_moment, second_moment
):
    x, y, z, core = (lax.axis_index(name) for name in ("x", "y", "z", "core"))
    odd = lax.rem(y, 2)
    place = jnp.stack([z, core, x, odd]).astype(jnp.int32)

    documents = jnp.arange(8, dtype=jnp.int32)
    first_of = jnp.sum((segments[0][None, :] < documents[:, None]).astype(jnp.int32), axis=1)
    start = jnp.sum(
        jnp.where(segments[0][None, :] == documents[:, None], first_of[:, None], 0), axis=0
    ).reshape(16, 1, BLOCK)

    own_keys = exchange(pack_columns(place, keys[0]), "x")
    packed = pack_layers(queries[0], cotangent[0])
    heads_and_grads = exchange(packed, "x")
    all_keys = stack(
        place, [own_keys] + [from_lower(own_keys, "z", shift) for shift in (1, 2, 3)]
    )

    weight_rows = weight.T
    sent_quarter = own_quarter(place, weight_rows, after=[own_keys])
    mine = stack(place, [from_lower(sent_quarter, "z", shift) for shift in (1, 2, 3)])

    *queries_to, features_to = split_queries(
        place, heads_and_grads, hidden[0], after=[mine, all_keys]
    )
    own_features = exchange(features_to, "x").reshape(4 * BLOCK, FEATS)
    queries_from = [heads_and_grads] + [
        from_lower(piece, "z", shift) for shift, piece in enumerate(queries_to, 1)
    ]

    grad_parts, key_heads = value_grad_parts(place, start, heads_and_grads, all_keys)
    grad_moved = exchange(grad_parts, "z")

    near = lax.ppermute(mine, "y", [(0, 1), (1, 0), (2, 3), (3, 2)])
    ready = [grad_parts, queries_from[1], queries_from[3]]
    far = swap_cores(stack(place, [mine, near], after=ready))
    parts_to = value_parts(place, own_features, weight_rows, mine, near, far)
    parts_from = [parts_to[0]] + [from_lower(parts_to[shift], "x", shift) for shift in (1, 2, 3)]
    values = sum_values(place, parts_from)
    values_from = [values[0]] + [from_lower(values[shift], "z", shift) for shift in (1, 2, 3)]

    grad_rows = sum_transposed(place, grad_moved, after=[values[0]])
    pieces = [grad_rows] + [from_lower(grad_rows, "x", shift) for shift in (1, 2, 3)]
    keep, send = gradient_parts(place, pieces, own_features, after=values_from[1:])
    both = add(place, keep, swap_cores(send))
    split = sum_and_split(
        place, exchange(both, "y"), after=[queries_from[2]]
    )
    by_feature = exchange(split, ("zh", "z"))
    attention = attend(place, start, queries_from, key_heads, values_from)
    new_master, new_first, new_second, shard = update(
        place, by_feature, master, first_moment, second_moment, after=[attention]
    )
    shards = exchange(shard, ("zh", "y"))
    fresh = join_cores(place, shards, swap_cores(shards)).T
    return (attention, new_master, new_first, new_second, fresh)


def solution(mesh):
    fine = Mesh(mesh.devices.reshape(2, 4, 2, 4, 4), DP + SEQ)
    in_specs = (
        P(DP, SEQ, None),
        P(DP, SEQ, None, None),
        P(DP, SEQ, None),
        P(DP, SEQ, None, None),
        P(DP, None),
        P(None, SEQ),
        P(DP, SEQ),
        P(DP, SEQ),
        P(DP, SEQ),
    )
    out_specs = (
        P(DP, None, None, SEQ),
        P(DP, SEQ),
        P(DP, SEQ),
        P(DP, SEQ),
        P(None, SEQ),
    )
    return jax.shard_map(
        per_device, mesh=fine, in_specs=in_specs, out_specs=out_specs, check_vma=False
    )
```

time: 361 us -> 256 us (0.71)
  waiting for transfers between devices: 224 us -> 94.9 us
  blocking collectives: 0 us -> 27.2 us
  starting transfers between devices: 75.2 us -> 59.7 us
  Pallas kernels: 47.1 us -> 58.5 us
  local copies, waits for them, and re-layouts: 7.34 us -> 13.4 us
    all_to_all x9 -> x6, waiting for transfers between devices: 120 us -> 0.53 us  [exchange(): return lax.all_to_all(parts, axes, split_axis=0, concat_axis=0, tiled=True)]
    all_to_all x0 -> x1, blocking collectives: none -> 27.2 us  [exchange(): return lax.all_to_all(parts, axes, split_axis=0, concat_axis=0, tiled=True)]
    all_to_all x9 -> x6, starting transfers between devices: 48.5 us -> 31.4 us  [exchange(): return lax.all_to_all(parts, axes, split_axis=0, concat_axis=0, tiled=True)]
    unnamed x28 -> x52, local copies, waits for them, and re-layouts: 2.58 us -> 13.4 us
    pallas_call x9 -> x15, Pallas kernels: 34 us -> 44.4 us  [the longest x13 38.6 us: call(): pl.pallas_call(kernel, grid_spec=pltpu.PrefetchScalarGridSpec(num_scalar_...]
    ppermute x15 -> x18, waiting for transfers between devices: 99.1 us -> 89.4 us  [from_lower(): return lax.ppermute(array, axis, [(i, (i + shift) % 4) for i in range(4)])]
    ppermute x15 -> x18, starting transfers between devices: 17.6 us -> 23.8 us  [from_lower(): return lax.ppermute(array, axis, [(i, (i + shift) % 4) for i in range(4)])]
    ppermute x5 -> x3, starting transfers between devices: 9.15 us -> 3.13 us  [swap_cores(): return lax.ppermute(array, 'core', [(0, 1), (1, 0)])]
  transfers between devices with their start and end apart: 29 -> 28, of which waited for: 20 -> 12; matrix products, arithmetic and copies ran while one was open for 1% -> 0% of each run, Pallas kernels for 10% -> 16%
where the time goes in v2:
time: 256 us; the launch traced here: 255 us
  waiting for transfers between devices  94.9 us (37%)
  starting transfers between devices  59.7 us (23%)
  Pallas kernels  58.5 us (23%)
  blocking collectives  27.2 us (11%)
  local copies, waits for them, and re-layouts  13.4 us (5%)
    ppermute x18, waiting for transfers between devices, from_lower(): return lax.ppermute(array, axis, [(i, (i + shift) % 4) for i in range(4)])  89.4 us
    pallas_call x13, Pallas kernels, call(): pl.pallas_call(kernel, grid_spec=pltpu.PrefetchScalarGridSpec(num_scalar_...  38.6 us
    all_to_all x6, starting transfers between devices, exchange(): return lax.all_to_all(parts, axes, split_axis=0, concat_axis=0, tiled=True)  31.4 us
    all_to_all x1, blocking collectives, exchange(): return lax.all_to_all(parts, axes, split_axis=0, concat_axis=0, tiled=True)  27.2 us
    ppermute x18, starting transfers between devices, from_lower(): return lax.ppermute(array, axis, [(i, (i + shift) % 4) for i in range(4)])  23.8 us
    unnamed x52, local copies, waits for them, and re-layouts  13.4 us
    pallas_call x1, Pallas kernels, attend(): pl.pallas_call(attention_kernel, grid_spec=pltpu.PrefetchScalarGridSpec(n...  12.3 us
  transfers between devices with their start and end apart: 28, of which 12 were waited for; matrix products, arithmetic and copies ran while one was open for 0% of the time, Pallas kernels for 16%

profile of v2, /device:TPU:33, one launch (start us, length us, event | category | flops | bytes accessed | tf_op | source)
XLA Modules:
  0.0 255.0 jit_solution(2398147599683516194)
XLA Ops:
  0.7 0.9 copy-done.12
  1.7 1.9 pack_columns.1
  3.6 4.0 %all-to-all-start.1 = ((bf16[4,128,256]{2,1,0:T(8,128)(2,1)}), bf16[4,128,256]{2,1,0:T(8,128)(2,1)S(1)}, u32[]{:S(2)}, u32[]{:S(2)}) async-start(bf16[4,128,256]{2,1,0:T(8,128)(2,1)} %pack_columns.1), calls=%async_computation.1 | async-start | bytes 524288 | tf_op jit(solution)/shard_map/all_to_all | solution.py:588
  7.6 5.0 %pack_layers.1 = bf16[4,2,2,128,1024]{4,3,2,1,0:T(8,128)(2,1)} custom-call(bf16[128,2,4096]{2,1,0:T(2,128)(2,1)} %bitcast.22, bf16[128,2,4096]{2,1,0:T(2,128)(2,1)} %bitcast.23), custom_call_target="tpu_custom_call" | custom-call | bytes 8388608 | tf_op jit(solution)/shard_map/pack_layers/pallas_call | solution.py:106
  13.1 4.9 %all-to-all-start = ((bf16[4,2,2,128,1024]{4,3,2,1,0:T(8,128)(2,1)}), bf16[4,2,2,128,1024]{4,3,2,1,0:T(8,128)(2,1)}, u32[]{:S(2)}, u32[]{:S(2)}) async-start(bf16[4,2,2,128,1024]{4,3,2,1,0:T(8,128)(2,1)} %pack_layers.1), calls=%async_computation | async-start | bytes 8388608 | tf_op jit(solution)/shard_map/all_to_all | solution.py:588
  18.6 1.7 collective-permute-start
  20.3 1.6 collective-permute-start.3
  22.2 1.0 collective-permute-start.5
  23.2 1.1 collective-permute-start.1
  24.3 2.3 collective-permute-start.2
  26.7 33.7 %collective-permute-done.1.refs_1_ = bf16[112,1024]{1,0:T(8,128)(2,1)S(1)} collective-permute-done((bf16[112,1024]{1,0:T(8,128)(2,1)S(1)}, bf16[112,1024]{1,0:T(8,128)(2,1)S(1)}, u32[]{:S(2)}, u32[]{:S(2)}) %collective-permute-start.1) | collective-permute-done | bytes 229408 | tf_op jit(solution)/shard_map/ppermute | solution.py:592
  60.3 4.8 %collective-permute-done.2.refs_2_ = bf16[112,1024]{1,0:T(8,128)(2,1)S(1)} collective-permute-done((bf16[112,1024]{1,0:T(8,128)(2,1)S(1)}, bf16[112,1024]{1,0:T(8,128)(2,1)S(1)}, u32[]{:S(2)}, u32[]{:S(2)}) %collective-permute-start.2) | collective-permute-done | bytes 229408 | tf_op jit(solution)/shard_map/ppermute | solution.py:592
  65.1 0.6 stack.23.refs_2_.refs_0_
  65.7 0.6 stack.24.refs_3_
  66.4 1.5 copy-done.3
  67.9 3.0 %split_queries.1 = (bf16[4,2,128,256]{3,2,1,0:T(8,128)(2,1)S(1)}, bf16[4,2,128,256]{3,2,1,0:T(8,128)(2,1)S(1)}, bf16[4,2,128,256]{3,2,1,0:T(8,128)(2,1)S(1)}, bf16[4,128,1792]{2,1,0:T(8,128)(2,1)S(1)}) custom-call(s32[4]{0:T(128)S(1)} %pad_add_fusion.at_ref, bf16[4,2,2,128,1024]{4,3,2,1,0:T(8,128)(2,1)} %all-to-all-done.refs_0_.refs_1_.refs_2_.q0, ...), custom_call_target="tpu_custom_call" | custom-call | bytes 8388608 | tf_op jit(solution)/shard_map/split_queries/pallas_call | solution.py:60
  70.9 1.2 copy-done.2
  72.1 0.8 copy-done.16
  72.9 4.5 %all-to-all-start.2 = ((bf16[4,128,1792]{2,1,0:T(8,128)(2,1)}), bf16[4,128,1792]{2,1,0:T(8,128)(2,1)}, u32[]{:S(2)}, u32[]{:S(2)}) async-start(bf16[4,128,1792]{2,1,0:T(8,128)(2,1)} %copy-done.2), calls=%async_computation.2 | async-start | bytes 3670016 | tf_op jit(solution)/shard_map/all_to_all | solution.py:588
  77.5 1.4 collective-permute-start.9
  79.0 1.4 collective-permute-start.8
  80.6 13.5 %value_grad_parts.1 = (bf16[4,4,128,256]{3,2,1,0:T(8,128)(2,1)}, bf16[4,4,128,128]{3,2,1,0:T(8,128)(2,1)S(1)}) custom-call(s32[4]{0:T(128)S(1)} %pad_add_fusion.at_ref, s32[16,1,128]{2,1,0:T(1,128)S(1)} %bitcast.20, bf16[4,2,2,128,1024]{4,3,2,1,0:T(8,128)(2,1)} %all-to-all-done.refs_0_.refs_1_.refs_2_.q0, ...), custom_call_target="tpu_custom_call" | custom-call | flops 2684354560 | bytes 6291456 | tf_op jit(solution)/shard_map/value_grad_parts/pallas_call | solution.py:60
  94.1 9.9 %collective-permute-done.8.refs_4_.q3 = bf16[4,2,128,256]{3,2,1,0:T(8,128)(2,1)S(1)} collective-permute-done((bf16[4,2,128,256]{3,2,1,0:T(8,128)(2,1)S(1)}, bf16[4,2,128,256]{3,2,1,0:T(8,128)(2,1)S(1)}, u32[]{:S(2)}, u32[]{:S(2)}) %collective-permute-start.8) | collective-permute-done | bytes 524320 | tf_op jit(solution)/shard_map/ppermute | solution.py:592
  104.0 1.3 stack.25
  105.9 4.7 %all-to-all-start.3 = ((bf16[4,4,128,256]{3,2,1,0:T(8,128)(2,1)}), bf16[4,4,128,256]{3,2,1,0:T(8,128)(2,1)S(1)}, u32[]{:S(2)}, u32[]{:S(2)}) async-start(bf16[4,4,128,256]{3,2,1,0:T(8,128)(2,1)} %get-tuple-element.30.refs_2_), calls=%async_computation.3 | async-start | bytes 2097152 | tf_op jit(solution)/shard_map/all_to_all | solution.py:588
  110.6 1.2 copy-done.5
  111.7 1.1 copy-done.7
  112.8 5.9 %value_parts.1 = (bf16[512,256]{1,0:T(8,128)(2,1)S(1)}, bf16[512,256]{1,0:T(8,128)(2,1)S(1)}, bf16[512,256]{1,0:T(8,128)(2,1)S(1)}, bf16[512,256]{1,0:T(8,128)(2,1)S(1)}) custom-call(s32[4]{0:T(128)S(1)} %pad_add_fusion.at_ref, bf16[512,1792]{1,0:T(8,128)(2,1)} %bitcast.11.refs_0_.refs_4_, bf16[448,1024]{1,0:T(8,128)(2,1)S(1)} %bitcast.18, ...), custom_call_target="tpu_custom_call" | custom-call | flops 1879048192 | bytes 7340032 | tf_op jit(solution)/shard_map/value_parts/pallas_call | solution.py:60
  118.7 1.6 collective-permute-start.11
  120.3 2.4 collective-permute-start.12
  122.7 1.2 collective-permute-start.13
  123.9 3.7 %collective-permute-done.11.p1 = bf16[512,256]{1,0:T(8,128)(2,1)S(1)} collective-permute-done((bf16[512,256]{1,0:T(8,128)(2,1)S(1)}, bf16[512,256]{1,0:T(8,128)(2,1)S(1)}, u32[]{:S(2)}, u32[]{:S(2)}) %collective-permute-start.11) | collective-permute-done | bytes 262176 | tf_op jit(solution)/shard_map/ppermute | solution.py:592
  127.6 6.6 %collective-permute-done.12.p2 = bf16[512,256]{1,0:T(8,128)(2,1)S(1)} collective-permute-done((bf16[512,256]{1,0:T(8,128)(2,1)S(1)}, bf16[512,256]{1,0:T(8,128)(2,1)S(1)}, u32[]{:S(2)}, u32[]{:S(2)}) %collective-permute-start.12) | collective-permute-done | bytes 262176 | tf_op jit(solution)/shard_map/ppermute | solution.py:592
  134.2 0.7 sum_values.1
  135.0 1.3 collective-permute-start.14
  136.3 0.7 sum_transposed.1.refs_0_
  137.0 1.1 collective-permute-start.17
  138.1 2.9 %collective-permute-start.18 = (bf16[256,512]{1,0:T(8,128)(2,1)S(1)}, bf16[256,512]{1,0:T(8,128)(2,1)S(1)}, u32[]{:S(2)}, u32[]{:S(2)}) collective-permute-start(bf16[256,512]{1,0:T(8,128)(2,1)S(1)} %sum_transposed.1.refs_0_), channel_id=1, source_target_pairs={{0,8},{4,12},{8,0},{12,4},{1,9},{5,13},{9,1},{13,5},{2,10},{6,14},... | collective-permute-start | bytes 786440 | tf_op jit(solution)/shard_map/ppermute | solution.py:592
  141.3 1.3 collective-permute-start.15
  142.6 1.1 collective-permute-start.16
  143.7 6.7 %collective-permute-done.15.v2.refs_6_ = bf16[4,128,128]{2,1,0:T(8,128)(2,1)S(1)} collective-permute-done((bf16[4,128,128]{2,1,0:T(8,128)(2,1)S(1)}, bf16[4,128,128]{2,1,0:T(8,128)(2,1)S(1)}, u32[]{:S(2)}, u32[]{:S(2)}) %collective-permute-start.15) | collective-permute-done | bytes 131104 | tf_op jit(solution)/shard_map/ppermute | solution.py:592
  150.4 1.0 collective-permute-done.16.v3.refs_7_
  151.4 0.8 collective-permute-done.18.refs_2_
  152.2 6.4 %gradient_parts.1 = (bf16[4,2,64,1792]{3,2,1,0:T(8,128)(2,1)S(1)}, bf16[4,2,64,1792]{3,2,1,0:T(8,128)(2,1)S(1)}) custom-call(s32[4]{0:T(128)S(1)} %pad_add_fusion.at_ref, bf16[256,512]{1,0:T(8,128)(2,1)S(1)} %sum_transposed.1.refs_0_, bf16[256,512]{1,0:T(8,128)(2,1)S(1)} %collective-permute-done.17.refs_1_, ...), custom_call_target="tpu_custom_call" | custom-call | flops 1879048192 | bytes 7340032 | tf_op jit(solution)/shard_map/gradient_parts/pallas_call | solution.py:60
  158.6 1.7 collective-permute-start.20
  160.4 3.4 %collective-permute-done.20.refs_1_ = bf16[4,2,64,1792]{3,2,1,0:T(8,128)(2,1)S(1)} collective-permute-done((bf16[4,2,64,1792]{3,2,1,0:T(8,128)(2,1)S(1)}, bf16[4,2,64,1792]{3,2,1,0:T(8,128)(2,1)S(1)}, u32[]{:S(2)}, u32[]{:S(2)}) %collective-permute-start.20) | collective-permute-done | bytes 1835040 | tf_op jit(solution)/shard_map/ppermute | solution.py:596
  163.8 1.0 add.7
  164.9 1.2 copy-done
  166.1 3.9 %all-to-all-start.4 = ((bf16[4,2,64,1792]{3,2,1,0:T(8,128)(2,1)}), bf16[4,2,64,1792]{3,2,1,0:T(8,128)(2,1)S(1)}, u32[]{:S(2)}, u32[]{:S(2)}) async-start(bf16[4,2,64,1792]{3,2,1,0:T(8,128)(2,1)} %copy-done), calls=%async_computation.4 | async-start | bytes 3670016 | tf_op jit(solution)/shard_map/all_to_all | solution.py:588
  170.0 1.1 collective-permute-start.7
  171.1 22.2 %collective-permute-done.7.q2.refs_1_ = bf16[4,2,128,256]{3,2,1,0:T(8,128)(2,1)S(1)} collective-permute-done((bf16[4,2,128,256]{3,2,1,0:T(8,128)(2,1)}, bf16[4,2,128,256]{3,2,1,0:T(8,128)(2,1)S(1)}, u32[]{:S(2)}, u32[]{:S(2)}) %collective-permute-start.7) | collective-permute-done | bytes 524320 | tf_op jit(solution)/shard_map/ppermute | solution.py:592
  193.3 1.8 sum_and_split.1
  195.1 9.4 %all-to-all-start.5 = ((bf16[8,64,448]{2,1,0:T(8,128)(2,1)}), bf16[8,64,448]{2,1,0:T(8,128)(2,1)S(1)}, u32[]{:S(2)}, u32[]{:S(2)}) async-start(bf16[8,64,448]{2,1,0:T(8,128)(2,1)} %sum_and_split.1), calls=%async_computation.5 | async-start | bytes 1048576 | tf_op jit(solution)/shard_map/all_to_all | solution.py:588
  204.5 0.9 copy-done.18
  205.4 0.9 copy-done.20
  206.3 0.9 copy-done.22
  207.2 1.0 copy-done.24
  208.3 12.3 %attend.1 = bf16[2,4,4,128,256]{4,3,2,1,0:T(8,128)(2,1)} custom-call(s32[4]{0:T(128)S(1)} %pad_add_fusion.at_ref, s32[16,1,128]{2,1,0:T(1,128)S(1)} %bitcast.21, bf16[4,2,2,128,1024]{4,3,2,1,0:T(8,128)(2,1)} %all-to-all-done.refs_0_.refs_1_.refs_2_.q0, bf16[4,2,128,256]{3,2,1,0:T(8,128)(2,1)S(1)} %copy-done.9, ...), custom_call_target="tpu_custom_call" | custom-call | flops 2684354560 | bytes 6291456 | tf_op jit(solution)/shard_map/attend/pallas_call | solution.py:325
  220.6 1.6 copy-done.1
  222.2 1.4 update.1
  223.6 27.2 %all_to_all.35.mine_ref = bf16[8,64,448]{2,1,0:T(8,128)(2,1)S(1)} all-to-all(bf16[8,64,448]{2,1,0:T(8,128)(2,1)S(1)} %get-tuple-element.44), channel_id=1, replica_groups=mesh['zh'=2,'y'=4,'core'=2,'x'=4,'z'=4] {'zh','y'}, dimensions={0} | all-to-all | bytes 917504 | tf_op jit(solution)/shard_map/all_to_all | solution.py:588
  250.8 0.8 collective-permute-start.21
  251.6 1.5 collective-permute-done.21.other_ref
  253.1 1.9 join_cores.1
  (65 shorter events, 2.7 us)
Async XLA Ops:
  0.7 1.0 copy-start.12
  3.6 9.6 %all-to-all-start.1 = ((bf16[4,128,256]{2,1,0:T(8,128)(2,1)}), bf16[4,128,256]{2,1,0:T(8,128)(2,1)S(1)}, u32[]{:S(2)}, u32[]{:S(2)}) async-start(bf16[4,128,256]{2,1,0:T(8,128)(2,1)} %pack_columns.1), calls=%async_computation.1 | async-start | bytes 524288 | tf_op jit(solution)/shard_map/all_to_all | solution.py:588
  12.6 5.4 %copy-start.4 = (bf16[1024,448]{0,1:T(8,128)(2,1)S(1)}, bf16[1024,448]{0,1:T(8,128)(2,1)}, u32[]{:S(2)}) copy-start(bf16[1024,448]{0,1:T(8,128)(2,1)} %param.14) | copy-start | bytes 2752516
  13.1 53.2 %all-to-all-start = ((bf16[4,2,2,128,1024]{4,3,2,1,0:T(8,128)(2,1)}), bf16[4,2,2,128,1024]{4,3,2,1,0:T(8,128)(2,1)}, u32[]{:S(2)}, u32[]{:S(2)}) async-start(bf16[4,2,2,128,1024]{4,3,2,1,0:T(8,128)(2,1)} %pack_layers.1), calls=%async_computation | async-start | bytes 8388608 | tf_op jit(solution)/shard_map/all_to_all | solution.py:588
  18.6 5.7 %collective-permute-start = (bf16[112,1024]{1,0:T(8,128)(2,1)S(1)}, bf16[112,1024]{1,0:T(8,128)(2,1)S(1)}, u32[]{:S(2)}, u32[]{:S(2)}) collective-permute-start(bf16[112,1024]{1,0:T(8,128)(2,1)S(1)} %own_quarter.1), channel_id=1, source_target_pairs={{0,1},{1,2},{2,3},{3,0},{4,5},{5,6},{6,7},{7,4},{8,9},{9,10},{10,1... | collective-permute-start | bytes 688136 | tf_op jit(solution)/shard_map/ppermute | solution.py:592
  20.3 45.4 %collective-permute-start.3 = (bf16[4,128,256]{2,1,0:T(8,128)(2,1)S(1)}, bf16[4,128,256]{2,1,0:T(8,128)(2,1)S(1)}, u32[]{:S(2)}, u32[]{:S(2)}) collective-permute-start(bf16[4,128,256]{2,1,0:T(8,128)(2,1)S(1)} %all-to-all-done.1.refs_1_.refs_0_), channel_id=1, source_target_pairs={{0,1},{1,2},{2,3},{3,0},{4,5},{5,6},{6,7},{7,4},{8,9},{9,10},{10,1... | collective-permute-start | bytes 786440 | tf_op jit(solution)/shard_map/ppermute | solution.py:592
  21.9 43.8 %collective-permute-start.4 = (bf16[4,128,256]{2,1,0:T(8,128)(2,1)S(1)}, bf16[4,128,256]{2,1,0:T(8,128)(2,1)S(1)}, u32[]{:S(2)}, u32[]{:S(2)}) collective-permute-start(bf16[4,128,256]{2,1,0:T(8,128)(2,1)S(1)} %all-to-all-done.1.refs_1_.refs_0_), channel_id=1, source_target_pairs={{0,2},{1,3},{2,0},{3,1},{4,6},{5,7},{6,4},{7,5},{8,10},{9,11},{10,... | collective-permute-start | bytes 786440 | tf_op jit(solution)/shard_map/ppermute | solution.py:592
  22.2 43.5 %collective-permute-start.5 = (bf16[4,128,256]{2,1,0:T(8,128)(2,1)S(1)}, bf16[4,128,256]{2,1,0:T(8,128)(2,1)S(1)}, u32[]{:S(2)}, u32[]{:S(2)}) collective-permute-start(bf16[4,128,256]{2,1,0:T(8,128)(2,1)S(1)} %all-to-all-done.1.refs_1_.refs_0_), channel_id=1, source_target_pairs={{0,3},{1,0},{2,1},{3,2},{4,7},{5,4},{6,5},{7,6},{8,11},{9,8},{10,9... | collective-permute-start | bytes 786440 | tf_op jit(solution)/shard_map/ppermute | solution.py:592
  23.2 37.1 %collective-permute-start.1 = (bf16[112,1024]{1,0:T(8,128)(2,1)S(1)}, bf16[112,1024]{1,0:T(8,128)(2,1)S(1)}, u32[]{:S(2)}, u32[]{:S(2)}) collective-permute-start(bf16[112,1024]{1,0:T(8,128)(2,1)S(1)} %own_quarter.1), channel_id=1, source_target_pairs={{0,2},{1,3},{2,0},{3,1},{4,6},{5,7},{6,4},{7,5},{8,10},{9,11},{10,... | collective-permute-start | bytes 688136 | tf_op jit(solution)/shard_map/ppermute | solution.py:592
  24.3 40.8 %collective-permute-start.2 = (bf16[112,1024]{1,0:T(8,128)(2,1)S(1)}, bf16[112,1024]{1,0:T(8,128)(2,1)S(1)}, u32[]{:S(2)}, u32[]{:S(2)}) collective-permute-start(bf16[112,1024]{1,0:T(8,128)(2,1)S(1)} %own_quarter.1), channel_id=1, source_target_pairs={{0,3},{1,0},{2,1},{3,2},{4,7},{5,4},{6,5},{7,6},{8,11},{9,8},{10,9... | collective-permute-start | bytes 688136 | tf_op jit(solution)/shard_map/ppermute | solution.py:592
  66.4 1.5 copy-start.3
  70.9 1.2 copy-start.2
  72.1 0.8 copy-start.16
  72.9 7.4 %copy-start.25 = (s32[1,2048]{1,0:T(1,128)S(1)}, s32[1,2048]{1,0:T(1,128)}, u32[]{:S(2)}) copy-start(s32[1,2048]{1,0:T(1,128)} %param.13) | copy-start | bytes 24580
  72.9 33.0 %all-to-all-start.2 = ((bf16[4,128,1792]{2,1,0:T(8,128)(2,1)}), bf16[4,128,1792]{2,1,0:T(8,128)(2,1)}, u32[]{:S(2)}, u32[]{:S(2)}) async-start(bf16[4,128,1792]{2,1,0:T(8,128)(2,1)} %copy-done.2), calls=%async_computation.2 | async-start | bytes 3670016 | tf_op jit(solution)/shard_map/all_to_all | solution.py:588
  77.5 16.6 %collective-permute-start.9 = (bf16[3,112,1024]{2,1,0:T(8,128)(2,1)S(1)}, bf16[3,112,1024]{2,1,0:T(8,128)(2,1)S(1)}, u32[]{:S(2)}, u32[]{:S(2)}) collective-permute-start(bf16[3,112,1024]{2,1,0:T(8,128)(2,1)S(1)} %stack.23.refs_2_.refs_0_), channel_id=1, source_target_pairs={{0,32},{32,0},{64,96},{96,64},{1,33},{33,1},{65,97},{97,65},{2,34}... | collective-permute-start | bytes 2064392 | tf_op jit(solution)/shard_map/ppermute | solution.py:634
  78.9 15.2 %collective-permute-start.6 = (bf16[4,2,128,256]{3,2,1,0:T(8,128)(2,1)S(1)}, bf16[4,2,128,256]{3,2,1,0:T(8,128)(2,1)S(1)}, u32[]{:S(2)}, u32[]{:S(2)}) collective-permute-start(bf16[4,2,128,256]{3,2,1,0:T(8,128)(2,1)S(1)} %get-tuple-element.25), channel_id=1, source_target_pairs={{0,1},{1,2},{2,3},{3,0},{4,5},{5,6},{6,7},{7,4},{8,9},{9,10},{10,1... | collective-permute-start | bytes 1572872 | tf_op jit(solution)/shard_map/ppermute | solution.py:592
  79.0 25.0 %collective-permute-start.8 = (bf16[4,2,128,256]{3,2,1,0:T(8,128)(2,1)S(1)}, bf16[4,2,128,256]{3,2,1,0:T(8,128)(2,1)S(1)}, u32[]{:S(2)}, u32[]{:S(2)}) collective-permute-start(bf16[4,2,128,256]{3,2,1,0:T(8,128)(2,1)S(1)} %get-tuple-element.27), channel_id=1, source_target_pairs={{0,3},{1,0},{2,1},{3,2},{4,7},{5,4},{6,5},{7,6},{8,11},{9,8},{10,9... | collective-permute-start | bytes 1572872 | tf_op jit(solution)/shard_map/ppermute | solution.py:592
  94.0 11.2 %copy-start.23 = (bf16[4,4,128,128]{3,2,1,0:T(8,128)(2,1)}, bf16[4,4,128,128]{3,2,1,0:T(8,128)(2,1)S(1)}, u32[]{:S(2)}) copy-start(bf16[4,4,128,128]{3,2,1,0:T(8,128)(2,1)S(1)} %get-tuple-element.28.key_ref) | copy-start | bytes 1572868
  94.0 11.2 %copy-start.6 = (bf16[3,112,1024]{2,1,0:T(8,128)(2,1)}, bf16[3,112,1024]{2,1,0:T(8,128)(2,1)S(1)}, u32[]{:S(2)}) copy-start(bf16[3,112,1024]{2,1,0:T(8,128)(2,1)S(1)} %collective-permute-done.9.refs_1_.refs_3_) | copy-start | bytes 2064388
  94.1 11.2 %copy-start.8 = (bf16[4,2,128,256]{3,2,1,0:T(8,128)(2,1)}, bf16[4,2,128,256]{3,2,1,0:T(8,128)(2,1)S(1)}, u32[]{:S(2)}) copy-start(bf16[4,2,128,256]{3,2,1,0:T(8,128)(2,1)S(1)} %collective-permute-done.6.refs_3_.q1) | copy-start | bytes 1572868
  104.0 1.4 copy-start.10
  105.3 5.3 %collective-permute-start.10 = (bf16[2,3,112,1024]{3,2,1,0:T(8,128)(2,1)S(1)}, bf16[2,3,112,1024]{3,2,1,0:T(8,128)(2,1)}, u32[]{:S(2)}, u32[]{:S(2)}) collective-permute-start(bf16[2,3,112,1024]{3,2,1,0:T(8,128)(2,1)S(1)} %stack.25), channel_id=1, source_target_pairs={{0,16},{16,0},{1,17},{17,1},{2,18},{18,2},{3,19},{19,3},{4,20},{20... | collective-permute-start | bytes 4128776 | tf_op jit(solution)/shard_map/ppermute | solution.py:596
  105.9 30.4 %all-to-all-start.3 = ((bf16[4,4,128,256]{3,2,1,0:T(8,128)(2,1)}), bf16[4,4,128,256]{3,2,1,0:T(8,128)(2,1)S(1)}, u32[]{:S(2)}, u32[]{:S(2)}) async-start(bf16[4,4,128,256]{3,2,1,0:T(8,128)(2,1)} %get-tuple-element.30.refs_2_), calls=%async_computation.3 | async-start | bytes 2097152 | tf_op jit(solution)/shard_map/all_to_all | solution.py:588
  110.6 1.2 copy-start.5
  111.7 1.1 copy-start.7
  118.7 8.9 %collective-permute-start.11 = (bf16[512,256]{1,0:T(8,128)(2,1)S(1)}, bf16[512,256]{1,0:T(8,128)(2,1)S(1)}, u32[]{:S(2)}, u32[]{:S(2)}) collective-permute-start(bf16[512,256]{1,0:T(8,128)(2,1)S(1)} %get-tuple-element.32), channel_id=1, source_target_pairs={{0,4},{4,8},{8,12},{12,0},{1,5},{5,9},{9,13},{13,1},{2,6},{6,10},{... | collective-permute-start | bytes 786440 | tf_op jit(solution)/shard_map/ppermute | solution.py:592
  120.3 13.9 %collective-permute-start.12 = (bf16[512,256]{1,0:T(8,128)(2,1)S(1)}, bf16[512,256]{1,0:T(8,128)(2,1)S(1)}, u32[]{:S(2)}, u32[]{:S(2)}) collective-permute-start(bf16[512,256]{1,0:T(8,128)(2,1)S(1)} %get-tuple-element.33), channel_id=1, source_target_pairs={{0,8},{4,12},{8,0},{12,4},{1,9},{5,13},{9,1},{13,5},{2,10},{6,14},... | collective-permute-start | bytes 786440 | tf_op jit(solution)/shard_map/ppermute | solution.py:592
  122.7 11.5 %collective-permute-start.13 = (bf16[512,256]{1,0:T(8,128)(2,1)S(1)}, bf16[512,256]{1,0:T(8,128)(2,1)S(1)}, u32[]{:S(2)}, u32[]{:S(2)}) collective-permute-start(bf16[512,256]{1,0:T(8,128)(2,1)S(1)} %get-tuple-element.34), channel_id=1, source_target_pairs={{0,12},{4,0},{8,4},{12,8},{1,13},{5,1},{9,5},{13,9},{2,14},{6,2},{... | collective-permute-start | bytes 786440 | tf_op jit(solution)/shard_map/ppermute | solution.py:592
  135.0 7.6 %collective-permute-start.14 = (bf16[4,128,128]{2,1,0:T(8,128)(2,1)S(1)}, bf16[4,128,128]{2,1,0:T(8,128)(2,1)S(1)}, u32[]{:S(2)}, u32[]{:S(2)}) collective-permute-start(bf16[4,128,128]{2,1,0:T(8,128)(2,1)S(1)} %get-tuple-element.36), channel_id=1, source_target_pairs={{0,1},{1,2},{2,3},{3,0},{4,5},{5,6},{6,7},{7,4},{8,9},{9,10},{10,1... | collective-permute-start | bytes 393224 | tf_op jit(solution)/shard_map/ppermute | solution.py:592
  137.0 14.4 %collective-permute-start.17 = (bf16[256,512]{1,0:T(8,128)(2,1)S(1)}, bf16[256,512]{1,0:T(8,128)(2,1)S(1)}, u32[]{:S(2)}, u32[]{:S(2)}) collective-permute-start(bf16[256,512]{1,0:T(8,128)(2,1)S(1)} %sum_transposed.1.refs_0_), channel_id=1, source_target_pairs={{0,4},{4,8},{8,12},{12,0},{1,5},{5,9},{9,13},{13,1},{2,6},{6,10},{... | collective-permute-start | bytes 786440 | tf_op jit(solution)/shard_map/ppermute | solution.py:592
  138.1 14.2 %collective-permute-start.18 = (bf16[256,512]{1,0:T(8,128)(2,1)S(1)}, bf16[256,512]{1,0:T(8,128)(2,1)S(1)}, u32[]{:S(2)}, u32[]{:S(2)}) collective-permute-start(bf16[256,512]{1,0:T(8,128)(2,1)S(1)} %sum_transposed.1.refs_0_), channel_id=1, source_target_pairs={{0,8},{4,12},{8,0},{12,4},{1,9},{5,13},{9,1},{13,5},{2,10},{6,14},... | collective-permute-start | bytes 786440 | tf_op jit(solution)/shard_map/ppermute | solution.py:592
  141.0 11.2 %collective-permute-start.19 = (bf16[256,512]{1,0:T(8,128)(2,1)S(1)}, bf16[256,512]{1,0:T(8,128)(2,1)S(1)}, u32[]{:S(2)}, u32[]{:S(2)}) collective-permute-start(bf16[256,512]{1,0:T(8,128)(2,1)S(1)} %sum_transposed.1.refs_0_), channel_id=1, source_target_pairs={{0,12},{4,0},{8,4},{12,8},{1,13},{5,1},{9,5},{13,9},{2,14},{6,2},{... | collective-permute-start | bytes 786440 | tf_op jit(solution)/shard_map/ppermute | solution.py:592
  141.3 9.1 %collective-permute-start.15 = (bf16[4,128,128]{2,1,0:T(8,128)(2,1)S(1)}, bf16[4,128,128]{2,1,0:T(8,128)(2,1)S(1)}, u32[]{:S(2)}, u32[]{:S(2)}) collective-permute-start(bf16[4,128,128]{2,1,0:T(8,128)(2,1)S(1)} %get-tuple-element.37), channel_id=1, source_target_pairs={{0,2},{1,3},{2,0},{3,1},{4,6},{5,7},{6,4},{7,5},{8,10},{9,11},{10,... | collective-permute-start | bytes 393224 | tf_op jit(solution)/shard_map/ppermute | solution.py:592
  142.6 16.0 %copy-start.17 = (bf16[4,128,128]{2,1,0:T(8,128)(2,1)}, bf16[4,128,128]{2,1,0:T(8,128)(2,1)S(1)}, u32[]{:S(2)}) copy-start(bf16[4,128,128]{2,1,0:T(8,128)(2,1)S(1)} %collective-permute-done.14.v1.refs_5_) | copy-start | bytes 393220
  142.6 8.8 %collective-permute-start.16 = (bf16[4,128,128]{2,1,0:T(8,128)(2,1)S(1)}, bf16[4,128,128]{2,1,0:T(8,128)(2,1)S(1)}, u32[]{:S(2)}, u32[]{:S(2)}) collective-permute-start(bf16[4,128,128]{2,1,0:T(8,128)(2,1)S(1)} %get-tuple-element.38), channel_id=1, source_target_pairs={{0,3},{1,0},{2,1},{3,2},{4,7},{5,4},{6,5},{7,6},{8,11},{9,8},{10,9... | collective-permute-start | bytes 393224 | tf_op jit(solution)/shard_map/ppermute | solution.py:592
  150.4 8.3 %copy-start.19 = (bf16[4,128,128]{2,1,0:T(8,128)(2,1)}, bf16[4,128,128]{2,1,0:T(8,128)(2,1)S(1)}, u32[]{:S(2)}) copy-start(bf16[4,128,128]{2,1,0:T(8,128)(2,1)S(1)} %collective-permute-done.15.v2.refs_6_) | copy-start | bytes 393220
  151.4 7.2 %copy-start.21 = (bf16[4,128,128]{2,1,0:T(8,128)(2,1)}, bf16[4,128,128]{2,1,0:T(8,128)(2,1)S(1)}, u32[]{:S(2)}) copy-start(bf16[4,128,128]{2,1,0:T(8,128)(2,1)S(1)} %collective-permute-done.16.v3.refs_7_) | copy-start | bytes 393220
  158.6 5.2 %collective-permute-start.20 = (bf16[4,2,64,1792]{3,2,1,0:T(8,128)(2,1)S(1)}, bf16[4,2,64,1792]{3,2,1,0:T(8,128)(2,1)S(1)}, u32[]{:S(2)}, u32[]{:S(2)}) collective-permute-start(bf16[4,2,64,1792]{3,2,1,0:T(8,128)(2,1)S(1)} %get-tuple-element.40), channel_id=1, source_target_pairs={{0,16},{16,0},{1,17},{17,1},{2,18},{18,2},{3,19},{19,3},{4,20},{20... | collective-permute-start | bytes 5505032 | tf_op jit(solution)/shard_map/ppermute | solution.py:596
  164.8 1.2 copy-start
  166.1 27.3 %all-to-all-start.4 = ((bf16[4,2,64,1792]{3,2,1,0:T(8,128)(2,1)}), bf16[4,2,64,1792]{3,2,1,0:T(8,128)(2,1)S(1)}, u32[]{:S(2)}, u32[]{:S(2)}) async-start(bf16[4,2,64,1792]{3,2,1,0:T(8,128)(2,1)} %copy-done), calls=%async_computation.4 | async-start | bytes 3670016 | tf_op jit(solution)/shard_map/all_to_all | solution.py:588
  170.0 34.5 %copy-start.9 = (bf16[4,2,128,256]{3,2,1,0:T(8,128)(2,1)S(1)}, bf16[4,2,128,256]{3,2,1,0:T(8,128)(2,1)}, u32[]{:S(2)}) copy-start(bf16[4,2,128,256]{3,2,1,0:T(8,128)(2,1)} %copy-done.8) | copy-start | bytes 1572868
  170.0 34.5 %copy-start.11 = (bf16[4,2,128,256]{3,2,1,0:T(8,128)(2,1)S(1)}, bf16[4,2,128,256]{3,2,1,0:T(8,128)(2,1)}, u32[]{:S(2)}) copy-start(bf16[4,2,128,256]{3,2,1,0:T(8,128)(2,1)} %copy-done.10) | copy-start | bytes 1572868
  170.0 23.4 %collective-permute-start.7 = (bf16[4,2,128,256]{3,2,1,0:T(8,128)(2,1)}, bf16[4,2,128,256]{3,2,1,0:T(8,128)(2,1)S(1)}, u32[]{:S(2)}, u32[]{:S(2)}) collective-permute-start(bf16[4,2,128,256]{3,2,1,0:T(8,128)(2,1)} %copy-done.16), channel_id=1, source_target_pairs={{0,2},{1,3},{2,0},{3,1},{4,6},{5,7},{6,4},{7,5},{8,10},{9,11},{10,... | collective-permute-start | bytes 1572872 | tf_op jit(solution)/shard_map/ppermute | solution.py:592
  195.1 25.5 %all-to-all-start.5 = ((bf16[8,64,448]{2,1,0:T(8,128)(2,1)}), bf16[8,64,448]{2,1,0:T(8,128)(2,1)S(1)}, u32[]{:S(2)}, u32[]{:S(2)}) async-start(bf16[8,64,448]{2,1,0:T(8,128)(2,1)} %sum_and_split.1), calls=%async_computation.5 | async-start | bytes 1048576 | tf_op jit(solution)/shard_map/all_to_all | solution.py:588
  204.5 0.9 copy-start.18
  205.4 0.9 copy-start.20
  206.3 0.9 copy-start.22
  207.2 1.0 copy-start.24
  208.2 12.3 %copy-start.13 = (f32[64,448]{1,0:T(8,128)S(1)}, f32[64,448]{1,0:T(8,128)}, u32[]{:S(2)}) copy-start(f32[64,448]{1,0:T(8,128)} %refs_1_.1) | copy-start | bytes 344068
  208.2 12.3 %copy-start.14 = (f32[64,448]{1,0:T(8,128)S(1)}, f32[64,448]{1,0:T(8,128)}, u32[]{:S(2)}) copy-start(f32[64,448]{1,0:T(8,128)} %refs_2_.1) | copy-start | bytes 344068
  208.3 12.3 %copy-start.15 = (f32[64,448]{1,0:T(8,128)S(1)}, f32[64,448]{1,0:T(8,128)}, u32[]{:S(2)}) copy-start(f32[64,448]{1,0:T(8,128)} %refs_3_.1) | copy-start | bytes 344068
  220.6 1.6 copy-start.1
  250.8 2.3 collective-permute-start.21

commit v3 on v2

--- a/solution.py
+++ b/solution.py
@@ -73,24 +73,24 @@
     )(place, *arrays, *after)
 
 
-def pack_columns(place, rows, after=()):
+def pack_columns(place, rows):
     tokens, width = rows.shape
     part = width // 4
 
     def body(at_ref, in_ref, out_ref):
-        out_ref[0] = in_ref[...]
+        for i in range(4):
+            out_ref[i] = in_ref[:, i * part : (i + 1) * part]
 
     return call(
         body,
         place,
         [rows],
-        [pl.BlockSpec((tokens, part), lambda i, at: (0, i))],
-        pl.BlockSpec((1, tokens, part), lambda i, at: (i, 0, 0)),
+        [pl.BlockSpec((tokens, width), lambda i, at: (0, 0))],
+        pl.BlockSpec((4, tokens, part), lambda i, at: (0, 0, 0)),
         jax.ShapeDtypeStruct((4, tokens, part), rows.dtype),
-        (4,),
+        (1,),
         cost(0, 4 * tokens * width),
         "pack_columns",
-        after=after,
     )
 
 
@@ -270,7 +270,7 @@
 STARTS = pl.BlockSpec((16, 1, BLOCK), lambda i, at: (0, 0, 0))
 
 
-def value_grad_parts(place, start, heads_and_grads, keys):
+def value_grad_parts(place, start, heads_and_grads, keys, after=()):
     whole = pl.BlockSpec((4, 4, BLOCK, 2 * HD), lambda i, at: (0, 0, 0, 0))
     heads = [
         pl.BlockSpec((1, 1, 2, BLOCK, 8 * HD), lambda i, at, which=which: (i, which, 0, 0, 0))
@@ -289,35 +289,61 @@
         (4,),
         cost(4 * HD * SCORES, 6 << 20, SCORES),
         "value_grad_parts",
+        after=after,
         scratch=[pltpu.VMEM((4, 4, BLOCK, 2 * HD), f32)],
     )
 
 
-def split_queries(place, heads_and_grads, hidden, after=()):
-    def body(at_ref, in_ref, hidden_ref, *out_refs):
-        *head_refs, features_ref = out_refs
-        for shift, out in enumerate(head_refs, 1):
+def split_queries(place, heads_and_grads, after=()):
+    def body(at_ref, in_ref, *out_refs):
+        for shift, out in enumerate(out_refs, 1):
             pair = lax.rem(at_ref[0] + shift, 4)
             out[0] = in_ref[0, 0, :, :, pl.ds(pl.multiple_of(pair * 2 * HD, 2 * HD), 2 * HD)]
-        features_ref[0] = hidden_ref[...]
 
     piece = pl.BlockSpec((1, 2, BLOCK, 2 * HD), lambda i, at: (i, 0, 0, 0))
     return call(
         body,
         place,
-        [heads_and_grads, hidden],
+        [heads_and_grads],
+        [pl.BlockSpec((1, 1, 2, BLOCK, 8 * HD), lambda i, at: (i, 0, 0, 0, 0))],
+        [piece] * 3,
+        [jax.ShapeDtypeStruct((4, 2, BLOCK, 2 * HD), bf16)] * 3,
+        (4,),
+        cost(0, 4 << 20),
+        "split_queries",
+        after=after,
+    )
+
+
+def split_columns(place, rows, after=()):
+    tokens, width = rows.shape
+    part = width // 4
+
+    def body(at_ref, *refs):
+        for in_ref, out_ref in zip(refs[:4], refs[4:]):
+            out_ref[...] = in_ref[...]
+
+    return call(
+        body,
+        place,
+        [rows] * 4,
         [
-            pl.BlockSpec((1, 1, 2, BLOCK, 8 * HD), lambda i, at: (i, 0, 0, 0, 0)),
-            pl.BlockSpec((BLOCK, FEATS), lambda i, at: (0, i)),
+            pl.BlockSpec((tokens, part), lambda i, at, shift=shift: (0, lax.rem(at[2] + shift, 4)))
+            for shift in range(4)
         ],
-        [piece] * 3 + [pl.BlockSpec((1, BLOCK, FEATS), lambda i, at: (i, 0, 0))],
-        [jax.ShapeDtypeStruct((4, 2, BLOCK, 2 * HD), bf16)] * 3
-        + [jax.ShapeDtypeStruct((4, BLOCK, FEATS), bf16)],
-        (4,),
-        cost(0, 8 << 20),
-        "split_queries",
-        after=after,
-    )
+        [pl.BlockSpec((tokens, part), lambda i, at: (0, 0))] * 4,
+        [jax.ShapeDtypeStruct((tokens, part), rows.dtype)] * 4,
+        (1,),
+        cost(0, 4 * tokens * width),
+        "split_columns",
+        after=after,
+    )
+
+
+def place_tokens(x, pieces, out_ref):
+    for shift, piece in enumerate(pieces):
+        at = pl.multiple_of(lax.rem(x + 4 - shift, 4) * BLOCK, BLOCK)
+        out_ref[pl.ds(at, BLOCK), :] = piece[...]
 
 
 def attend(place, start, queries, keys, values):
@@ -340,11 +366,16 @@
         compiler_params=params(),
         cost_estimate=cost(4 * HD * SCORES, 6 << 20, SCORES),
         name="attend",
-    )(place, start, *queries, keys, *values).reshape(1, 2, 16 * BLOCK, 2 * HD)
-
-
-def value_parts_kernel(at_ref, h_ref, w_ref, mine_ref, near_ref, far_ref, *refs):
-    *out_refs, w_all = refs
+    )(place, start, *queries, keys, *values)
+
+
+def value_parts_kernel(at_ref, h0, h1, h2, h3, w_ref, mine_ref, near_ref, far_ref, *refs):
+    *out_refs, h_all, w_all = refs
+
+    @pl.when(pl.program_id(0) == 0)
+    def _():
+        place_tokens(at_ref[2], (h0, h1, h2, h3), h_all)
+
     z = at_ref[0]
     core = at_ref[1]
     odd = at_ref[3]
@@ -361,7 +392,7 @@
         ):
             at = pl.multiple_of(base + whose * quarter, 16)
             w_all[pl.ds(at, quarter), :] = piece
-    part = jnp.dot(h_ref[...], w_all[...], preferred_element_type=f32)
+    part = jnp.dot(h_all[...], w_all[...], preferred_element_type=f32)
     part = (part * D**-0.5).astype(bf16)
     for shift, out in enumerate(out_refs):
 
@@ -371,22 +402,24 @@
 
 
 def value_parts(place, features, weight_rows, mine, near, far, after=()):
-    tokens = features.shape[0]
+    tokens = 4 * BLOCK
     rows, channels = weight_rows.shape
     piece = pl.BlockSpec((3, rows // 4, 256), lambda n, at: (0, 0, lax.rem(at[2] + n, 4)))
     return call(
         value_parts_kernel,
         place,
-        [features, weight_rows, mine, near, far],
-        [
-            pl.BlockSpec((tokens, FEATS), lambda n, at: (0, 0)),
+        [*features, weight_rows, mine, near, far],
+        [pl.BlockSpec((BLOCK, FEATS), lambda n, at: (0, 0))] * 4
+        + [
             pl.BlockSpec((rows, 256), lambda n, at: (0, lax.rem(at[2] + n, 4))),
             piece,
             piece,
             pl.BlockSpec((2, 3, rows // 4, 256), lambda n, at: (0, 0, 0, lax.rem(at[2] + n, 4))),
         ],
-        [pl.BlockSpec((tokens, 256), lambda n, at: (0, 0))] * 4,
-        [jax.ShapeDtypeStruct((tokens, 256), bf16)] * 4,
+        [pl.BlockSpec((tokens, 256), lambda n, at: (0, 0))] * 4
+        + [pl.BlockSpec((tokens, FEATS), lambda n, at: (0, 0))],
+        [jax.ShapeDtypeStruct((tokens, 256), bf16)] * 4
+        + [jax.ShapeDtypeStruct((tokens, FEATS), bf16)],
         (channels // 256,),
         cost(2 * tokens * FEATS * channels, 7 << 20),
         "value_parts",
@@ -461,7 +494,7 @@
 
 
 def gradient_parts(place, pieces, features, after=()):
-    tokens = features.shape[0]
+    tokens = 4 * BLOCK
     out = pl.BlockSpec((4, 2, 64, 256), lambda n, at: (0, 0, 0, n))
     return call(
         gradient_kernel,
@@ -557,7 +590,7 @@
     )
 
 
-def join_cores(place, mine, other):
+def join_cores(place, mine, other, after=()):
     count, rows, width = mine.shape
 
     def body(at_ref, mine_ref, other_ref, out_ref):
@@ -568,20 +601,18 @@
             both = jnp.concatenate([jnp.where(low, a, b), jnp.where(low, b, a)], axis=0)
             out_ref[:, pl.ds(at * 2 * rows, 2 * rows)] = both.T.astype(bf16)
 
-    whole = pl.BlockSpec(mine.shape, lambda at: (0, 0, 0))
-    return pl.pallas_call(
-        body,
-        grid_spec=pltpu.PrefetchScalarGridSpec(
-            num_scalar_prefetch=1,
-            grid=(),
-            in_specs=[whole, whole],
-            out_specs=pl.BlockSpec((width, 2 * count * rows), lambda at: (0, 0)),
-        ),
-        out_shape=jax.ShapeDtypeStruct((width, 2 * count * rows), bf16),
-        compiler_params=params(),
-        cost_estimate=cost(0, 2 << 20),
-        name="join_cores",
-    )(place, mine, other)
+    return call(
+        body,
+        place,
+        [mine, other],
+        [pl.BlockSpec(mine.shape, lambda i, at: (0, 0, 0))] * 2,
+        pl.BlockSpec((width, 2 * count * rows), lambda i, at: (0, 0)),
+        jax.ShapeDtypeStruct((width, 2 * count * rows), bf16),
+        (1,),
+        cost(0, 2 << 20),
+        "join_cores",
+        after=after,
+    )
 
 
 def exchange(parts, axes):
@@ -620,31 +651,36 @@
     sent_quarter = own_quarter(place, weight_rows, after=[own_keys])
     mine = stack(place, [from_lower(sent_quarter, "z", shift) for shift in (1, 2, 3)])
 
-    *queries_to, features_to = split_queries(
-        place, heads_and_grads, hidden[0], after=[mine, all_keys]
-    )
-    own_features = exchange(features_to, "x").reshape(4 * BLOCK, FEATS)
+    grad_parts, key_heads = value_grad_parts(
+        place, start, heads_and_grads, all_keys, after=[mine]
+    )
+    grad_moved = exchange(grad_parts, "z")
+
+    features_to = split_columns(place, hidden[0], after=[grad_parts])
+    own_features = [features_to[0]] + [
+        from_lower(features_to[shift], "x", shift) for shift in (1, 2, 3)
+    ]
+    queries_to = split_queries(place, heads_and_grads, after=[grad_parts])
     queries_from = [heads_and_grads] + [
         from_lower(piece, "z", shift) for shift, piece in enumerate(queries_to, 1)
     ]
 
-    grad_parts, key_heads = value_grad_parts(place, start, heads_and_grads, all_keys)
-    grad_moved = exchange(grad_parts, "z")
+    grad_rows = sum_transposed(place, grad_moved)
+    pieces = [grad_rows] + [from_lower(grad_rows, "x", shift) for shift in (1, 2, 3)]
 
     near = lax.ppermute(mine, "y", [(0, 1), (1, 0), (2, 3), (3, 2)])
-    ready = [grad_parts, queries_from[1], queries_from[3]]
-    far = swap_cores(stack(place, [mine, near], after=ready))
-    parts_to = value_parts(place, own_features, weight_rows, mine, near, far)
+    far = swap_cores(stack(place, [mine, near], after=[grad_parts]))
+    *parts_to, all_features = value_parts(place, own_features, weight_rows, mine, near, far)
     parts_from = [parts_to[0]] + [from_lower(parts_to[shift], "x", shift) for shift in (1, 2, 3)]
     values = sum_values(place, parts_from)
     values_from = [values[0]] + [from_lower(values[shift], "z", shift) for shift in (1, 2, 3)]
 
-    grad_rows = sum_transposed(place, grad_moved, after=[values[0]])
-    pieces = [grad_rows] + [from_lower(grad_rows, "x", shift) for shift in (1, 2, 3)]
-    keep, send = gradient_parts(place, pieces, own_features, after=values_from[1:])
+    keep, send = gradient_parts(
+        place, pieces, all_features, after=[queries_from[1], queries_from[3]]
+    )
     both = add(place, keep, swap_cores(send))
     split = sum_and_split(
-        place, exchange(both, "y"), after=[queries_from[2]]
+        place, exchange(both, "y"), after=[queries_from[2]] + values_from[1:]
     )
     by_feature = exchange(split, ("zh", "z"))
     attention = attend(place, start, queries_from, key_heads, values_from)
@@ -653,6 +689,7 @@
     )
     shards = exchange(shard, ("zh", "y"))
     fresh = join_cores(place, shards, swap_cores(shards)).T
+    attention = attention.reshape(1, 2, 16 * BLOCK, 2 * HD)
     return (attention, new_master, new_first, new_second, fresh)
 
 

time: 256 us -> 243 us (0.949)
  waiting for transfers between devices: 94.9 us -> 79.8 us
  local copies, waits for them, and re-layouts: 13.4 us -> 16.4 us
    ppermute x18 -> x21, waiting for transfers between devices: 89.4 us -> 73.3 us  [from_lower(): return lax.ppermute(array, axis, [(i, (i + shift) % 4) for i in range(4)])]
    all_to_all x6 -> x5, starting transfers between devices: 31.4 us -> 23.8 us  [exchange(): return lax.all_to_all(parts, axes, split_axis=0, concat_axis=0, tiled=True)]
    ppermute x18 -> x21, starting transfers between devices: 23.8 us -> 27.5 us  [from_lower(): return lax.ppermute(array, axis, [(i, (i + shift) % 4) for i in range(4)])]
    pallas_call x13 -> x15, Pallas kernels: 38.6 us -> 41.7 us  [call(): pl.pallas_call(kernel, grid_spec=pltpu.PrefetchScalarGridSpec(num_scalar_...]
    ppermute x3, starting transfers between devices: 3.13 us -> 6.16 us  [swap_cores(): return lax.ppermute(array, 'core', [(0, 1), (1, 0)])]
    unnamed x52 -> x48, local copies, waits for them, and re-layouts: 13.4 us -> 16.4 us
  transfers between devices with their start and end apart: 28 -> 30, of which waited for: 12 -> 17; matrix products, arithmetic and copies ran while one was open for 0% -> 0% of each run, Pallas kernels for 16% -> 20%
where the time goes in v3:
time: 243 us; the launch traced here: 242 us
  waiting for transfers between devices  79.8 us (33%)
  Pallas kernels  59.8 us (25%)
  starting transfers between devices  58.9 us (24%)
  blocking collectives  26.2 us (11%)
  local copies, waits for them, and re-layouts  16.4 us (7%)
    ppermute x21, waiting for transfers between devices, from_lower(): return lax.ppermute(array, axis, [(i, (i + shift) % 4) for i in range(4)])  73.3 us
    pallas_call x15, Pallas kernels, call(): pl.pallas_call(kernel, grid_spec=pltpu.PrefetchScalarGridSpec(num_scalar_...  41.7 us
    ppermute x21, starting transfers between devices, from_lower(): return lax.ppermute(array, axis, [(i, (i + shift) % 4) for i in range(4)])  27.5 us
    all_to_all x1, blocking collectives, exchange(): return lax.all_to_all(parts, axes, split_axis=0, concat_axis=0, tiled=True)  26.2 us
    all_to_all x5, starting transfers between devices, exchange(): return lax.all_to_all(parts, axes, split_axis=0, concat_axis=0, tiled=True)  23.8 us
    unnamed x48, local copies, waits for them, and re-layouts  16.4 us
    pallas_call x1, Pallas kernels, attend(): pl.pallas_call(attention_kernel, grid_spec=pltpu.PrefetchScalarGridSpec(n...  12.4 us
    ppermute x3, starting transfers between devices, swap_cores(): return lax.ppermute(array, 'core', [(0, 1), (1, 0)])  6.16 us
  transfers between devices with their start and end apart: 30, of which 17 were waited for; matrix products, arithmetic and copies ran while one was open for 0% of the time, Pallas kernels for 20%

profile of v3, /device:TPU:33, one launch (start us, length us, event | category | flops | bytes accessed | tf_op | source)
XLA Modules:
  0.0 242.3 jit_solution(16536107186402290251)
XLA Ops:
  0.7 0.9 copy-done.8
  1.7 1.3 pack_columns.1
  2.9 4.0 %all-to-all-start.1 = ((bf16[4,128,256]{2,1,0:T(8,128)(2,1)}), bf16[4,128,256]{2,1,0:T(8,128)(2,1)S(1)}, u32[]{:S(2)}, u32[]{:S(2)}) async-start(bf16[4,128,256]{2,1,0:T(8,128)(2,1)} %pack_columns.1), calls=%async_computation.1 | async-start | bytes 524288 | tf_op jit(solution)/shard_map/all_to_all | solution.py:619
  6.9 5.0 %pack_layers.1 = bf16[4,2,2,128,1024]{4,3,2,1,0:T(8,128)(2,1)} custom-call(bf16[128,2,4096]{2,1,0:T(2,128)(2,1)} %bitcast.23, bf16[128,2,4096]{2,1,0:T(2,128)(2,1)} %bitcast.24), custom_call_target="tpu_custom_call" | custom-call | bytes 8388608 | tf_op jit(solution)/shard_map/pack_layers/pallas_call | solution.py:106
  12.5 4.9 %all-to-all-start = ((bf16[4,2,2,128,1024]{4,3,2,1,0:T(8,128)(2,1)}), bf16[4,2,2,128,1024]{4,3,2,1,0:T(8,128)(2,1)}, u32[]{:S(2)}, u32[]{:S(2)}) async-start(bf16[4,2,2,128,1024]{4,3,2,1,0:T(8,128)(2,1)} %pack_layers.1), calls=%async_computation | async-start | bytes 8388608 | tf_op jit(solution)/shard_map/all_to_all | solution.py:619
  18.0 1.7 collective-permute-start.3
  19.7 1.5 collective-permute-start.4
  21.1 1.4 collective-permute-start.5
  22.6 2.7 %collective-permute-start.1 = (bf16[4,128,256]{2,1,0:T(8,128)(2,1)S(1)}, bf16[4,128,256]{2,1,0:T(8,128)(2,1)S(1)}, u32[]{:S(2)}, u32[]{:S(2)}) collective-permute-start(bf16[4,128,256]{2,1,0:T(8,128)(2,1)S(1)} %all-to-all-done.1.refs_0_.refs_1_), channel_id=1, source_target_pairs={{0,2},{1,3},{2,0},{3,1},{4,6},{5,7},{6,4},{7,5},{8,10},{9,11},{10,... | collective-permute-start | bytes 786440 | tf_op jit(solution)/shard_map/ppermute | solution.py:623
  25.3 0.8 collective-permute-start.2
  26.1 11.0 %collective-permute-done.4.refs_1_ = bf16[112,1024]{1,0:T(8,128)(2,1)S(1)} collective-permute-done((bf16[112,1024]{1,0:T(8,128)(2,1)S(1)}, bf16[112,1024]{1,0:T(8,128)(2,1)S(1)}, u32[]{:S(2)}, u32[]{:S(2)}) %collective-permute-start.4) | collective-permute-done | bytes 229408 | tf_op jit(solution)/shard_map/ppermute | solution.py:623
  37.1 16.1 %collective-permute-done.5.refs_2_ = bf16[112,1024]{1,0:T(8,128)(2,1)S(1)} collective-permute-done((bf16[112,1024]{1,0:T(8,128)(2,1)S(1)}, bf16[112,1024]{1,0:T(8,128)(2,1)S(1)}, u32[]{:S(2)}, u32[]{:S(2)}) %collective-permute-start.5) | collective-permute-done | bytes 229408 | tf_op jit(solution)/shard_map/ppermute | solution.py:623
  53.8 1.4 collective-permute-start.12
  55.4 4.3 %collective-permute-done.1.refs_2_ = bf16[4,128,256]{2,1,0:T(8,128)(2,1)S(1)} collective-permute-done((bf16[4,128,256]{2,1,0:T(8,128)(2,1)S(1)}, bf16[4,128,256]{2,1,0:T(8,128)(2,1)S(1)}, u32[]{:S(2)}, u32[]{:S(2)}) %collective-permute-start.1) | collective-permute-done | bytes 262176 | tf_op jit(solution)/shard_map/ppermute | solution.py:623
  59.7 4.7 %collective-permute-done.2.refs_3_ = bf16[4,128,256]{2,1,0:T(8,128)(2,1)S(1)} collective-permute-done((bf16[4,128,256]{2,1,0:T(8,128)(2,1)S(1)}, bf16[4,128,256]{2,1,0:T(8,128)(2,1)S(1)}, u32[]{:S(2)}, u32[]{:S(2)}) %collective-permute-start.2) | collective-permute-done | bytes 262176 | tf_op jit(solution)/shard_map/ppermute | solution.py:623
  65.1 13.4 %value_grad_parts.1 = (bf16[4,4,128,256]{3,2,1,0:T(8,128)(2,1)}, bf16[4,4,128,128]{3,2,1,0:T(8,128)(2,1)S(1)}) custom-call(s32[4]{0:T(128)S(1)} %pad_add_fusion.at_ref, s32[16,1,128]{2,1,0:T(1,128)S(1)} %bitcast.21, bf16[4,2,2,128,1024]{4,3,2,1,0:T(8,128)(2,1)} %all-to-all-done.refs_1_.refs_2_.refs_0_.q0, ...), custom_call_target="tpu_custom_call" | custom-call | flops 2684354560 | bytes 6291456 | tf_op jit(solution)/shard_map/value_grad_parts/pallas_call | solution.py:60
  78.4 0.8 copy-done.12
  79.2 4.6 %all-to-all-start.2 = ((bf16[4,4,128,256]{3,2,1,0:T(8,128)(2,1)}), bf16[4,4,128,256]{3,2,1,0:T(8,128)(2,1)S(1)}, u32[]{:S(2)}, u32[]{:S(2)}) async-start(bf16[4,4,128,256]{3,2,1,0:T(8,128)(2,1)} %get-tuple-element.29.refs_1_.refs_4_.refs_2_), calls=%async_computation.2 | async-start | bytes 2097152 | tf_op jit(solution)/shard_map/all_to_all | solution.py:619
  83.8 0.8 copy-done.5
  84.7 1.1 copy-done.6
  85.8 1.3 stack.25
  87.1 3.6 %collective-permute-start.13 = (bf16[2,3,112,1024]{3,2,1,0:T(8,128)(2,1)S(1)}, bf16[2,3,112,1024]{3,2,1,0:T(8,128)(2,1)}, u32[]{:S(2)}, u32[]{:S(2)}) collective-permute-start(bf16[2,3,112,1024]{3,2,1,0:T(8,128)(2,1)S(1)} %stack.25), channel_id=1, source_target_pairs={{0,16},{16,0},{1,17},{17,1},{2,18},{18,2},{3,19},{19,3},{4,20},{20... | collective-permute-start | bytes 4128776 | tf_op jit(solution)/shard_map/ppermute | solution.py:627
  90.7 2.4 split_columns.1
  94.2 2.4 collective-permute-start.11
  96.6 4.2 %split_queries.1 = (bf16[4,2,128,256]{3,2,1,0:T(8,128)(2,1)}, bf16[4,2,128,256]{3,2,1,0:T(8,128)(2,1)S(1)}, bf16[4,2,128,256]{3,2,1,0:T(8,128)(2,1)}) custom-call(s32[4]{0:T(128)S(1)} %pad_add_fusion.at_ref, bf16[4,2,2,128,1024]{4,3,2,1,0:T(8,128)(2,1)} %all-to-all-done.refs_1_.refs_2_.refs_0_.q0, ...), custom_call_target="tpu_custom_call" | custom-call | bytes 4194304 | tf_op jit(solution)/shard_map/split_queries/pallas_call | solution.py:60
  100.8 0.8 copy-done.14
  101.6 1.2 collective-permute-start.6
  102.8 4.8 %collective-permute-done.10.refs_2_ = bf16[128,1792]{1,0:T(8,128)(2,1)S(1)} collective-permute-done((bf16[128,1792]{1,0:T(8,128)(2,1)S(1)}, bf16[128,1792]{1,0:T(8,128)(2,1)S(1)}, u32[]{:S(2)}, u32[]{:S(2)}) %collective-permute-start.10) | collective-permute-done | bytes 458784 | tf_op jit(solution)/shard_map/ppermute | solution.py:623
  109.1 6.9 %collective-permute-done.11.refs_3_ = bf16[128,1792]{1,0:T(8,128)(2,1)} collective-permute-done((bf16[128,1792]{1,0:T(8,128)(2,1)}, bf16[128,1792]{1,0:T(8,128)(2,1)}, u32[]{:S(2)}, u32[]{:S(2)}) %collective-permute-start.11) | collective-permute-done | bytes 458784 | tf_op jit(solution)/shard_map/ppermute | solution.py:623
  116.0 1.8 collective-permute-start.20
  117.8 2.0 collective-permute-start.21
  120.5 1.2 copy-done.4
  121.6 1.1 copy-done.7
  122.7 1.0 copy-done.17
  123.8 1.0 copy-done.19
  124.8 5.7 %value_parts.1 = (bf16[512,256]{1,0:T(8,128)(2,1)S(1)}, bf16[512,256]{1,0:T(8,128)(2,1)S(1)}, bf16[512,256]{1,0:T(8,128)(2,1)S(1)}, bf16[512,256]{1,0:T(8,128)(2,1)S(1)}, bf16[512,1792]{1,0:T(8,128)(2,1)S(1)}) custom-call(s32[4]{0:T(128)S(1)} %pad_add_fusion.at_ref, bf16[128,1792]{1,0:T(8,128)(2,1)S(1)} %copy-done.17, ...), custom_call_target="tpu_custom_call" | custom-call | flops 1879048192 | bytes 7340032 | tf_op jit(solution)/shard_map/value_parts/pallas_call | solution.py:60
  132.6 4.9 %gradient_parts.1 = (bf16[4,2,64,1792]{3,2,1,0:T(8,128)(2,1)S(1)}, bf16[4,2,64,1792]{3,2,1,0:T(8,128)(2,1)S(1)}) custom-call(s32[4]{0:T(128)S(1)} %pad_add_fusion.at_ref, bf16[256,512]{1,0:T(8,128)(2,1)S(1)} %sum_transposed.1.refs_0_, bf16[256,512]{1,0:T(8,128)(2,1)S(1)} %collective-permute-done.20.refs_1_, ...), custom_call_target="tpu_custom_call" | custom-call | flops 1879048192 | bytes 7340032 | tf_op jit(solution)/shard_map/gradient_parts/pallas_call | solution.py:60
  137.5 1.7 collective-permute-start.23
  139.3 3.4 %collective-permute-done.23.refs_1_ = bf16[4,2,64,1792]{3,2,1,0:T(8,128)(2,1)S(1)} collective-permute-done((bf16[4,2,64,1792]{3,2,1,0:T(8,128)(2,1)S(1)}, bf16[4,2,64,1792]{3,2,1,0:T(8,128)(2,1)S(1)}, u32[]{:S(2)}, u32[]{:S(2)}) %collective-permute-start.23) | collective-permute-done | bytes 1835040 | tf_op jit(solution)/shard_map/ppermute | solution.py:627
  142.7 1.0 add.7
  143.7 1.2 copy-done.1
  145.0 4.3 %all-to-all-start.3 = ((bf16[4,2,64,1792]{3,2,1,0:T(8,128)(2,1)}), bf16[4,2,64,1792]{3,2,1,0:T(8,128)(2,1)S(1)}, u32[]{:S(2)}, u32[]{:S(2)}) async-start(bf16[4,2,64,1792]{3,2,1,0:T(8,128)(2,1)} %copy-done.1), calls=%async_computation.3 | async-start | bytes 3670016 | tf_op jit(solution)/shard_map/all_to_all | solution.py:619
  149.3 2.1 collective-permute-start.7
  151.9 1.1 collective-permute-start.15
  153.0 1.3 collective-permute-start.16
  154.3 6.4 %collective-permute-done.14.p1 = bf16[512,256]{1,0:T(8,128)(2,1)S(1)} collective-permute-done((bf16[512,256]{1,0:T(8,128)(2,1)}, bf16[512,256]{1,0:T(8,128)(2,1)S(1)}, u32[]{:S(2)}, u32[]{:S(2)}) %collective-permute-start.14) | collective-permute-done | bytes 262176 | tf_op jit(solution)/shard_map/ppermute | solution.py:623
  160.7 3.5 %collective-permute-done.15.p2 = bf16[512,256]{1,0:T(8,128)(2,1)S(1)} collective-permute-done((bf16[512,256]{1,0:T(8,128)(2,1)}, bf16[512,256]{1,0:T(8,128)(2,1)S(1)}, u32[]{:S(2)}, u32[]{:S(2)}) %collective-permute-start.15) | collective-permute-done | bytes 262176 | tf_op jit(solution)/shard_map/ppermute | solution.py:623
  164.3 1.9 collective-permute-done.16.p3
  166.9 4.7 %collective-permute-start.17 = (bf16[4,128,128]{2,1,0:T(8,128)(2,1)S(1)}, bf16[4,128,128]{2,1,0:T(8,128)(2,1)S(1)}, u32[]{:S(2)}, u32[]{:S(2)}) collective-permute-start(bf16[4,128,128]{2,1,0:T(8,128)(2,1)S(1)} %get-tuple-element.43), channel_id=1, source_target_pairs={{0,1},{1,2},{2,3},{3,0},{4,5},{5,6},{6,7},{7,4},{8,9},{9,10},{10,1... | collective-permute-start | bytes 393224 | tf_op jit(solution)/shard_map/ppermute | solution.py:623
  171.6 1.0 collective-permute-start.18
  173.3 8.4 %collective-permute-done.17.v1.refs_2_ = bf16[4,128,128]{2,1,0:T(8,128)(2,1)S(1)} collective-permute-done((bf16[4,128,128]{2,1,0:T(8,128)(2,1)S(1)}, bf16[4,128,128]{2,1,0:T(8,128)(2,1)S(1)}, u32[]{:S(2)}, u32[]{:S(2)}) %collective-permute-start.17) | collective-permute-done | bytes 131104 | tf_op jit(solution)/shard_map/ppermute | solution.py:623
  181.7 2.8 %collective-permute-done.18.v2.refs_3_ = bf16[4,128,128]{2,1,0:T(8,128)(2,1)S(1)} collective-permute-done((bf16[4,128,128]{2,1,0:T(8,128)(2,1)S(1)}, bf16[4,128,128]{2,1,0:T(8,128)(2,1)S(1)}, u32[]{:S(2)}, u32[]{:S(2)}) %collective-permute-start.18) | collective-permute-done | bytes 131104 | tf_op jit(solution)/shard_map/ppermute | solution.py:623
  184.5 2.0 collective-permute-done.19.v3.refs_4_
  186.5 1.8 sum_and_split.1
  188.3 6.1 %all-to-all-start.4 = ((bf16[8,64,448]{2,1,0:T(8,128)(2,1)}), bf16[8,64,448]{2,1,0:T(8,128)(2,1)S(1)}, u32[]{:S(2)}, u32[]{:S(2)}) async-start(bf16[8,64,448]{2,1,0:T(8,128)(2,1)} %sum_and_split.1), calls=%async_computation.4 | async-start | bytes 1048576 | tf_op jit(solution)/shard_map/all_to_all | solution.py:619
  194.3 1.0 copy-done.13
  195.4 12.4 %attend.1.refs_4_ = bf16[2,4,4,128,256]{4,3,2,1,0:T(8,128)(2,1)} custom-call(s32[4]{0:T(128)S(1)} %pad_add_fusion.at_ref, s32[16,1,128]{2,1,0:T(1,128)S(1)} %bitcast.22, bf16[4,2,2,128,1024]{4,3,2,1,0:T(8,128)(2,1)} %all-to-all-done.refs_1_.refs_2_.refs_0_.q0, bf16[4,2,128,256]{3,2,1,0:T(8,128)(2,1)} %collective-permute-done.6.q1.refs_5_, ...), custom_call_target="tpu_custom_call" | custom-call | flops 2684354560 | bytes 6291456 | tf_op jit(solution)/shard_map/attend/pallas_call | solution.py:351
  207.8 1.1 all-to-all-done.4.refs_0_
  208.9 1.6 copy-done.2
  210.4 1.4 update.1
  211.8 26.2 %all_to_all.30.refs_0_ = bf16[8,64,448]{2,1,0:T(8,128)(2,1)S(1)} all-to-all(bf16[8,64,448]{2,1,0:T(8,128)(2,1)S(1)} %get-tuple-element.52), channel_id=1, replica_groups=mesh['zh'=2,'y'=4,'core'=2,'x'=4,'z'=4] {'zh','y'}, dimensions={0} | all-to-all | bytes 917504 | tf_op jit(solution)/shard_map/all_to_all | solution.py:619
  238.1 0.8 collective-permute-start.24
  238.9 1.5 collective-permute-done.24.refs_1_
  240.4 1.9 join_cores.1
  (66 shorter events, 9.9 us)
Async XLA Ops:
  0.7 1.0 copy-start.8
  2.9 9.6 %all-to-all-start.1 = ((bf16[4,128,256]{2,1,0:T(8,128)(2,1)}), bf16[4,128,256]{2,1,0:T(8,128)(2,1)S(1)}, u32[]{:S(2)}, u32[]{:S(2)}) async-start(bf16[4,128,256]{2,1,0:T(8,128)(2,1)} %pack_columns.1), calls=%async_computation.1 | async-start | bytes 524288 | tf_op jit(solution)/shard_map/all_to_all | solution.py:619
  12.0 5.4 %copy-start.3 = (bf16[1024,448]{0,1:T(8,128)(2,1)S(1)}, bf16[1024,448]{0,1:T(8,128)(2,1)}, u32[]{:S(2)}) copy-start(bf16[1024,448]{0,1:T(8,128)(2,1)} %param.14) | copy-start | bytes 2752516
  12.5 52.6 %all-to-all-start = ((bf16[4,2,2,128,1024]{4,3,2,1,0:T(8,128)(2,1)}), bf16[4,2,2,128,1024]{4,3,2,1,0:T(8,128)(2,1)}, u32[]{:S(2)}, u32[]{:S(2)}) async-start(bf16[4,2,2,128,1024]{4,3,2,1,0:T(8,128)(2,1)} %pack_layers.1), calls=%async_computation | async-start | bytes 8388608 | tf_op jit(solution)/shard_map/all_to_all | solution.py:619
  17.4 37.8 %copy-start.23 = (s32[1,2048]{1,0:T(1,128)S(1)}, s32[1,2048]{1,0:T(1,128)}, u32[]{:S(2)}) copy-start(s32[1,2048]{1,0:T(1,128)} %param.13) | copy-start | bytes 24580
  18.0 7.3 %collective-permute-start.3 = (bf16[112,1024]{1,0:T(8,128)(2,1)S(1)}, bf16[112,1024]{1,0:T(8,128)(2,1)S(1)}, u32[]{:S(2)}, u32[]{:S(2)}) collective-permute-start(bf16[112,1024]{1,0:T(8,128)(2,1)S(1)} %own_quarter.1), channel_id=1, source_target_pairs={{0,1},{1,2},{2,3},{3,0},{4,5},{5,6},{6,7},{7,4},{8,9},{9,10},{10,1... | collective-permute-start | bytes 688136 | tf_op jit(solution)/shard_map/ppermute | solution.py:623
  19.7 17.4 %collective-permute-start.4 = (bf16[112,1024]{1,0:T(8,128)(2,1)S(1)}, bf16[112,1024]{1,0:T(8,128)(2,1)S(1)}, u32[]{:S(2)}, u32[]{:S(2)}) collective-permute-start(bf16[112,1024]{1,0:T(8,128)(2,1)S(1)} %own_quarter.1), channel_id=1, source_target_pairs={{0,2},{1,3},{2,0},{3,1},{4,6},{5,7},{6,4},{7,5},{8,10},{9,11},{10,... | collective-permute-start | bytes 688136 | tf_op jit(solution)/shard_map/ppermute | solution.py:623
  21.1 32.1 %collective-permute-start.5 = (bf16[112,1024]{1,0:T(8,128)(2,1)S(1)}, bf16[112,1024]{1,0:T(8,128)(2,1)S(1)}, u32[]{:S(2)}, u32[]{:S(2)}) collective-permute-start(bf16[112,1024]{1,0:T(8,128)(2,1)S(1)} %own_quarter.1), channel_id=1, source_target_pairs={{0,3},{1,0},{2,1},{3,2},{4,7},{5,4},{6,5},{7,6},{8,11},{9,8},{10,9... | collective-permute-start | bytes 688136 | tf_op jit(solution)/shard_map/ppermute | solution.py:623
  22.5 32.9 %collective-permute-start = (bf16[4,128,256]{2,1,0:T(8,128)(2,1)S(1)}, bf16[4,128,256]{2,1,0:T(8,128)(2,1)S(1)}, u32[]{:S(2)}, u32[]{:S(2)}) collective-permute-start(bf16[4,128,256]{2,1,0:T(8,128)(2,1)S(1)} %all-to-all-done.1.refs_0_.refs_1_), channel_id=1, source_target_pairs={{0,1},{1,2},{2,3},{3,0},{4,5},{5,6},{6,7},{7,4},{8,9},{9,10},{10,1... | collective-permute-start | bytes 786440 | tf_op jit(solution)/shard_map/ppermute | solution.py:623
  22.6 37.1 %collective-permute-start.1 = (bf16[4,128,256]{2,1,0:T(8,128)(2,1)S(1)}, bf16[4,128,256]{2,1,0:T(8,128)(2,1)S(1)}, u32[]{:S(2)}, u32[]{:S(2)}) collective-permute-start(bf16[4,128,256]{2,1,0:T(8,128)(2,1)S(1)} %all-to-all-done.1.refs_0_.refs_1_), channel_id=1, source_target_pairs={{0,2},{1,3},{2,0},{3,1},{4,6},{5,7},{6,4},{7,5},{8,10},{9,11},{10,... | collective-permute-start | bytes 786440 | tf_op jit(solution)/shard_map/ppermute | solution.py:623
  25.3 39.1 %collective-permute-start.2 = (bf16[4,128,256]{2,1,0:T(8,128)(2,1)S(1)}, bf16[4,128,256]{2,1,0:T(8,128)(2,1)S(1)}, u32[]{:S(2)}, u32[]{:S(2)}) collective-permute-start(bf16[4,128,256]{2,1,0:T(8,128)(2,1)S(1)} %all-to-all-done.1.refs_0_.refs_1_), channel_id=1, source_target_pairs={{0,3},{1,0},{2,1},{3,2},{4,7},{5,4},{6,5},{7,6},{8,11},{9,8},{10,9... | collective-permute-start | bytes 786440 | tf_op jit(solution)/shard_map/ppermute | solution.py:623
  53.8 30.0 %collective-permute-start.12 = (bf16[3,112,1024]{2,1,0:T(8,128)(2,1)S(1)}, bf16[3,112,1024]{2,1,0:T(8,128)(2,1)S(1)}, u32[]{:S(2)}, u32[]{:S(2)}) collective-permute-start(bf16[3,112,1024]{2,1,0:T(8,128)(2,1)S(1)} %stack.24.refs_4_.refs_0_.refs_5_), channel_id=1, source_target_pairs={{0,32},{32,0},{64,96},{96,64},{1,33},{33,1},{65,97},{97,65},{2,34}... | collective-permute-start | bytes 2064392 | tf_op jit(solution)/shard_map/ppermute | solution.py:671
  78.4 0.8 copy-start.12
  79.2 29.1 %all-to-all-start.2 = ((bf16[4,4,128,256]{3,2,1,0:T(8,128)(2,1)}), bf16[4,4,128,256]{3,2,1,0:T(8,128)(2,1)S(1)}, u32[]{:S(2)}, u32[]{:S(2)}) async-start(bf16[4,4,128,256]{3,2,1,0:T(8,128)(2,1)} %get-tuple-element.29.refs_1_.refs_4_.refs_2_), calls=%async_computation.2 | async-start | bytes 2097152 | tf_op jit(solution)/shard_map/all_to_all | solution.py:619
  83.8 6.9 %copy-start = (bf16[1,128,7168]{2,1,0:T(8,128)(2,1)S(1)}, bf16[1,128,7168]{2,1,0:T(8,128)(2,1)}, u32[]{:S(2)}) copy-start(bf16[1,128,7168]{2,1,0:T(8,128)(2,1)} %param.9) | copy-start | bytes 5505028
  83.8 0.8 copy-start.5
  84.7 1.1 copy-start.6
  87.1 32.8 %collective-permute-start.13 = (bf16[2,3,112,1024]{3,2,1,0:T(8,128)(2,1)S(1)}, bf16[2,3,112,1024]{3,2,1,0:T(8,128)(2,1)}, u32[]{:S(2)}, u32[]{:S(2)}) collective-permute-start(bf16[2,3,112,1024]{3,2,1,0:T(8,128)(2,1)S(1)} %stack.25), channel_id=1, source_target_pairs={{0,16},{16,0},{1,17},{17,1},{2,18},{18,2},{3,19},{19,3},{4,20},{20... | collective-permute-start | bytes 4128776 | tf_op jit(solution)/shard_map/ppermute | solution.py:627
  93.1 0.8 copy-start.16
  93.9 13.7 %collective-permute-start.10 = (bf16[128,1792]{1,0:T(8,128)(2,1)S(1)}, bf16[128,1792]{1,0:T(8,128)(2,1)S(1)}, u32[]{:S(2)}, u32[]{:S(2)}) collective-permute-start(bf16[128,1792]{1,0:T(8,128)(2,1)S(1)} %get-tuple-element.36), channel_id=1, source_target_pairs={{0,8},{4,12},{8,0},{12,4},{1,9},{5,13},{9,1},{13,5},{2,10},{6,14},... | collective-permute-start | bytes 1376264 | tf_op jit(solution)/shard_map/ppermute | solution.py:623
  94.2 21.8 %collective-permute-start.11 = (bf16[128,1792]{1,0:T(8,128)(2,1)}, bf16[128,1792]{1,0:T(8,128)(2,1)}, u32[]{:S(2)}, u32[]{:S(2)}) collective-permute-start(bf16[128,1792]{1,0:T(8,128)(2,1)} %get-tuple-element.37), channel_id=1, source_target_pairs={{0,12},{4,0},{8,4},{12,8},{1,13},{5,1},{9,5},{13,9},{2,14},{6,2},{... | collective-permute-start | bytes 1376264 | tf_op jit(solution)/shard_map/ppermute | solution.py:623
  96.6 21.3 %collective-permute-start.9 = (bf16[128,1792]{1,0:T(8,128)(2,1)}, bf16[128,1792]{1,0:T(8,128)(2,1)}, u32[]{:S(2)}, u32[]{:S(2)}) collective-permute-start(bf16[128,1792]{1,0:T(8,128)(2,1)} %get-tuple-element.35), channel_id=1, source_target_pairs={{0,4},{4,8},{8,12},{12,0},{1,5},{5,9},{9,13},{13,1},{2,6},{6,10},{... | collective-permute-start | bytes 1376264 | tf_op jit(solution)/shard_map/ppermute | solution.py:623
  100.8 0.8 copy-start.14
  101.6 31.0 %collective-permute-start.6 = (bf16[4,2,128,256]{3,2,1,0:T(8,128)(2,1)}, bf16[4,2,128,256]{3,2,1,0:T(8,128)(2,1)}, u32[]{:S(2)}, u32[]{:S(2)}) collective-permute-start(bf16[4,2,128,256]{3,2,1,0:T(8,128)(2,1)} %get-tuple-element.30), channel_id=1, source_target_pairs={{0,1},{1,2},{2,3},{3,0},{4,5},{5,6},{6,7},{7,4},{8,9},{9,10},{10,1... | collective-permute-start | bytes 1572872 | tf_op jit(solution)/shard_map/ppermute | solution.py:623
  107.5 0.8 copy-start.18
  108.3 24.3 %collective-permute-start.8 = (bf16[4,2,128,256]{3,2,1,0:T(8,128)(2,1)}, bf16[4,2,128,256]{3,2,1,0:T(8,128)(2,1)}, u32[]{:S(2)}, u32[]{:S(2)}) collective-permute-start(bf16[4,2,128,256]{3,2,1,0:T(8,128)(2,1)} %get-tuple-element.32), channel_id=1, source_target_pairs={{0,3},{1,0},{2,1},{3,2},{4,7},{5,4},{6,5},{7,6},{8,11},{9,8},{10,9... | collective-permute-start | bytes 1572872 | tf_op jit(solution)/shard_map/ppermute | solution.py:623
  116.0 16.6 %collective-permute-start.20 = (bf16[256,512]{1,0:T(8,128)(2,1)S(1)}, bf16[256,512]{1,0:T(8,128)(2,1)S(1)}, u32[]{:S(2)}, u32[]{:S(2)}) collective-permute-start(bf16[256,512]{1,0:T(8,128)(2,1)S(1)} %sum_transposed.1.refs_0_), channel_id=1, source_target_pairs={{0,4},{4,8},{8,12},{12,0},{1,5},{5,9},{9,13},{13,1},{2,6},{6,10},{... | collective-permute-start | bytes 786440 | tf_op jit(solution)/shard_map/ppermute | solution.py:623
  117.8 14.8 %collective-permute-start.21 = (bf16[256,512]{1,0:T(8,128)(2,1)S(1)}, bf16[256,512]{1,0:T(8,128)(2,1)S(1)}, u32[]{:S(2)}, u32[]{:S(2)}) collective-permute-start(bf16[256,512]{1,0:T(8,128)(2,1)S(1)} %sum_transposed.1.refs_0_), channel_id=1, source_target_pairs={{0,8},{4,12},{8,0},{12,4},{1,9},{5,13},{9,1},{13,5},{2,10},{6,14},... | collective-permute-start | bytes 786440 | tf_op jit(solution)/shard_map/ppermute | solution.py:623
  119.9 12.7 %collective-permute-start.22 = (bf16[256,512]{1,0:T(8,128)(2,1)S(1)}, bf16[256,512]{1,0:T(8,128)(2,1)S(1)}, u32[]{:S(2)}, u32[]{:S(2)}) collective-permute-start(bf16[256,512]{1,0:T(8,128)(2,1)S(1)} %sum_transposed.1.refs_0_), channel_id=1, source_target_pairs={{0,12},{4,0},{8,4},{12,8},{1,13},{5,1},{9,5},{13,9},{2,14},{6,2},{... | collective-permute-start | bytes 786440 | tf_op jit(solution)/shard_map/ppermute | solution.py:623
  120.5 1.2 copy-start.4
  121.6 1.1 copy-start.7
  122.7 1.0 copy-start.17
  123.8 1.0 copy-start.19
  130.5 0.7 copy-start.20
  131.2 0.7 copy-start.21
  131.9 0.7 copy-start.22
  137.5 5.1 %collective-permute-start.23 = (bf16[4,2,64,1792]{3,2,1,0:T(8,128)(2,1)S(1)}, bf16[4,2,64,1792]{3,2,1,0:T(8,128)(2,1)S(1)}, u32[]{:S(2)}, u32[]{:S(2)}) collective-permute-start(bf16[4,2,64,1792]{3,2,1,0:T(8,128)(2,1)S(1)} %get-tuple-element.48), channel_id=1, source_target_pairs={{0,16},{16,0},{1,17},{17,1},{2,18},{18,2},{3,19},{19,3},{4,20},{20... | collective-permute-start | bytes 5505032 | tf_op jit(solution)/shard_map/ppermute | solution.py:627
  143.7 1.2 copy-start.1
  145.0 4.3 %copy-start.15 = (bf16[4,2,128,256]{3,2,1,0:T(8,128)(2,1)S(1)}, bf16[4,2,128,256]{3,2,1,0:T(8,128)(2,1)}, u32[]{:S(2)}) copy-start(bf16[4,2,128,256]{3,2,1,0:T(8,128)(2,1)} %copy-done.14) | copy-start | bytes 1572868
  145.0 41.5 %all-to-all-start.3 = ((bf16[4,2,64,1792]{3,2,1,0:T(8,128)(2,1)}), bf16[4,2,64,1792]{3,2,1,0:T(8,128)(2,1)S(1)}, u32[]{:S(2)}, u32[]{:S(2)}) async-start(bf16[4,2,64,1792]{3,2,1,0:T(8,128)(2,1)} %copy-done.1), calls=%async_computation.3 | async-start | bytes 3670016 | tf_op jit(solution)/shard_map/all_to_all | solution.py:619
  149.3 24.0 %collective-permute-start.7 = (bf16[4,2,128,256]{3,2,1,0:T(8,128)(2,1)S(1)}, bf16[4,2,128,256]{3,2,1,0:T(8,128)(2,1)S(1)}, u32[]{:S(2)}, u32[]{:S(2)}) collective-permute-start(bf16[4,2,128,256]{3,2,1,0:T(8,128)(2,1)S(1)} %copy-done.15), channel_id=1, source_target_pairs={{0,2},{1,3},{2,0},{3,1},{4,6},{5,7},{6,4},{7,5},{8,10},{9,11},{10,... | collective-permute-start | bytes 1572872 | tf_op jit(solution)/shard_map/ppermute | solution.py:623
  151.4 9.4 %collective-permute-start.14 = (bf16[512,256]{1,0:T(8,128)(2,1)}, bf16[512,256]{1,0:T(8,128)(2,1)S(1)}, u32[]{:S(2)}, u32[]{:S(2)}) collective-permute-start(bf16[512,256]{1,0:T(8,128)(2,1)} %copy-done.22), channel_id=1, source_target_pairs={{0,4},{4,8},{8,12},{12,0},{1,5},{5,9},{9,13},{13,1},{2,6},{6,10},{... | collective-permute-start | bytes 786440 | tf_op jit(solution)/shard_map/ppermute | solution.py:623
  151.9 12.4 %collective-permute-start.15 = (bf16[512,256]{1,0:T(8,128)(2,1)}, bf16[512,256]{1,0:T(8,128)(2,1)S(1)}, u32[]{:S(2)}, u32[]{:S(2)}) collective-permute-start(bf16[512,256]{1,0:T(8,128)(2,1)} %copy-done.21), channel_id=1, source_target_pairs={{0,8},{4,12},{8,0},{12,4},{1,9},{5,13},{9,1},{13,5},{2,10},{6,14},... | collective-permute-start | bytes 786440 | tf_op jit(solution)/shard_map/ppermute | solution.py:623
  153.0 13.2 %collective-permute-start.16 = (bf16[512,256]{1,0:T(8,128)(2,1)}, bf16[512,256]{1,0:T(8,128)(2,1)S(1)}, u32[]{:S(2)}, u32[]{:S(2)}) collective-permute-start(bf16[512,256]{1,0:T(8,128)(2,1)} %copy-done.20), channel_id=1, source_target_pairs={{0,12},{4,0},{8,4},{12,8},{1,13},{5,1},{9,5},{13,9},{2,14},{6,2},{... | collective-permute-start | bytes 786440 | tf_op jit(solution)/shard_map/ppermute | solution.py:623
  166.9 14.8 %collective-permute-start.17 = (bf16[4,128,128]{2,1,0:T(8,128)(2,1)S(1)}, bf16[4,128,128]{2,1,0:T(8,128)(2,1)S(1)}, u32[]{:S(2)}, u32[]{:S(2)}) collective-permute-start(bf16[4,128,128]{2,1,0:T(8,128)(2,1)S(1)} %get-tuple-element.43), channel_id=1, source_target_pairs={{0,1},{1,2},{2,3},{3,0},{4,5},{5,6},{6,7},{7,4},{8,9},{9,10},{10,1... | collective-permute-start | bytes 393224 | tf_op jit(solution)/shard_map/ppermute | solution.py:623
  171.6 12.8 %collective-permute-start.18 = (bf16[4,128,128]{2,1,0:T(8,128)(2,1)S(1)}, bf16[4,128,128]{2,1,0:T(8,128)(2,1)S(1)}, u32[]{:S(2)}, u32[]{:S(2)}) collective-permute-start(bf16[4,128,128]{2,1,0:T(8,128)(2,1)S(1)} %get-tuple-element.44), channel_id=1, source_target_pairs={{0,2},{1,3},{2,0},{3,1},{4,6},{5,7},{6,4},{7,5},{8,10},{9,11},{10,... | collective-permute-start | bytes 393224 | tf_op jit(solution)/shard_map/ppermute | solution.py:623
  172.6 13.9 %collective-permute-start.19 = (bf16[4,128,128]{2,1,0:T(8,128)(2,1)S(1)}, bf16[4,128,128]{2,1,0:T(8,128)(2,1)S(1)}, u32[]{:S(2)}, u32[]{:S(2)}) collective-permute-start(bf16[4,128,128]{2,1,0:T(8,128)(2,1)S(1)} %get-tuple-element.45), channel_id=1, source_target_pairs={{0,3},{1,0},{2,1},{3,2},{4,7},{5,4},{6,5},{7,6},{8,11},{9,8},{10,9... | collective-permute-start | bytes 393224 | tf_op jit(solution)/shard_map/ppermute | solution.py:623
  188.3 20.6 %all-to-all-start.4 = ((bf16[8,64,448]{2,1,0:T(8,128)(2,1)}), bf16[8,64,448]{2,1,0:T(8,128)(2,1)S(1)}, u32[]{:S(2)}, u32[]{:S(2)}) async-start(bf16[8,64,448]{2,1,0:T(8,128)(2,1)} %sum_and_split.1), calls=%async_computation.4 | async-start | bytes 1048576 | tf_op jit(solution)/shard_map/all_to_all | solution.py:619
  194.3 1.0 copy-start.13
  195.3 13.5 %copy-start.9 = (f32[64,448]{1,0:T(8,128)S(1)}, f32[64,448]{1,0:T(8,128)}, u32[]{:S(2)}) copy-start(f32[64,448]{1,0:T(8,128)} %refs_1_.1) | copy-start | bytes 344068
  195.3 13.5 %copy-start.10 = (f32[64,448]{1,0:T(8,128)S(1)}, f32[64,448]{1,0:T(8,128)}, u32[]{:S(2)}) copy-start(f32[64,448]{1,0:T(8,128)} %refs_2_.1) | copy-start | bytes 344068
  195.4 13.5 %copy-start.11 = (f32[64,448]{1,0:T(8,128)S(1)}, f32[64,448]{1,0:T(8,128)}, u32[]{:S(2)}) copy-start(f32[64,448]{1,0:T(8,128)} %refs_3_.1) | copy-start | bytes 344068
  208.9 1.6 copy-start.2
  238.1 2.3 collective-permute-start.24

commit v4 on v3

--- a/solution.py
+++ b/solution.py
@@ -218,13 +218,17 @@
 
     own, places = key_places(i, z, 0)
     bias = mask_bias(i, own, start_ref[4 * i + own])
+    contribs = []
     for kv in range(2):
         keys = jnp.concatenate(
             [key_ref[held, at, :, pl.ds(kv * HD, HD)] for held, at in places], axis=0
         )
         exps, inverse = exp_scores(keys, head_rows(q_ref, kv), bias)
         probabilities = (exps * inverse).astype(bf16)
-        contrib = jnp.dot(probabilities, head_rows(g_ref, kv), preferred_element_type=f32)
+        contribs.append(
+            jnp.dot(probabilities, head_rows(g_ref, kv), preferred_element_type=f32)
+        )
+    for kv, contrib in enumerate(contribs):
         for back, (held, at) in enumerate(places):
             acc[held, at, :, pl.ds(kv * HD, HD)] += contrib[back * BLOCK : (back + 1) * BLOCK]
 

time: 243 us -> 243 us (level)
  no operation moved by 1% of the time
where the time goes in v4:
time: 243 us; the launch traced here: 242 us
  waiting for transfers between devices  79.8 us (33%)
  Pallas kernels  59.8 us (25%)
  starting transfers between devices  58.9 us (24%)
  blocking collectives  26.2 us (11%)
  local copies, waits for them, and re-layouts  16.4 us (7%)
    ppermute x21, waiting for transfers between devices, from_lower(): return lax.ppermute(array, axis, [(i, (i + shift) % 4) for i in range(4)])  73.3 us
    pallas_call x15, Pallas kernels, call(): pl.pallas_call(kernel, grid_spec=pltpu.PrefetchScalarGridSpec(num_scalar_...  41.7 us
    ppermute x21, starting transfers between devices, from_lower(): return lax.ppermute(array, axis, [(i, (i + shift) % 4) for i in range(4)])  27.5 us
    all_to_all x1, blocking collectives, exchange(): return lax.all_to_all(parts, axes, split_axis=0, concat_axis=0, tiled=True)  26.2 us
    all_to_all x5, starting transfers between devices, exchange(): return lax.all_to_all(parts, axes, split_axis=0, concat_axis=0, tiled=True)  23.8 us
    unnamed x48, local copies, waits for them, and re-layouts  16.4 us
    pallas_call x1, Pallas kernels, attend(): pl.pallas_call(attention_kernel, grid_spec=pltpu.PrefetchScalarGridSpec(n...  12.4 us
    ppermute x3, starting transfers between devices, swap_cores(): return lax.ppermute(array, 'core', [(0, 1), (1, 0)])  6.16 us
  transfers between devices with their start and end apart: 30, of which 17 were waited for; matrix products, arithmetic and copies ran while one was open for 0% of the time, Pallas kernels for 20%

profile of v4, /device:TPU:33, one launch (start us, length us, event | category | flops | bytes accessed | tf_op | source)
XLA Modules:
  0.0 242.3 jit_solution(16536107186402290251)
XLA Ops:
  0.7 0.9 copy-done.8
  1.7 1.3 pack_columns.1
  2.9 4.0 %all-to-all-start.1 = ((bf16[4,128,256]{2,1,0:T(8,128)(2,1)}), bf16[4,128,256]{2,1,0:T(8,128)(2,1)S(1)}, u32[]{:S(2)}, u32[]{:S(2)}) async-start(bf16[4,128,256]{2,1,0:T(8,128)(2,1)} %pack_columns.1), calls=%async_computation.1 | async-start | bytes 524288 | tf_op jit(solution)/shard_map/all_to_all | solution.py:623
  6.9 5.0 %pack_layers.1 = bf16[4,2,2,128,1024]{4,3,2,1,0:T(8,128)(2,1)} custom-call(bf16[128,2,4096]{2,1,0:T(2,128)(2,1)} %bitcast.23, bf16[128,2,4096]{2,1,0:T(2,128)(2,1)} %bitcast.24), custom_call_target="tpu_custom_call" | custom-call | bytes 8388608 | tf_op jit(solution)/shard_map/pack_layers/pallas_call | solution.py:106
  12.5 4.9 %all-to-all-start = ((bf16[4,2,2,128,1024]{4,3,2,1,0:T(8,128)(2,1)}), bf16[4,2,2,128,1024]{4,3,2,1,0:T(8,128)(2,1)}, u32[]{:S(2)}, u32[]{:S(2)}) async-start(bf16[4,2,2,128,1024]{4,3,2,1,0:T(8,128)(2,1)} %pack_layers.1), calls=%async_computation | async-start | bytes 8388608 | tf_op jit(solution)/shard_map/all_to_all | solution.py:623
  18.0 1.7 collective-permute-start.3
  19.7 1.5 collective-permute-start.4
  21.1 1.4 collective-permute-start.5
  22.6 2.7 %collective-permute-start.1 = (bf16[4,128,256]{2,1,0:T(8,128)(2,1)S(1)}, bf16[4,128,256]{2,1,0:T(8,128)(2,1)S(1)}, u32[]{:S(2)}, u32[]{:S(2)}) collective-permute-start(bf16[4,128,256]{2,1,0:T(8,128)(2,1)S(1)} %all-to-all-done.1.refs_0_.refs_1_), channel_id=1, source_target_pairs={{0,2},{1,3},{2,0},{3,1},{4,6},{5,7},{6,4},{7,5},{8,10},{9,11},{10,... | collective-permute-start | bytes 786440 | tf_op jit(solution)/shard_map/ppermute | solution.py:627
  25.3 0.8 collective-permute-start.2
  26.1 11.0 %collective-permute-done.4.refs_1_ = bf16[112,1024]{1,0:T(8,128)(2,1)S(1)} collective-permute-done((bf16[112,1024]{1,0:T(8,128)(2,1)S(1)}, bf16[112,1024]{1,0:T(8,128)(2,1)S(1)}, u32[]{:S(2)}, u32[]{:S(2)}) %collective-permute-start.4) | collective-permute-done | bytes 229408 | tf_op jit(solution)/shard_map/ppermute | solution.py:627
  37.1 16.1 %collective-permute-done.5.refs_2_ = bf16[112,1024]{1,0:T(8,128)(2,1)S(1)} collective-permute-done((bf16[112,1024]{1,0:T(8,128)(2,1)S(1)}, bf16[112,1024]{1,0:T(8,128)(2,1)S(1)}, u32[]{:S(2)}, u32[]{:S(2)}) %collective-permute-start.5) | collective-permute-done | bytes 229408 | tf_op jit(solution)/shard_map/ppermute | solution.py:627
  53.8 1.4 collective-permute-start.12
  55.4 4.3 %collective-permute-done.1.refs_2_ = bf16[4,128,256]{2,1,0:T(8,128)(2,1)S(1)} collective-permute-done((bf16[4,128,256]{2,1,0:T(8,128)(2,1)S(1)}, bf16[4,128,256]{2,1,0:T(8,128)(2,1)S(1)}, u32[]{:S(2)}, u32[]{:S(2)}) %collective-permute-start.1) | collective-permute-done | bytes 262176 | tf_op jit(solution)/shard_map/ppermute | solution.py:627
  59.7 4.7 %collective-permute-done.2.refs_3_ = bf16[4,128,256]{2,1,0:T(8,128)(2,1)S(1)} collective-permute-done((bf16[4,128,256]{2,1,0:T(8,128)(2,1)S(1)}, bf16[4,128,256]{2,1,0:T(8,128)(2,1)S(1)}, u32[]{:S(2)}, u32[]{:S(2)}) %collective-permute-start.2) | collective-permute-done | bytes 262176 | tf_op jit(solution)/shard_map/ppermute | solution.py:627
  65.1 13.4 %value_grad_parts.1 = (bf16[4,4,128,256]{3,2,1,0:T(8,128)(2,1)}, bf16[4,4,128,128]{3,2,1,0:T(8,128)(2,1)S(1)}) custom-call(s32[4]{0:T(128)S(1)} %pad_add_fusion.at_ref, s32[16,1,128]{2,1,0:T(1,128)S(1)} %bitcast.21, bf16[4,2,2,128,1024]{4,3,2,1,0:T(8,128)(2,1)} %all-to-all-done.refs_1_.refs_2_.refs_0_.q0, ...), custom_call_target="tpu_custom_call" | custom-call | flops 2684354560 | bytes 6291456 | tf_op jit(solution)/shard_map/value_grad_parts/pallas_call | solution.py:60
  78.4 0.8 copy-done.12
  79.2 4.6 %all-to-all-start.2 = ((bf16[4,4,128,256]{3,2,1,0:T(8,128)(2,1)}), bf16[4,4,128,256]{3,2,1,0:T(8,128)(2,1)S(1)}, u32[]{:S(2)}, u32[]{:S(2)}) async-start(bf16[4,4,128,256]{3,2,1,0:T(8,128)(2,1)} %get-tuple-element.29.refs_1_.refs_4_.refs_2_), calls=%async_computation.2 | async-start | bytes 2097152 | tf_op jit(solution)/shard_map/all_to_all | solution.py:623
  83.8 0.8 copy-done.5
  84.7 1.1 copy-done.6
  85.8 1.3 stack.25
  87.1 3.6 %collective-permute-start.13 = (bf16[2,3,112,1024]{3,2,1,0:T(8,128)(2,1)S(1)}, bf16[2,3,112,1024]{3,2,1,0:T(8,128)(2,1)}, u32[]{:S(2)}, u32[]{:S(2)}) collective-permute-start(bf16[2,3,112,1024]{3,2,1,0:T(8,128)(2,1)S(1)} %stack.25), channel_id=1, source_target_pairs={{0,16},{16,0},{1,17},{17,1},{2,18},{18,2},{3,19},{19,3},{4,20},{20... | collective-permute-start | bytes 4128776 | tf_op jit(solution)/shard_map/ppermute | solution.py:631
  90.7 2.4 split_columns.1
  94.2 2.4 collective-permute-start.11
  96.6 4.2 %split_queries.1 = (bf16[4,2,128,256]{3,2,1,0:T(8,128)(2,1)}, bf16[4,2,128,256]{3,2,1,0:T(8,128)(2,1)S(1)}, bf16[4,2,128,256]{3,2,1,0:T(8,128)(2,1)}) custom-call(s32[4]{0:T(128)S(1)} %pad_add_fusion.at_ref, bf16[4,2,2,128,1024]{4,3,2,1,0:T(8,128)(2,1)} %all-to-all-done.refs_1_.refs_2_.refs_0_.q0, ...), custom_call_target="tpu_custom_call" | custom-call | bytes 4194304 | tf_op jit(solution)/shard_map/split_queries/pallas_call | solution.py:60
  100.8 0.8 copy-done.14
  101.6 1.2 collective-permute-start.6
  102.8 4.8 %collective-permute-done.10.refs_2_ = bf16[128,1792]{1,0:T(8,128)(2,1)S(1)} collective-permute-done((bf16[128,1792]{1,0:T(8,128)(2,1)S(1)}, bf16[128,1792]{1,0:T(8,128)(2,1)S(1)}, u32[]{:S(2)}, u32[]{:S(2)}) %collective-permute-start.10) | collective-permute-done | bytes 458784 | tf_op jit(solution)/shard_map/ppermute | solution.py:627
  109.1 6.9 %collective-permute-done.11.refs_3_ = bf16[128,1792]{1,0:T(8,128)(2,1)} collective-permute-done((bf16[128,1792]{1,0:T(8,128)(2,1)}, bf16[128,1792]{1,0:T(8,128)(2,1)}, u32[]{:S(2)}, u32[]{:S(2)}) %collective-permute-start.11) | collective-permute-done | bytes 458784 | tf_op jit(solution)/shard_map/ppermute | solution.py:627
  116.0 1.8 collective-permute-start.20
  117.8 2.0 collective-permute-start.21
  120.5 1.2 copy-done.4
  121.6 1.1 copy-done.7
  122.7 1.0 copy-done.17
  123.8 1.0 copy-done.19
  124.8 5.7 %value_parts.1 = (bf16[512,256]{1,0:T(8,128)(2,1)S(1)}, bf16[512,256]{1,0:T(8,128)(2,1)S(1)}, bf16[512,256]{1,0:T(8,128)(2,1)S(1)}, bf16[512,256]{1,0:T(8,128)(2,1)S(1)}, bf16[512,1792]{1,0:T(8,128)(2,1)S(1)}) custom-call(s32[4]{0:T(128)S(1)} %pad_add_fusion.at_ref, bf16[128,1792]{1,0:T(8,128)(2,1)S(1)} %copy-done.17, ...), custom_call_target="tpu_custom_call" | custom-call | flops 1879048192 | bytes 7340032 | tf_op jit(solution)/shard_map/value_parts/pallas_call | solution.py:60
  132.6 4.9 %gradient_parts.1 = (bf16[4,2,64,1792]{3,2,1,0:T(8,128)(2,1)S(1)}, bf16[4,2,64,1792]{3,2,1,0:T(8,128)(2,1)S(1)}) custom-call(s32[4]{0:T(128)S(1)} %pad_add_fusion.at_ref, bf16[256,512]{1,0:T(8,128)(2,1)S(1)} %sum_transposed.1.refs_0_, bf16[256,512]{1,0:T(8,128)(2,1)S(1)} %collective-permute-done.20.refs_1_, ...), custom_call_target="tpu_custom_call" | custom-call | flops 1879048192 | bytes 7340032 | tf_op jit(solution)/shard_map/gradient_parts/pallas_call | solution.py:60
  137.5 1.7 collective-permute-start.23
  139.3 3.4 %collective-permute-done.23.refs_1_ = bf16[4,2,64,1792]{3,2,1,0:T(8,128)(2,1)S(1)} collective-permute-done((bf16[4,2,64,1792]{3,2,1,0:T(8,128)(2,1)S(1)}, bf16[4,2,64,1792]{3,2,1,0:T(8,128)(2,1)S(1)}, u32[]{:S(2)}, u32[]{:S(2)}) %collective-permute-start.23) | collective-permute-done | bytes 1835040 | tf_op jit(solution)/shard_map/ppermute | solution.py:631
  142.7 1.0 add.7
  143.7 1.2 copy-done.1
  145.0 4.3 %all-to-all-start.3 = ((bf16[4,2,64,1792]{3,2,1,0:T(8,128)(2,1)}), bf16[4,2,64,1792]{3,2,1,0:T(8,128)(2,1)S(1)}, u32[]{:S(2)}, u32[]{:S(2)}) async-start(bf16[4,2,64,1792]{3,2,1,0:T(8,128)(2,1)} %copy-done.1), calls=%async_computation.3 | async-start | bytes 3670016 | tf_op jit(solution)/shard_map/all_to_all | solution.py:623
  149.3 2.1 collective-permute-start.7
  151.9 1.1 collective-permute-start.15
  153.0 1.3 collective-permute-start.16
  154.3 6.4 %collective-permute-done.14.p1 = bf16[512,256]{1,0:T(8,128)(2,1)S(1)} collective-permute-done((bf16[512,256]{1,0:T(8,128)(2,1)}, bf16[512,256]{1,0:T(8,128)(2,1)S(1)}, u32[]{:S(2)}, u32[]{:S(2)}) %collective-permute-start.14) | collective-permute-done | bytes 262176 | tf_op jit(solution)/shard_map/ppermute | solution.py:627
  160.7 3.5 %collective-permute-done.15.p2 = bf16[512,256]{1,0:T(8,128)(2,1)S(1)} collective-permute-done((bf16[512,256]{1,0:T(8,128)(2,1)}, bf16[512,256]{1,0:T(8,128)(2,1)S(1)}, u32[]{:S(2)}, u32[]{:S(2)}) %collective-permute-start.15) | collective-permute-done | bytes 262176 | tf_op jit(solution)/shard_map/ppermute | solution.py:627
  164.3 1.9 collective-permute-done.16.p3
  166.9 4.7 %collective-permute-start.17 = (bf16[4,128,128]{2,1,0:T(8,128)(2,1)S(1)}, bf16[4,128,128]{2,1,0:T(8,128)(2,1)S(1)}, u32[]{:S(2)}, u32[]{:S(2)}) collective-permute-start(bf16[4,128,128]{2,1,0:T(8,128)(2,1)S(1)} %get-tuple-element.43), channel_id=1, source_target_pairs={{0,1},{1,2},{2,3},{3,0},{4,5},{5,6},{6,7},{7,4},{8,9},{9,10},{10,1... | collective-permute-start | bytes 393224 | tf_op jit(solution)/shard_map/ppermute | solution.py:627
  171.6 1.0 collective-permute-start.18
  173.3 8.4 %collective-permute-done.17.v1.refs_2_ = bf16[4,128,128]{2,1,0:T(8,128)(2,1)S(1)} collective-permute-done((bf16[4,128,128]{2,1,0:T(8,128)(2,1)S(1)}, bf16[4,128,128]{2,1,0:T(8,128)(2,1)S(1)}, u32[]{:S(2)}, u32[]{:S(2)}) %collective-permute-start.17) | collective-permute-done | bytes 131104 | tf_op jit(solution)/shard_map/ppermute | solution.py:627
  181.7 2.8 %collective-permute-done.18.v2.refs_3_ = bf16[4,128,128]{2,1,0:T(8,128)(2,1)S(1)} collective-permute-done((bf16[4,128,128]{2,1,0:T(8,128)(2,1)S(1)}, bf16[4,128,128]{2,1,0:T(8,128)(2,1)S(1)}, u32[]{:S(2)}, u32[]{:S(2)}) %collective-permute-start.18) | collective-permute-done | bytes 131104 | tf_op jit(solution)/shard_map/ppermute | solution.py:627
  184.5 2.0 collective-permute-done.19.v3.refs_4_
  186.5 1.8 sum_and_split.1
  188.3 6.1 %all-to-all-start.4 = ((bf16[8,64,448]{2,1,0:T(8,128)(2,1)}), bf16[8,64,448]{2,1,0:T(8,128)(2,1)S(1)}, u32[]{:S(2)}, u32[]{:S(2)}) async-start(bf16[8,64,448]{2,1,0:T(8,128)(2,1)} %sum_and_split.1), calls=%async_computation.4 | async-start | bytes 1048576 | tf_op jit(solution)/shard_map/all_to_all | solution.py:623
  194.3 1.0 copy-done.13
  195.4 12.4 %attend.1.refs_4_ = bf16[2,4,4,128,256]{4,3,2,1,0:T(8,128)(2,1)} custom-call(s32[4]{0:T(128)S(1)} %pad_add_fusion.at_ref, s32[16,1,128]{2,1,0:T(1,128)S(1)} %bitcast.22, bf16[4,2,2,128,1024]{4,3,2,1,0:T(8,128)(2,1)} %all-to-all-done.refs_1_.refs_2_.refs_0_.q0, bf16[4,2,128,256]{3,2,1,0:T(8,128)(2,1)} %collective-permute-done.6.q1.refs_5_, ...), custom_call_target="tpu_custom_call" | custom-call | flops 2684354560 | bytes 6291456 | tf_op jit(solution)/shard_map/attend/pallas_call | solution.py:355
  207.8 1.1 all-to-all-done.4.refs_0_
  208.9 1.6 copy-done.2
  210.4 1.4 update.1
  211.8 26.2 %all_to_all.30.refs_0_ = bf16[8,64,448]{2,1,0:T(8,128)(2,1)S(1)} all-to-all(bf16[8,64,448]{2,1,0:T(8,128)(2,1)S(1)} %get-tuple-element.52), channel_id=1, replica_groups=mesh['zh'=2,'y'=4,'core'=2,'x'=4,'z'=4] {'zh','y'}, dimensions={0} | all-to-all | bytes 917504 | tf_op jit(solution)/shard_map/all_to_all | solution.py:623
  238.1 0.8 collective-permute-start.24
  238.9 1.5 collective-permute-done.24.refs_1_
  240.4 1.9 join_cores.1
  (66 shorter events, 9.9 us)
Async XLA Ops:
  0.7 1.0 copy-start.8
  2.9 9.6 %all-to-all-start.1 = ((bf16[4,128,256]{2,1,0:T(8,128)(2,1)}), bf16[4,128,256]{2,1,0:T(8,128)(2,1)S(1)}, u32[]{:S(2)}, u32[]{:S(2)}) async-start(bf16[4,128,256]{2,1,0:T(8,128)(2,1)} %pack_columns.1), calls=%async_computation.1 | async-start | bytes 524288 | tf_op jit(solution)/shard_map/all_to_all | solution.py:623
  12.0 5.4 %copy-start.3 = (bf16[1024,448]{0,1:T(8,128)(2,1)S(1)}, bf16[1024,448]{0,1:T(8,128)(2,1)}, u32[]{:S(2)}) copy-start(bf16[1024,448]{0,1:T(8,128)(2,1)} %param.14) | copy-start | bytes 2752516
  12.5 52.6 %all-to-all-start = ((bf16[4,2,2,128,1024]{4,3,2,1,0:T(8,128)(2,1)}), bf16[4,2,2,128,1024]{4,3,2,1,0:T(8,128)(2,1)}, u32[]{:S(2)}, u32[]{:S(2)}) async-start(bf16[4,2,2,128,1024]{4,3,2,1,0:T(8,128)(2,1)} %pack_layers.1), calls=%async_computation | async-start | bytes 8388608 | tf_op jit(solution)/shard_map/all_to_all | solution.py:623
  17.4 37.8 %copy-start.23 = (s32[1,2048]{1,0:T(1,128)S(1)}, s32[1,2048]{1,0:T(1,128)}, u32[]{:S(2)}) copy-start(s32[1,2048]{1,0:T(1,128)} %param.13) | copy-start | bytes 24580
  18.0 7.3 %collective-permute-start.3 = (bf16[112,1024]{1,0:T(8,128)(2,1)S(1)}, bf16[112,1024]{1,0:T(8,128)(2,1)S(1)}, u32[]{:S(2)}, u32[]{:S(2)}) collective-permute-start(bf16[112,1024]{1,0:T(8,128)(2,1)S(1)} %own_quarter.1), channel_id=1, source_target_pairs={{0,1},{1,2},{2,3},{3,0},{4,5},{5,6},{6,7},{7,4},{8,9},{9,10},{10,1... | collective-permute-start | bytes 688136 | tf_op jit(solution)/shard_map/ppermute | solution.py:627
  19.7 17.4 %collective-permute-start.4 = (bf16[112,1024]{1,0:T(8,128)(2,1)S(1)}, bf16[112,1024]{1,0:T(8,128)(2,1)S(1)}, u32[]{:S(2)}, u32[]{:S(2)}) collective-permute-start(bf16[112,1024]{1,0:T(8,128)(2,1)S(1)} %own_quarter.1), channel_id=1, source_target_pairs={{0,2},{1,3},{2,0},{3,1},{4,6},{5,7},{6,4},{7,5},{8,10},{9,11},{10,... | collective-permute-start | bytes 688136 | tf_op jit(solution)/shard_map/ppermute | solution.py:627
  21.1 32.1 %collective-permute-start.5 = (bf16[112,1024]{1,0:T(8,128)(2,1)S(1)}, bf16[112,1024]{1,0:T(8,128)(2,1)S(1)}, u32[]{:S(2)}, u32[]{:S(2)}) collective-permute-start(bf16[112,1024]{1,0:T(8,128)(2,1)S(1)} %own_quarter.1), channel_id=1, source_target_pairs={{0,3},{1,0},{2,1},{3,2},{4,7},{5,4},{6,5},{7,6},{8,11},{9,8},{10,9... | collective-permute-start | bytes 688136 | tf_op jit(solution)/shard_map/ppermute | solution.py:627
  22.5 32.9 %collective-permute-start = (bf16[4,128,256]{2,1,0:T(8,128)(2,1)S(1)}, bf16[4,128,256]{2,1,0:T(8,128)(2,1)S(1)}, u32[]{:S(2)}, u32[]{:S(2)}) collective-permute-start(bf16[4,128,256]{2,1,0:T(8,128)(2,1)S(1)} %all-to-all-done.1.refs_0_.refs_1_), channel_id=1, source_target_pairs={{0,1},{1,2},{2,3},{3,0},{4,5},{5,6},{6,7},{7,4},{8,9},{9,10},{10,1... | collective-permute-start | bytes 786440 | tf_op jit(solution)/shard_map/ppermute | solution.py:627
  22.6 37.1 %collective-permute-start.1 = (bf16[4,128,256]{2,1,0:T(8,128)(2,1)S(1)}, bf16[4,128,256]{2,1,0:T(8,128)(2,1)S(1)}, u32[]{:S(2)}, u32[]{:S(2)}) collective-permute-start(bf16[4,128,256]{2,1,0:T(8,128)(2,1)S(1)} %all-to-all-done.1.refs_0_.refs_1_), channel_id=1, source_target_pairs={{0,2},{1,3},{2,0},{3,1},{4,6},{5,7},{6,4},{7,5},{8,10},{9,11},{10,... | collective-permute-start | bytes 786440 | tf_op jit(solution)/shard_map/ppermute | solution.py:627
  25.3 39.1 %collective-permute-start.2 = (bf16[4,128,256]{2,1,0:T(8,128)(2,1)S(1)}, bf16[4,128,256]{2,1,0:T(8,128)(2,1)S(1)}, u32[]{:S(2)}, u32[]{:S(2)}) collective-permute-start(bf16[4,128,256]{2,1,0:T(8,128)(2,1)S(1)} %all-to-all-done.1.refs_0_.refs_1_), channel_id=1, source_target_pairs={{0,3},{1,0},{2,1},{3,2},{4,7},{5,4},{6,5},{7,6},{8,11},{9,8},{10,9... | collective-permute-start | bytes 786440 | tf_op jit(solution)/shard_map/ppermute | solution.py:627
  53.8 30.0 %collective-permute-start.12 = (bf16[3,112,1024]{2,1,0:T(8,128)(2,1)S(1)}, bf16[3,112,1024]{2,1,0:T(8,128)(2,1)S(1)}, u32[]{:S(2)}, u32[]{:S(2)}) collective-permute-start(bf16[3,112,1024]{2,1,0:T(8,128)(2,1)S(1)} %stack.24.refs_4_.refs_0_.refs_5_), channel_id=1, source_target_pairs={{0,32},{32,0},{64,96},{96,64},{1,33},{33,1},{65,97},{97,65},{2,34}... | collective-permute-start | bytes 2064392 | tf_op jit(solution)/shard_map/ppermute | solution.py:675
  78.4 0.8 copy-start.12
  79.2 29.1 %all-to-all-start.2 = ((bf16[4,4,128,256]{3,2,1,0:T(8,128)(2,1)}), bf16[4,4,128,256]{3,2,1,0:T(8,128)(2,1)S(1)}, u32[]{:S(2)}, u32[]{:S(2)}) async-start(bf16[4,4,128,256]{3,2,1,0:T(8,128)(2,1)} %get-tuple-element.29.refs_1_.refs_4_.refs_2_), calls=%async_computation.2 | async-start | bytes 2097152 | tf_op jit(solution)/shard_map/all_to_all | solution.py:623
  83.8 6.9 %copy-start = (bf16[1,128,7168]{2,1,0:T(8,128)(2,1)S(1)}, bf16[1,128,7168]{2,1,0:T(8,128)(2,1)}, u32[]{:S(2)}) copy-start(bf16[1,128,7168]{2,1,0:T(8,128)(2,1)} %param.9) | copy-start | bytes 5505028
  83.8 0.8 copy-start.5
  84.7 1.1 copy-start.6
  87.1 32.8 %collective-permute-start.13 = (bf16[2,3,112,1024]{3,2,1,0:T(8,128)(2,1)S(1)}, bf16[2,3,112,1024]{3,2,1,0:T(8,128)(2,1)}, u32[]{:S(2)}, u32[]{:S(2)}) collective-permute-start(bf16[2,3,112,1024]{3,2,1,0:T(8,128)(2,1)S(1)} %stack.25), channel_id=1, source_target_pairs={{0,16},{16,0},{1,17},{17,1},{2,18},{18,2},{3,19},{19,3},{4,20},{20... | collective-permute-start | bytes 4128776 | tf_op jit(solution)/shard_map/ppermute | solution.py:631
  93.1 0.8 copy-start.16
  93.9 13.7 %collective-permute-start.10 = (bf16[128,1792]{1,0:T(8,128)(2,1)S(1)}, bf16[128,1792]{1,0:T(8,128)(2,1)S(1)}, u32[]{:S(2)}, u32[]{:S(2)}) collective-permute-start(bf16[128,1792]{1,0:T(8,128)(2,1)S(1)} %get-tuple-element.36), channel_id=1, source_target_pairs={{0,8},{4,12},{8,0},{12,4},{1,9},{5,13},{9,1},{13,5},{2,10},{6,14},... | collective-permute-start | bytes 1376264 | tf_op jit(solution)/shard_map/ppermute | solution.py:627
  94.2 21.8 %collective-permute-start.11 = (bf16[128,1792]{1,0:T(8,128)(2,1)}, bf16[128,1792]{1,0:T(8,128)(2,1)}, u32[]{:S(2)}, u32[]{:S(2)}) collective-permute-start(bf16[128,1792]{1,0:T(8,128)(2,1)} %get-tuple-element.37), channel_id=1, source_target_pairs={{0,12},{4,0},{8,4},{12,8},{1,13},{5,1},{9,5},{13,9},{2,14},{6,2},{... | collective-permute-start | bytes 1376264 | tf_op jit(solution)/shard_map/ppermute | solution.py:627
  96.6 21.3 %collective-permute-start.9 = (bf16[128,1792]{1,0:T(8,128)(2,1)}, bf16[128,1792]{1,0:T(8,128)(2,1)}, u32[]{:S(2)}, u32[]{:S(2)}) collective-permute-start(bf16[128,1792]{1,0:T(8,128)(2,1)} %get-tuple-element.35), channel_id=1, source_target_pairs={{0,4},{4,8},{8,12},{12,0},{1,5},{5,9},{9,13},{13,1},{2,6},{6,10},{... | collective-permute-start | bytes 1376264 | tf_op jit(solution)/shard_map/ppermute | solution.py:627
  100.8 0.8 copy-start.14
  101.6 31.0 %collective-permute-start.6 = (bf16[4,2,128,256]{3,2,1,0:T(8,128)(2,1)}, bf16[4,2,128,256]{3,2,1,0:T(8,128)(2,1)}, u32[]{:S(2)}, u32[]{:S(2)}) collective-permute-start(bf16[4,2,128,256]{3,2,1,0:T(8,128)(2,1)} %get-tuple-element.30), channel_id=1, source_target_pairs={{0,1},{1,2},{2,3},{3,0},{4,5},{5,6},{6,7},{7,4},{8,9},{9,10},{10,1... | collective-permute-start | bytes 1572872 | tf_op jit(solution)/shard_map/ppermute | solution.py:627
  107.5 0.8 copy-start.18
  108.3 24.3 %collective-permute-start.8 = (bf16[4,2,128,256]{3,2,1,0:T(8,128)(2,1)}, bf16[4,2,128,256]{3,2,1,0:T(8,128)(2,1)}, u32[]{:S(2)}, u32[]{:S(2)}) collective-permute-start(bf16[4,2,128,256]{3,2,1,0:T(8,128)(2,1)} %get-tuple-element.32), channel_id=1, source_target_pairs={{0,3},{1,0},{2,1},{3,2},{4,7},{5,4},{6,5},{7,6},{8,11},{9,8},{10,9... | collective-permute-start | bytes 1572872 | tf_op jit(solution)/shard_map/ppermute | solution.py:627
  116.0 16.6 %collective-permute-start.20 = (bf16[256,512]{1,0:T(8,128)(2,1)S(1)}, bf16[256,512]{1,0:T(8,128)(2,1)S(1)}, u32[]{:S(2)}, u32[]{:S(2)}) collective-permute-start(bf16[256,512]{1,0:T(8,128)(2,1)S(1)} %sum_transposed.1.refs_0_), channel_id=1, source_target_pairs={{0,4},{4,8},{8,12},{12,0},{1,5},{5,9},{9,13},{13,1},{2,6},{6,10},{... | collective-permute-start | bytes 786440 | tf_op jit(solution)/shard_map/ppermute | solution.py:627
  117.8 14.8 %collective-permute-start.21 = (bf16[256,512]{1,0:T(8,128)(2,1)S(1)}, bf16[256,512]{1,0:T(8,128)(2,1)S(1)}, u32[]{:S(2)}, u32[]{:S(2)}) collective-permute-start(bf16[256,512]{1,0:T(8,128)(2,1)S(1)} %sum_transposed.1.refs_0_), channel_id=1, source_target_pairs={{0,8},{4,12},{8,0},{12,4},{1,9},{5,13},{9,1},{13,5},{2,10},{6,14},... | collective-permute-start | bytes 786440 | tf_op jit(solution)/shard_map/ppermute | solution.py:627
  119.9 12.7 %collective-permute-start.22 = (bf16[256,512]{1,0:T(8,128)(2,1)S(1)}, bf16[256,512]{1,0:T(8,128)(2,1)S(1)}, u32[]{:S(2)}, u32[]{:S(2)}) collective-permute-start(bf16[256,512]{1,0:T(8,128)(2,1)S(1)} %sum_transposed.1.refs_0_), channel_id=1, source_target_pairs={{0,12},{4,0},{8,4},{12,8},{1,13},{5,1},{9,5},{13,9},{2,14},{6,2},{... | collective-permute-start | bytes 786440 | tf_op jit(solution)/shard_map/ppermute | solution.py:627
  120.5 1.2 copy-start.4
  121.6 1.1 copy-start.7
  122.7 1.0 copy-start.17
  123.8 1.0 copy-start.19
  130.5 0.7 copy-start.20
  131.2 0.7 copy-start.21
  131.9 0.7 copy-start.22
  137.5 5.1 %collective-permute-start.23 = (bf16[4,2,64,1792]{3,2,1,0:T(8,128)(2,1)S(1)}, bf16[4,2,64,1792]{3,2,1,0:T(8,128)(2,1)S(1)}, u32[]{:S(2)}, u32[]{:S(2)}) collective-permute-start(bf16[4,2,64,1792]{3,2,1,0:T(8,128)(2,1)S(1)} %get-tuple-element.48), channel_id=1, source_target_pairs={{0,16},{16,0},{1,17},{17,1},{2,18},{18,2},{3,19},{19,3},{4,20},{20... | collective-permute-start | bytes 5505032 | tf_op jit(solution)/shard_map/ppermute | solution.py:631
  143.7 1.2 copy-start.1
  145.0 4.3 %copy-start.15 = (bf16[4,2,128,256]{3,2,1,0:T(8,128)(2,1)S(1)}, bf16[4,2,128,256]{3,2,1,0:T(8,128)(2,1)}, u32[]{:S(2)}) copy-start(bf16[4,2,128,256]{3,2,1,0:T(8,128)(2,1)} %copy-done.14) | copy-start | bytes 1572868
  145.0 41.5 %all-to-all-start.3 = ((bf16[4,2,64,1792]{3,2,1,0:T(8,128)(2,1)}), bf16[4,2,64,1792]{3,2,1,0:T(8,128)(2,1)S(1)}, u32[]{:S(2)}, u32[]{:S(2)}) async-start(bf16[4,2,64,1792]{3,2,1,0:T(8,128)(2,1)} %copy-done.1), calls=%async_computation.3 | async-start | bytes 3670016 | tf_op jit(solution)/shard_map/all_to_all | solution.py:623
  149.3 24.0 %collective-permute-start.7 = (bf16[4,2,128,256]{3,2,1,0:T(8,128)(2,1)S(1)}, bf16[4,2,128,256]{3,2,1,0:T(8,128)(2,1)S(1)}, u32[]{:S(2)}, u32[]{:S(2)}) collective-permute-start(bf16[4,2,128,256]{3,2,1,0:T(8,128)(2,1)S(1)} %copy-done.15), channel_id=1, source_target_pairs={{0,2},{1,3},{2,0},{3,1},{4,6},{5,7},{6,4},{7,5},{8,10},{9,11},{10,... | collective-permute-start | bytes 1572872 | tf_op jit(solution)/shard_map/ppermute | solution.py:627
  151.4 9.4 %collective-permute-start.14 = (bf16[512,256]{1,0:T(8,128)(2,1)}, bf16[512,256]{1,0:T(8,128)(2,1)S(1)}, u32[]{:S(2)}, u32[]{:S(2)}) collective-permute-start(bf16[512,256]{1,0:T(8,128)(2,1)} %copy-done.22), channel_id=1, source_target_pairs={{0,4},{4,8},{8,12},{12,0},{1,5},{5,9},{9,13},{13,1},{2,6},{6,10},{... | collective-permute-start | bytes 786440 | tf_op jit(solution)/shard_map/ppermute | solution.py:627
  151.9 12.4 %collective-permute-start.15 = (bf16[512,256]{1,0:T(8,128)(2,1)}, bf16[512,256]{1,0:T(8,128)(2,1)S(1)}, u32[]{:S(2)}, u32[]{:S(2)}) collective-permute-start(bf16[512,256]{1,0:T(8,128)(2,1)} %copy-done.21), channel_id=1, source_target_pairs={{0,8},{4,12},{8,0},{12,4},{1,9},{5,13},{9,1},{13,5},{2,10},{6,14},... | collective-permute-start | bytes 786440 | tf_op jit(solution)/shard_map/ppermute | solution.py:627
  153.0 13.2 %collective-permute-start.16 = (bf16[512,256]{1,0:T(8,128)(2,1)}, bf16[512,256]{1,0:T(8,128)(2,1)S(1)}, u32[]{:S(2)}, u32[]{:S(2)}) collective-permute-start(bf16[512,256]{1,0:T(8,128)(2,1)} %copy-done.20), channel_id=1, source_target_pairs={{0,12},{4,0},{8,4},{12,8},{1,13},{5,1},{9,5},{13,9},{2,14},{6,2},{... | collective-permute-start | bytes 786440 | tf_op jit(solution)/shard_map/ppermute | solution.py:627
  166.9 14.8 %collective-permute-start.17 = (bf16[4,128,128]{2,1,0:T(8,128)(2,1)S(1)}, bf16[4,128,128]{2,1,0:T(8,128)(2,1)S(1)}, u32[]{:S(2)}, u32[]{:S(2)}) collective-permute-start(bf16[4,128,128]{2,1,0:T(8,128)(2,1)S(1)} %get-tuple-element.43), channel_id=1, source_target_pairs={{0,1},{1,2},{2,3},{3,0},{4,5},{5,6},{6,7},{7,4},{8,9},{9,10},{10,1... | collective-permute-start | bytes 393224 | tf_op jit(solution)/shard_map/ppermute | solution.py:627
  171.6 12.8 %collective-permute-start.18 = (bf16[4,128,128]{2,1,0:T(8,128)(2,1)S(1)}, bf16[4,128,128]{2,1,0:T(8,128)(2,1)S(1)}, u32[]{:S(2)}, u32[]{:S(2)}) collective-permute-start(bf16[4,128,128]{2,1,0:T(8,128)(2,1)S(1)} %get-tuple-element.44), channel_id=1, source_target_pairs={{0,2},{1,3},{2,0},{3,1},{4,6},{5,7},{6,4},{7,5},{8,10},{9,11},{10,... | collective-permute-start | bytes 393224 | tf_op jit(solution)/shard_map/ppermute | solution.py:627
  172.6 13.9 %collective-permute-start.19 = (bf16[4,128,128]{2,1,0:T(8,128)(2,1)S(1)}, bf16[4,128,128]{2,1,0:T(8,128)(2,1)S(1)}, u32[]{:S(2)}, u32[]{:S(2)}) collective-permute-start(bf16[4,128,128]{2,1,0:T(8,128)(2,1)S(1)} %get-tuple-element.45), channel_id=1, source_target_pairs={{0,3},{1,0},{2,1},{3,2},{4,7},{5,4},{6,5},{7,6},{8,11},{9,8},{10,9... | collective-permute-start | bytes 393224 | tf_op jit(solution)/shard_map/ppermute | solution.py:627
  188.3 20.6 %all-to-all-start.4 = ((bf16[8,64,448]{2,1,0:T(8,128)(2,1)}), bf16[8,64,448]{2,1,0:T(8,128)(2,1)S(1)}, u32[]{:S(2)}, u32[]{:S(2)}) async-start(bf16[8,64,448]{2,1,0:T(8,128)(2,1)} %sum_and_split.1), calls=%async_computation.4 | async-start | bytes 1048576 | tf_op jit(solution)/shard_map/all_to_all | solution.py:623
  194.3 1.0 copy-start.13
  195.3 13.5 %copy-start.9 = (f32[64,448]{1,0:T(8,128)S(1)}, f32[64,448]{1,0:T(8,128)}, u32[]{:S(2)}) copy-start(f32[64,448]{1,0:T(8,128)} %refs_1_.1) | copy-start | bytes 344068
  195.3 13.5 %copy-start.10 = (f32[64,448]{1,0:T(8,128)S(1)}, f32[64,448]{1,0:T(8,128)}, u32[]{:S(2)}) copy-start(f32[64,448]{1,0:T(8,128)} %refs_2_.1) | copy-start | bytes 344068
  195.4 13.5 %copy-start.11 = (f32[64,448]{1,0:T(8,128)S(1)}, f32[64,448]{1,0:T(8,128)}, u32[]{:S(2)}) copy-start(f32[64,448]{1,0:T(8,128)} %refs_3_.1) | copy-start | bytes 344068
  208.9 1.6 copy-start.2
  238.1 2.3 collective-permute-start.24
